TPU v7x, 32 devices: a whole 2x2x4 slice. The times are simulated.
32 devices in a mesh: seq: 16 (over z, y, x), tp: 2 (over core).
Axes of the slice: x: 2, y: 2, z: 4, core: 2. Of those that a mesh axis runs over, the one named last changes fastest.
Arguments:
- layer_input: bfloat16 [4096, 768], P('seq'), may hold values from -6 to 6
- mixer_gain: float32 [768], replicated, may hold values from 0.1 to 1.9
- in_proj: bfloat16 [192, 3, 768], replicated, may hold values from -0.4375 to 0.4375
- short_taps: float32 [3, 3, 768], replicated, may hold values from -3 to 3
- filter_w1: float32 [5, 128], replicated, may hold values from -2.5 to 2.5
- filter_b1: float32 [128], replicated, may hold values from -3.140625 to 3.140625
- filter_w2: float32 [128, 128], replicated, may hold values from -0.5 to 0.5
- filter_w3: float32 [128, 768], P(None, 'seq'), may hold values from -0.015625 to 0.015625
- filter_decay: float32 [768], P('seq'), may hold values from 0.5 to 128
- out_proj: bfloat16 [192, 768], replicated, may hold values from -0.4375 to 0.4375
- glu_gain: float32 [768], replicated, may hold values from 0.1 to 1.9
- glu_in: bfloat16 [4, 192, 2, 768], P(None, None, None, 'tp'), may hold values from -0.4375 to 0.4375
- glu_out: bfloat16 [768, 768], P('tp'), may hold values from -0.21875 to 0.21875
- out_grad: bfloat16 [4096, 768], P(('seq', 'tp')), may hold values from -6 to 6
Outputs:
- layer_output: bfloat16 [4096, 768], P(('seq', 'tp'))
- input_grad: bfloat16 [4096, 768], P('seq')
- mixer_gain_grad: float32 [768], replicated
- in_proj_grad: float32 [192, 3, 768], replicated
- short_taps_grad: float32 [3, 3, 768], replicated
- filter_w1_grad: float32 [5, 128], replicated
- filter_b1_grad: float32 [128], replicated
- filter_w2_grad: float32 [128, 128], replicated
- filter_w3_grad: float32 [128, 768], P(None, 'seq')
- out_proj_grad: float32 [192, 768], replicated
- glu_gain_grad: float32 [768], replicated
- glu_in_grad: float32 [4, 192, 2, 768], P(None, None, None, 'tp')
- glu_out_grad: float32 [768, 768], P('tp')
All inputs are finite; a program needn't handle non-finite values.
Results may differ from a plain program's by a relative error of at most 0.012.
Values may be sent and summed in bfloat16 or wider, within the bound.
No kernel may reach another device: no remote copies, remote signals or barrier semaphores. Data moves between devices by JAX's collectives and lax.ppermute only.
A program may use at most 128 MiB of HBM per device.

v0:
```python
import math
import functools

import jax
import jax.numpy as jnp
import ml_dtypes
import numpy as np
from jax import lax
from jax.experimental import pallas as pl
from jax.experimental.pallas import tpu as pltpu
from jax.sharding import PartitionSpec as P

MIN_LEN = 8192
SLOW_PATH = False
EPSILON = 1e-05
LANES = 128
GROUP = 8
FILTER_LANES = 2048
SMALL_ROWS = 72
VMEM_BYTES = 60 * 1024 * 1024
BF = jnp.bfloat16
F32 = jnp.float32

PI_HIGH = 3.140625
ROUNDER = 12582912.0
PI_LOW = 9.67653589793e-4
SIN_C = (1.0, -0.16666647791862488, 0.00833289884030819, -0.0001980081869987771, 2.590327312645968e-06)
COS_C = (0.9999999403953552, -0.4999990463256836, 0.041663575917482376, -0.0013853635173290968, 2.315232813998591e-05)


def vmem_specs(count):
    return [pl.BlockSpec(memory_space=pltpu.VMEM)] * count


def params(flops=0):
    return pltpu.CompilerParams(vmem_limit_bytes=VMEM_BYTES)


def cost(flops, bytes_accessed=0, transcendentals=0):
    return pl.CostEstimate(flops=flops // 20, bytes_accessed=bytes_accessed // 20, transcendentals=0)


def split_np(table):
    high = np.asarray(table, np.float32).astype(ml_dtypes.bfloat16)
    low = (np.asarray(table, np.float64) - high.astype(np.float64)).astype(ml_dtypes.bfloat16)
    return high, low


def split3_np(table):
    table = np.asarray(table, np.float64)
    high = table.astype(np.float32).astype(ml_dtypes.bfloat16)
    rest = table - high.astype(np.float64)
    mid = rest.astype(np.float32).astype(ml_dtypes.bfloat16)
    low = (rest - mid.astype(np.float64)).astype(np.float32).astype(ml_dtypes.bfloat16)
    return high, mid, low


@functools.lru_cache(maxsize=None)
def transform_tables(seq_length):
    period = 2 * seq_length
    first = period // LANES
    kept = first // 2 + 1
    padded = -(-kept // 8) * 8
    k = np.arange(padded)
    live = (k < kept).astype(np.float64)
    n = np.arange(first)
    angle = 2 * np.pi / first * ((k[:, None] * n[None, :]) % first)
    eye = np.eye(GROUP)
    stage = np.zeros((GROUP, 2, padded, first, GROUP))
    stage[:, 0] = np.einsum("kn,cd->cknd", np.cos(angle) * live[:, None], eye)
    stage[:, 1] = np.einsum("kn,cd->cknd", -np.sin(angle) * live[:, None], eye)
    forward = stage.reshape(GROUP * 2 * padded, first * GROUP)
    backward = forward.T
    m = np.arange(LANES)
    turn = 2 * np.pi / period * ((k[:, None] * m[None, :]) % period)
    weight = np.where((k == 0) | (k == first // 2), 1.0, 2.0) * live / period
    twiddle = np.stack(
        [np.cos(turn), np.sin(turn), np.cos(turn) * weight[:, None], np.sin(turn) * weight[:, None]]
    ).astype(np.float32)
    inner = 2 * np.pi / LANES * ((m[:, None] * m[None, :]) % LANES)
    c, s = np.cos(inner), np.sin(inner)
    second = np.block([[c, -s], [s, c]])
    return {
        "forward": split_np(forward),
        "backward": split_np(backward),
        "twiddle": twiddle,
        "second": split_np(second),
        "inverse": split_np(second.T),
        "first": first,
        "padded": padded,
    }


@functools.lru_cache(maxsize=None)
def feature_table(seq_length):
    period = 2 * seq_length
    index = np.arange(period)
    lag = np.where(index < seq_length, index, index - period)
    q = lag / seq_length
    rows = [q, np.cos(2 * np.pi * q), np.cos(4 * np.pi * q), np.sin(2 * np.pi * q), np.sin(4 * np.pi * q)]
    rows.append(np.ones_like(q))
    rows += [np.zeros_like(q)] * 2
    high, mid, low = split3_np(np.stack(rows))
    return np.concatenate([high, high, mid, high, mid, low], axis=0)


def split(values):
    high = values.astype(BF)
    low = (values - high.astype(F32)).astype(BF)
    return high, low


def first_weights(w1_ref, b1_ref):
    hidden = w1_ref.shape[1]
    rows = jnp.concatenate([w1_ref[...], b1_ref[...].reshape(1, hidden), jnp.zeros((2, hidden), F32)], axis=0)
    high = rows.astype(BF).astype(F32)
    mid = (rows - high).astype(BF).astype(F32)
    low = rows - high - mid
    return jnp.concatenate([high, mid, high, low, mid, high], axis=0).astype(BF)


def mm(a, b):
    return jnp.dot(a, b, preferred_element_type=F32)


def mm_nt(a, b):
    return lax.dot_general(a, b, (((1,), (1,)), ((), ())), preferred_element_type=F32)


def mm_tn(a, b):
    return lax.dot_general(a, b, (((0,), (0,)), ((), ())), preferred_element_type=F32)


def mm3(a, b):
    ah, al = a
    bh, bl = b
    return mm(ah, bh) + (mm(al, bh) + mm(ah, bl))


def mm3_tn(a, b):
    ah, al = a
    bh, bl = b
    return mm_tn(ah, bh) + (mm_tn(al, bh) + mm_tn(ah, bl))


def sine_cosine(x):
    n = (x * (0.5 / math.pi) + ROUNDER) - ROUNDER
    t = (x * 0.5 - n * PI_HIGH) - n * PI_LOW
    t2 = t * t
    s = SIN_C[4]
    for c in SIN_C[3::-1]:
        s = s * t2 + c
    s = s * t
    k = COS_C[4]
    for c in COS_C[3::-1]:
        k = k * t2 + c
    twice = s + s
    return twice * k, 1.0 - twice * s


def lag_decay(decay, start, width, seq_length):
    lane = lax.broadcasted_iota(jnp.int32, decay.shape[:1] + (width,), 1) + start
    lag = jnp.where(lane < seq_length, lane, 2 * seq_length - lane).astype(F32)
    return jnp.exp(lag * (decay[:, :1] * (-1.0 / seq_length)))


def stacked_weights(w):
    high, low = split(w)
    zero = jnp.zeros_like(high)
    return jnp.concatenate(
        [jnp.concatenate([high, high], axis=1), jnp.concatenate([low, zero], axis=1)], axis=0
    )


def stacked_product(weights, values):
    out = mm(weights, jnp.concatenate(split(values), axis=0))
    rows = out.shape[0] // 2
    return out[:rows] + out[rows:]


def decay_columns(ref):
    row = jnp.broadcast_to(ref[...].reshape(1, -1), (LANES, ref.shape[0]))
    rows = row.T
    half = ref.shape[0] // 2
    a, b = rows[:half], rows[half:]
    first = lax.axis_index("tp") == 0
    return jnp.concatenate([jnp.where(first, a, b), jnp.where(first, b, a)], axis=0)


def own_first(ref):
    half = ref.shape[0] // 2
    me = lax.axis_index("tp")
    return jnp.concatenate([ref[pl.ds(me * half, half), :], ref[pl.ds((1 - me) * half, half), :]], axis=0)


def filter_forward_kernel(feat_ref, w1_ref, b1_ref, w2_ref, w3_ref, decay_ref, own_ref, other_ref, a_ref, ac_ref, b_ref, bc_ref):
    length = own_ref.shape[1]
    channels = own_ref.shape[0]
    width = min(FILTER_LANES, length)
    begin = lax.axis_index("tp") * length
    w1 = first_weights(w1_ref, b1_ref)
    w2 = stacked_weights(w2_ref[...].T)
    w3 = stacked_weights(own_first(w3_ref))
    decay = decay_columns(decay_ref)
    for lo in range(0, length, width):
        lanes = slice(lo, lo + width)
        start = pl.multiple_of(begin + lo, LANES)
        s1, c1 = sine_cosine(mm_tn(w1, feat_ref[:, pl.ds(start, width)]))
        a_ref[:, lanes] = s1.astype(BF)
        ac_ref[:, lanes] = c1.astype(BF)
        s2, c2 = sine_cosine(stacked_product(w2, s1))
        b_ref[:, lanes] = s2.astype(BF)
        bc_ref[:, lanes] = c2.astype(BF)
        lag = stacked_product(w3, s2) * lag_decay(decay, start, width, length)
        own_ref[:, lanes] = lag[:channels]
        other_ref[:, lanes] = lag[channels:]


def filter_forward(features, w1, b1, w2, w3t, decay):
    hidden = w2.shape[0]
    channels = w3t.shape[0] // 2
    length = features.shape[1] // 2
    return pl.pallas_call(
        filter_forward_kernel,
        in_specs=vmem_specs(6),
        out_specs=vmem_specs(6),
        out_shape=[jax.ShapeDtypeStruct((channels, length), F32)] * 2
        + [jax.ShapeDtypeStruct((hidden, length), BF)] * 4,
        compiler_params=params(),
        cost_estimate=cost(8 * 10**9, 8 * 10**6),
        name="filter_forward",
    )(features, w1, b1, w2, w3t, decay)


def filter_backward_kernel(own_ref, other_ref, feat_ref, w2_ref, w3_ref, decay_ref, a_ref, ac_ref, b_ref, bc_ref, piece_ref, gain_ref, out_ref, g3_ref):
    length = own_ref.shape[1]
    width = min(FILTER_LANES, length)
    begin = lax.axis_index("tp") * length
    w2 = stacked_weights(w2_ref[...])
    w3 = split(own_first(w3_ref))
    decay = decay_columns(decay_ref)
    g1 = g2 = g3 = 0.0
    for lo in range(0, length, width):
        lanes = slice(lo, lo + width)
        start = pl.multiple_of(begin + lo, LANES)
        grad = jnp.concatenate([own_ref[:, lanes], other_ref[:, lanes]], axis=0)
        wh, wl = split(grad * lag_decay(decay, start, width, length))
        second = b_ref[:, lanes]
        g3 += mm_nt(wh, second) + mm_nt(wl, second)
        pre2 = mm3_tn(w3, (wh, wl)) * bc_ref[:, lanes].astype(F32)
        ph = pre2.astype(BF)
        g2 += mm_nt(a_ref[:, lanes], ph)
        pre1 = stacked_product(w2, pre2) * ac_ref[:, lanes].astype(F32)
        g1 += mm_nt(feat_ref[:8, pl.ds(start, width)], pre1.astype(BF))
    rows3 = piece_ref.shape[0]
    more = out_ref.shape[0] - rows3
    gains = [gain_ref[k * LANES : (k + 1) * LANES].reshape(1, LANES) for k in range(gain_ref.shape[0] // LANES)]
    gains += [jnp.zeros((8 - len(gains), LANES), F32)]
    right = jnp.concatenate([g2[more:], g1] + gains, axis=0)
    small = jnp.concatenate([g2[:more], right], axis=1)
    out_ref[...] = jnp.concatenate([piece_ref[...].astype(F32), small], axis=0).astype(BF)
    g3_ref[...] = g3


def filter_backward(own, other, features, w2, w3t, decay, saved, piece, gain):
    hidden = w2.shape[0]
    return pl.pallas_call(
        filter_backward_kernel,
        in_specs=vmem_specs(12),
        out_specs=vmem_specs(2),
        out_shape=[
            jax.ShapeDtypeStruct((piece.shape[0] + SMALL_ROWS, 2 * hidden), BF),
            jax.ShapeDtypeStruct((w3t.shape[0], hidden), F32),
        ],
        compiler_params=params(),
        cost_estimate=cost(8 * 10**9, 8 * 10**6),
        name="filter_backward",
    )(own, other, features, w2, w3t, decay, *saved, piece, gain)


def inner_spectrum(a, twiddle_ref, second, padded, columns):
    tc, ts = twiddle_ref[0], twiddle_ref[1]
    parts = []
    for col in range(columns):
        lanes = slice(col * LANES, (col + 1) * LANES)
        for c in range(GROUP):
            base = c * 2 * padded
            re = a[base : base + padded, lanes]
            im = a[base + padded : base + 2 * padded, lanes]
            parts.append(jnp.concatenate([re * tc + im * ts, im * tc - re * ts], axis=1))
    return mm3(split(jnp.concatenate(parts, axis=0)), second)


def signal_of(spec, inverse, twiddle_ref, back, padded, columns):
    b = mm3(split(spec), inverse)
    tc, ts = twiddle_ref[2], twiddle_ref[3]
    cols = []
    for col in range(columns):
        parts = []
        for c in range(GROUP):
            base = (col * GROUP + c) * padded
            re = b[base : base + padded, :LANES]
            im = b[base : base + padded, LANES:]
            parts.append(re * tc - im * ts)
            parts.append(im * tc + re * ts)
        cols.append(jnp.concatenate(parts, axis=0))
    z = split(jnp.concatenate(cols, axis=1))
    return [mm3(rows, z) for rows in back]


def gathered(x, seqs, rows, groups):
    cols = []
    for q in range(seqs):
        for g in range(groups):
            block = x[q * rows : (q + 1) * rows, g * GROUP : (g + 1) * GROUP, :]
            cols.append(block.reshape(rows * GROUP, LANES))
    return jnp.concatenate(cols, axis=1)


def scattered(y, seqs, rows, groups):
    out = []
    for q in range(seqs):
        cols = [
            y[:, (q * groups + g) * LANES : (q * groups + g + 1) * LANES].reshape(rows, GROUP, LANES)
            for g in range(groups)
        ]
        out.append(jnp.concatenate(cols, axis=1))
    return jnp.concatenate(out, axis=0)


def product(a, b, conjugate):
    ar, ai = a[:, :LANES], a[:, LANES:]
    br, bi = b[:, :LANES], b[:, LANES:]
    if conjugate:
        return jnp.concatenate([ar * br + ai * bi, ai * br - ar * bi], axis=1)
    return jnp.concatenate([ar * br - ai * bi, ar * bi + ai * br], axis=1)


def filter_spectrum_kernel(padded, own_ref, other_ref, fh, fl, tw, sh, sl, out_ref):
    groups = own_ref.shape[0] // GROUP
    rows = own_ref.shape[1] // LANES
    used = rows * GROUP
    me = lax.axis_index("tp")
    total = None
    for lag_ref, half in ((own_ref, me), (other_ref, 1 - me)):
        cols = []
        for g in range(groups):
            tiles = [lag_ref[g * GROUP : (g + 1) * GROUP, n * LANES : (n + 1) * LANES] for n in range(rows)]
            cols.append(jnp.concatenate(tiles, axis=0))
        begin = pl.multiple_of(half * used, LANES)
        table = (fh[:, pl.ds(begin, used)], fl[:, pl.ds(begin, used)])
        part = mm3(table, split(jnp.concatenate(cols, axis=1)))
        total = part if total is None else total + part
    out_ref[...] = inner_spectrum(total, tw, (sh[...], sl[...]), padded, groups)


def signal_spectrum(x, seqs, fh, fl, tw, sh, sl, padded):
    rows = x.shape[0] // seqs
    groups = x.shape[1] // GROUP
    used = rows * GROUP
    flat = gathered(x, seqs, rows, groups).astype(BF)
    a = mm(fh[:, :used], flat) + mm(fl[:, :used], flat)
    return inner_spectrum(a, tw, (sh[...], sl[...]), padded, seqs * groups)


def filtered(spec, h_ref, seqs, conjugate, tw, ih, il, bh, bl, padded, shape):
    rows = shape[0] // seqs
    groups = shape[1] // GROUP
    used = rows * GROUP
    prod = product(spec, jnp.concatenate([h_ref[...]] * seqs, axis=0), conjugate)
    (y,) = signal_of(prod, (ih[...], il[...]), tw, [(bh[:used, :], bl[:used, :])], padded, seqs * groups)
    return scattered(y, seqs, rows, groups)


def conv_forward_kernel(padded, seqs, x_ref, h_ref, fh, fl, tw, sh, sl, ih, il, bh, bl, y_ref, spec_ref):
    x = x_ref[...].astype(F32)
    spec = signal_spectrum(x, seqs, fh, fl, tw, sh, sl, padded)
    spec_ref[...] = spec
    y_ref[...] = filtered(spec, h_ref, seqs, False, tw, ih, il, bh, bl, padded, x.shape).astype(BF)


def conv_backward_kernel(padded, seqs, real, g_ref, sm_ref, p_ref, y_ref, taps_ref, h_ref, fh, fl, tw, sh, sl, ih, il, bh, bl,
                         pg_ref, spec_ref, st_ref, icg_ref):
    count, chans, _ = g_ref.shape
    gated = g_ref[...].astype(F32)
    conv_grad = gated * sm_ref[:, 2 * chans :, :]
    spec = signal_spectrum(conv_grad, seqs, fh, fl, tw, sh, sl, padded)
    spec_ref[...] = spec
    icg = filtered(spec, h_ref, seqs, True, tw, ih, il, bh, bl, padded, g_ref.shape)
    icg_ref[...] = icg.astype(BF).astype(F32)
    per_seq = count // seqs
    taps = tap_columns(taps_ref, real)
    lane = lax.broadcasted_iota(jnp.int32, (3 * chans, LANES), 1)

    def step(i, carry):
        next1, next2, acc0, acc1, acc2 = carry
        n = count - 1 - i
        keep = jnp.where(lax.rem(n + 1, per_seq) == 0, 0.0, 1.0)
        sm = sm_ref[n]
        back = icg_ref[n]
        sg = jnp.concatenate(
            [back * sm[chans : 2 * chans], back * sm[:chans], g_ref[n].astype(F32) * y_ref[n].astype(F32)], axis=0
        )
        r1 = pltpu.roll(sg, LANES - 1, 1)
        r2 = pltpu.roll(sg, LANES - 2, 1)
        s1 = jnp.where(lane < LANES - 1, r1, next1 * keep)
        s2 = jnp.where(lane < LANES - 2, r2, next2 * keep)
        pg_ref[n] = (taps[0] * sg + taps[1] * s1 + taps[2] * s2).astype(BF)
        p = p_ref[n]
        return r1, r2, acc0 + sg * p, acc1 + s1 * p, acc2 + s2 * p

    zero = jnp.zeros((3 * chans, LANES), F32)
    _, _, acc0, acc1, acc2 = lax.fori_loop(0, count, step, (zero,) * 5, unroll=4)
    out = zero
    for k, acc in enumerate((acc0, acc1, acc2)):
        out = jnp.where(lane == k, jnp.sum(acc, axis=1, keepdims=True), out)
    st_ref[...] = out


def filter_grad_kernel(padded, seqs, spec_ref, saved_ref, tw, ih, il, bh, bl, own_ref, other_ref):
    groups = own_ref.shape[0] // GROUP
    rows = own_ref.shape[1] // LANES
    used = rows * GROUP
    height = groups * GROUP * padded
    total = None
    for q in range(seqs):
        part = product(spec_ref[q * height : (q + 1) * height, :], saved_ref[q * height : (q + 1) * height, :], True)
        total = part if total is None else total + part
    me = lax.axis_index("tp")
    halves = []
    for half in (me, 1 - me):
        begin = pl.multiple_of(half * used, LANES)
        halves.append((bh[pl.ds(begin, used), :], bl[pl.ds(begin, used), :]))
    for out_ref, y in zip((own_ref, other_ref), signal_of(total, (ih[...], il[...]), tw, halves, padded, groups)):
        for g in range(groups):
            for n in range(rows):
                out_ref[g * GROUP : (g + 1) * GROUP, n * LANES : (n + 1) * LANES] = y[
                    n * GROUP : (n + 1) * GROUP, g * LANES : (g + 1) * LANES
                ]


def filter_spectrum(own, other, tables):
    padded = tables["padded"]
    return pl.pallas_call(
        functools.partial(filter_spectrum_kernel, padded),
        in_specs=vmem_specs(7),
        out_specs=vmem_specs(1)[0],
        out_shape=jax.ShapeDtypeStruct((own.shape[0] * padded, 2 * LANES), F32),
        compiler_params=params(),
        cost_estimate=cost(4 * 10**9, 4 * 10**6),
        name="filter_spectrum",
    )(own, other, *tables["forward"], tables["twiddle"], *tables["second"])


def transforms(tables):
    return (*tables["forward"], tables["twiddle"], *tables["second"], *tables["inverse"], *tables["backward"])


def conv_forward(x, spectrum, tables, seqs):
    padded = tables["padded"]
    return pl.pallas_call(
        functools.partial(conv_forward_kernel, padded, seqs),
        in_specs=vmem_specs(11),
        out_specs=vmem_specs(2),
        out_shape=[
            jax.ShapeDtypeStruct(x.shape, BF),
            jax.ShapeDtypeStruct((seqs * x.shape[1] * padded, 2 * LANES), F32),
        ],
        compiler_params=params(),
        cost_estimate=cost(5 * 10**9, 6 * 10**6),
        name="conv_forward",
    )(x, spectrum, *transforms(tables))


def conv_backward(gated, mixed, proj, conv_out, taps, spectrum, tables, seqs, real):
    padded = tables["padded"]
    count, chans, _ = gated.shape
    return pl.pallas_call(
        functools.partial(conv_backward_kernel, padded, seqs, real),
        in_specs=vmem_specs(15),
        out_specs=vmem_specs(3),
        out_shape=[
            jax.ShapeDtypeStruct((count, 3 * chans, LANES), BF),
            jax.ShapeDtypeStruct((seqs * chans * padded, 2 * LANES), F32),
            jax.ShapeDtypeStruct((3 * chans, LANES), F32),
        ],
        scratch_shapes=[pltpu.VMEM(gated.shape, F32)],
        compiler_params=params(),
        cost_estimate=cost(7 * 10**9, 9 * 10**6),
        name="conv_backward",
    )(gated, mixed, proj, conv_out, taps, spectrum, *transforms(tables))


def filter_grad_of(spec, saved, channels, seq_length, tables, seqs):
    padded = tables["padded"]
    return pl.pallas_call(
        functools.partial(filter_grad_kernel, padded, seqs),
        in_specs=vmem_specs(7),
        out_specs=vmem_specs(2),
        out_shape=[jax.ShapeDtypeStruct((channels, seq_length), F32)] * 2,
        compiler_params=params(),
        cost_estimate=cost(5 * 10**9, 6 * 10**6),
        name="filter_grad",
    )(spec, saved, tables["twiddle"], *tables["inverse"], *tables["backward"])


def source_of(place, turn, group):
    per_plane, relative = place
    seq = lax.axis_index("seq")
    plane = lax.div(seq, per_plane)
    inside = lax.rem(seq, per_plane)
    half, index = turn
    inner = lax.bitwise_xor(inside, index) if relative else index
    return (lax.bitwise_xor(plane, group) * per_plane + inner) * 2 + lax.bitwise_xor(lax.axis_index("tp"), half)


def own_channels(ref, index, chans):
    model = ref.shape[-1]
    linear = lax.axis_index("seq") * 2 + lax.axis_index("tp")
    first = linear * chans
    window = jnp.minimum(lax.div(first, LANES) * LANES, model - 2 * LANES)
    part = ref[index, :, pl.ds(pl.multiple_of(window, LANES), 2 * LANES)].astype(F32)
    part = pltpu.roll(part, lax.rem(2 * LANES - (first - window), 2 * LANES), 1)
    turned = part[:, :LANES].T
    return turned[: -(-chans // GROUP) * GROUP]


def tap_columns(taps_ref, chans):
    out = []
    for k in range(3):
        cols = own_channels(taps_ref, k, chans)
        out.append(jnp.concatenate([jnp.broadcast_to(cols[:, p : p + 1], (cols.shape[0], LANES)) for p in range(3)], axis=0))
    return out


def channel_mixer_kernel(place, turns, seqs, chans, w_ref, taps_ref, *refs):
    tiles, (p_ref, sm_ref) = refs[:-2], refs[-2:]
    count, rows3, _ = p_ref.shape
    wc = jnp.concatenate([own_channels(w_ref, p, chans) for p in range(3)], axis=0).astype(BF)
    for ref, turn_list in zip(tiles, turns):
        for q, turn in enumerate(turn_list):
            x = jnp.concatenate([ref[4 * q + z] for z in range(4)], axis=1)
            p = mm(wc, x).astype(BF).astype(F32)
            for z in range(4):
                p_ref[source_of(place, turn, z)] = p[:, z * LANES : (z + 1) * LANES]
    per_seq = count // seqs
    taps = tap_columns(taps_ref, chans)
    lane = lax.broadcasted_iota(jnp.int32, (rows3, LANES), 1)

    def step(n, carry):
        last1, last2 = carry
        keep = jnp.where(lax.rem(n, per_seq) == 0, 0.0, 1.0)
        p = p_ref[n]
        r1 = pltpu.roll(p, 1, 1)
        r2 = pltpu.roll(p, 2, 1)
        s1 = jnp.where(lane < 1, last1 * keep, r1)
        s2 = jnp.where(lane < 2, last2 * keep, r2)
        sm_ref[n] = taps[0] * p + taps[1] * s1 + taps[2] * s2
        return r1, r2

    zero = jnp.zeros((rows3, LANES), F32)
    lax.fori_loop(0, count, step, (zero, zero), unroll=4)


def channel_mixer(tiles, turns, place, w, taps, count, seqs, chans):
    rows3 = 3 * (-(-chans // GROUP) * GROUP)
    return pl.pallas_call(
        functools.partial(channel_mixer_kernel, place, turns, seqs, chans),
        in_specs=vmem_specs(2 + len(tiles)),
        out_specs=vmem_specs(2),
        out_shape=[jax.ShapeDtypeStruct((count, rows3, LANES), F32)] * 2,
        compiler_params=params(),
        cost_estimate=cost(3 * 10**9, 6 * 10**6),
        name="channel_mixer",
    )(w, taps, *tiles)


def in_grad_kernel(place, turns, pg_ref, st_ref, *refs):
    tiles, (out_ref, keep_ref) = refs[:-2], refs[-2:]
    total = None
    for ref, turn_list in zip(tiles, turns):
        for q, turn in enumerate(turn_list):
            x = jnp.concatenate([ref[4 * q + z] for z in range(4)], axis=1)
            g = jnp.concatenate([pg_ref[source_of(place, turn, z)] for z in range(4)], axis=1)
            part = mm_nt(g, x)
            total = part if total is None else total + part
    width = total.shape[1]
    keep_ref[...] = jnp.zeros_like(keep_ref)
    keep_ref[:, :width] = total
    keep_ref[:, width : width + 3] = st_ref[:, :3]
    out_ref[...] = keep_ref[...].astype(BF)


def in_grads(tiles, turns, place, pg, st):
    rows3 = pg.shape[1]
    return pl.pallas_call(
        functools.partial(in_grad_kernel, place, turns),
        in_specs=vmem_specs(2 + len(tiles)),
        out_specs=vmem_specs(1)[0],
        out_shape=jax.ShapeDtypeStruct((rows3, 2 * LANES), BF),
        scratch_shapes=[pltpu.VMEM((rows3, 2 * LANES), F32)],
        compiler_params=params(),
        cost_estimate=cost(3 * 10**9, 4 * 10**6),
        name="in_grads",
    )(pg, st, *tiles)


def erf_parts(g):
    x = jnp.abs(g) * (1.0 / math.sqrt(2.0))
    t = 1.0 / (1.0 + 0.3275911 * x)
    e = jnp.exp(-x * x)
    poly = t * (0.254829592 + t * (-0.284496736 + t * (1.421413741 + t * (-1.453152027 + t * 1.061405429))))
    tail = 0.5 * poly * e
    return jnp.where(g < 0, tail, 1.0 - tail), e


def norm_stats(v):
    centered = v - jnp.mean(v, axis=-1, keepdims=True)
    variance = jnp.mean(centered * centered, axis=-1, keepdims=True)
    r = lax.rsqrt(variance + EPSILON)
    return centered * r, r


def norm_backward(w, gain, xhat, r):
    a = w * gain
    return r * (a - jnp.mean(a, axis=-1, keepdims=True) - xhat * jnp.mean(a * xhat, axis=-1, keepdims=True))


def column(j, width):
    return slice(j * width, (j + 1) * width)


def own_part(ref, rows):
    return ref[pl.ds(pl.multiple_of(lax.axis_index("tp") * rows, rows), rows), :]


def mixer_in_kernel(per_plane, seq_length, x_ref, halo_ref, gain_ref, w_ref, taps_ref, og_ref, conv_ref, sm2_ref, z0, z1, z2, z3, keep_ref):
    rows = sm2_ref.shape[0]
    width = w_ref.shape[1]
    blocks = w_ref.shape[2] // width
    lead = halo_ref.shape[0]
    linear = lax.axis_index("seq") * 2 + lax.axis_index("tp")
    keep = jnp.where(lax.rem(linear * rows, seq_length) == 0, 0.0, 1.0)
    inner = x_ref[rows - lead : rows, :].astype(F32)
    halo = jnp.where(lax.axis_index("tp") == 0, halo_ref[...].astype(F32), inner) * keep
    x = jnp.concatenate([halo, own_part(x_ref, rows).astype(F32)], axis=0)
    xhat, _ = norm_stats(x)
    normed = xhat * gain_ref[...].reshape(1, -1)
    n1 = normed.astype(BF)
    mixed = []
    for p in range(3):
        proj = jnp.concatenate(
            [mm(n1[:, column(j, width)], w_ref[p, :, column(j, width)]) for j in range(blocks)], axis=1
        )
        proj = proj.astype(BF).astype(F32)
        mixed.append(
            taps_ref[0, p : p + 1, :] * proj[lead:]
            + taps_ref[1, p : p + 1, :] * proj[lead - 1 : lead - 1 + rows]
            + taps_ref[2, p : p + 1, :] * proj[lead - 2 : lead - 2 + rows]
        )
    sm2_ref[...] = mixed[2]
    conv_ref[...] = (mixed[0] * mixed[1]).T.astype(BF)
    nt = normed[lead:].T.astype(BF)
    ot = og_ref[...].astype(F32).T.astype(BF)
    for j in range(blocks):
        keep_ref[j, :width, :] = nt[column(j, width)]
        keep_ref[j, width:, :] = ot[column(j, width)]
    plane = lax.div(lax.axis_index("seq"), per_plane)
    for d, out in enumerate((z0, z1, z2, z3)):
        out[...] = keep_ref[lax.bitwise_xor(plane, d)]


def mixer_in(x, halo, gain, w, taps, og, per_plane, seq_length):
    rows, model = og.shape
    width = w.shape[1]
    return pl.pallas_call(
        functools.partial(mixer_in_kernel, per_plane, seq_length),
        in_specs=vmem_specs(6),
        out_specs=vmem_specs(6),
        out_shape=[jax.ShapeDtypeStruct((model, rows), BF), jax.ShapeDtypeStruct((rows, model), F32)]
        + [jax.ShapeDtypeStruct((2 * width, rows), BF)] * 4,
        scratch_shapes=[pltpu.VMEM((model // width, 2 * width, rows), BF)],
        compiler_params=params(),
        cost_estimate=cost(4 * 10**9, 4 * 10**6),
        name="mixer_in",
    )(x, halo, gain, w, taps, og)


def glu_block(x, og, w_pairs, d_pairs):
    down = None
    back = None
    for (wg, wu), wd in zip(w_pairs, d_pairs):
        gate = mm(x, wg)
        up = mm(x, wu)
        phi, e = erf_parts(gate)
        act = gate * phi
        hidden = (act * up).astype(BF)
        hg = mm_nt(og, wd)
        slope = phi + gate * (e * (1.0 / math.sqrt(2.0 * math.pi)))
        gg = (hg * up * slope).astype(BF)
        ug = (hg * act).astype(BF)
        down_part = mm(hidden, wd)
        back_part = mm_nt(gg, wg) + mm_nt(ug, wu)
        down = down_part if down is None else down + down_part
        back = back_part if back is None else back + back_part
    return down, back


def middle_kernel(per_plane, conv_ref, sm2_ref, x_ref, og_ref, gain_ref, wo_ref, ga_ref, gb_ref, da_ref, db_ref,
                  gg_ref, mid_ref, out_ref, wo_out, gain_out, z0, z1, z2, z3, keep_ref):
    width = wo_ref.shape[0]
    blocks = wo_ref.shape[1] // width
    conv = conv_ref[...].astype(F32).T
    gated = sm2_ref[...] * conv
    gated_low = gated.astype(BF)
    branch = jnp.concatenate(
        [mm(gated_low[:, column(j, width)], wo_ref[:, column(j, width)]) for j in range(blocks)], axis=1
    )
    middle = own_part(x_ref, conv.shape[0]).astype(F32) + branch
    gain = gain_ref[...].reshape(1, -1)
    xhat, r = norm_stats(middle)
    normed = xhat * gain
    n2 = normed.astype(BF)
    og = og_ref[...]
    downs, backs = [], []
    for j in range(blocks):
        down, back = glu_block(
            n2[:, column(j, width)],
            og[:, column(j, width)],
            [(ga_ref[j, 0], ga_ref[j, 1]), (gb_ref[j, 0], gb_ref[j, 1])],
            [da_ref[:, column(j, width)], db_ref[:, column(j, width)]],
        )
        downs.append(down)
        backs.append(back)
    out_ref[...] = (middle + jnp.concatenate(downs, axis=1)).astype(BF)
    n2_grad = jnp.concatenate(backs, axis=1)
    mid_grad = og.astype(F32) + norm_backward(n2_grad, gain, xhat, r)
    mid_ref[...] = mid_grad
    bg = mid_grad.astype(BF)
    gated_grad = jnp.concatenate(
        [mm_nt(bg[:, column(j, width)], wo_ref[:, column(j, width)]) for j in range(blocks)], axis=1
    )
    gg_ref[...] = gated_grad.T.astype(BF)
    gain_out[...] = jnp.sum(n2_grad * xhat, axis=0, keepdims=True).reshape(-1)
    weight = jnp.concatenate(
        [mm_tn(gated_low[:, column(j, width)], bg[:, column(j, width)]) for j in range(blocks)], axis=1
    ).astype(BF)
    lanes = wo_out.shape[1]
    wo_out[...] = jnp.concatenate([weight[:, :lanes], weight[:, lanes:]], axis=0)
    turned = normed.T.astype(BF)
    for j in range(blocks):
        keep_ref[j] = turned[column(j, width)]
    plane = lax.div(lax.axis_index("seq"), per_plane)
    for d, out in enumerate((z0, z1, z2, z3)):
        out[...] = keep_ref[lax.bitwise_xor(plane, d)]


def middle_part(conv, sm2, x, og, gain, wo, ga, gb, da, db, per_plane):
    rows, model = og.shape
    width = wo.shape[0]
    return pl.pallas_call(
        functools.partial(middle_kernel, per_plane),
        in_specs=vmem_specs(10),
        out_specs=vmem_specs(9),
        out_shape=[
            jax.ShapeDtypeStruct((model, rows), BF),
            jax.ShapeDtypeStruct((rows, model), F32),
            jax.ShapeDtypeStruct((rows, model), BF),
            jax.ShapeDtypeStruct((2 * width, model // 2), BF),
            jax.ShapeDtypeStruct((model,), F32),
        ]
        + [jax.ShapeDtypeStruct((width, rows), BF)] * 4,
        scratch_shapes=[pltpu.VMEM((model // width, width, rows), BF)],
        compiler_params=params(),
        cost_estimate=cost(9 * 10**9, 6 * 10**6),
        name="middle_part",
    )(conv, sm2, x, og, gain, wo, ga, gb, da, db)


def glu_grad_kernel(per_plane, za, zb, zc, zd, oa, ob, oc, od, ga_ref, gb_ref, da_ref, db_ref, own_ref, other_ref):
    j = lax.div(lax.axis_index("seq"), per_plane)
    width = ga_ref.shape[2]
    xt = jnp.concatenate([ref[...] for ref in (za, zb, zc, zd)], axis=1)
    ot = jnp.concatenate([ref[width:, :] for ref in (oa, ob, oc, od)], axis=1)
    x = xt.astype(F32).T.astype(BF)
    og = ot.astype(F32).T.astype(BF)
    for g_ref, d_ref, out_ref in ((gb_ref, db_ref, other_ref), (ga_ref, da_ref, own_ref)):
        wg, wu = g_ref[j, 0], g_ref[j, 1]
        wd = d_ref[:, :width]
        for k in range(1, d_ref.shape[1] // width):
            wd = jnp.where(j == k, d_ref[:, column(k, width)], wd)
        gate = mm(x, wg)
        up = mm(x, wu)
        phi, e = erf_parts(gate)
        act = gate * phi
        hidden = (act * up).astype(BF)
        hg = mm_nt(og, wd)
        slope = phi + gate * (e * (1.0 / math.sqrt(2.0 * math.pi)))
        out_ref[0:width, :] = mm(xt, (hg * up * slope).astype(BF)).astype(out_ref.dtype)
        out_ref[width : 2 * width, :] = mm(xt, (hg * act).astype(BF)).astype(out_ref.dtype)
        out_ref[2 * width : 3 * width, :] = mm(ot, hidden).astype(out_ref.dtype)


def glu_grads(z_parts, o_parts, ga, gb, da, db, per_plane):
    width, half = ga.shape[2:]
    return pl.pallas_call(
        functools.partial(glu_grad_kernel, per_plane),
        in_specs=vmem_specs(12),
        out_specs=vmem_specs(2),
        out_shape=[
            jax.ShapeDtypeStruct((3 * width, half), F32),
            jax.ShapeDtypeStruct((3 * width, half), BF),
        ],
        compiler_params=params(),
        cost_estimate=cost(9 * 10**9, 4 * 10**6),
        name="glu_grads",
    )(*z_parts, *o_parts, ga, gb, da, db)


def plane_add_kernel(own_ref, other_ref, mine_ref, theirs_ref, out_ref):
    total = (own_ref[...] + other_ref[...].astype(F32)).astype(BF)
    extra = (mine_ref[...].astype(F32) + theirs_ref[...].astype(F32)).astype(BF)
    count = out_ref.shape[0]
    rows, more = total.shape[0] // count, extra.shape[0] // count
    for k in range(count):
        out_ref[k, :rows, :] = total[k * rows : (k + 1) * rows]
        out_ref[k, rows:, :] = extra[k * more : (k + 1) * more]


def plane_add(own, other, mine, theirs, count):
    half = own.shape[1]
    rows = (own.shape[0] + mine.shape[0]) // count
    return pl.pallas_call(
        plane_add_kernel,
        in_specs=vmem_specs(4),
        out_specs=vmem_specs(1)[0],
        out_shape=jax.ShapeDtypeStruct((count, rows, half), BF),
        compiler_params=params(),
        cost_estimate=cost(10**8, 2 * 10**6),
        name="plane_add",
    )(own, other, mine, theirs)


def plane_join_kernel(cut, a0, a1, a2, a3, out_ref):
    refs = (a0, a1, a2, a3)
    last = sum(ref[cut:, :].astype(F32) for ref in refs).astype(BF)
    if len(out_ref.shape) == 2:
        for z, ref in enumerate(refs):
            out_ref[z * cut : (z + 1) * cut, :] = ref[:cut, :]
        out_ref[4 * cut :, :] = last
        return
    for k in range(out_ref.shape[0]):
        for z, ref in enumerate(refs):
            out_ref[k, z * cut : (z + 1) * cut, :] = ref[:cut, :]
        out_ref[k, 4 * cut :, :] = last


def plane_join(parts, cut, copies=()):
    rows, half = parts[0].shape
    return pl.pallas_call(
        functools.partial(plane_join_kernel, cut),
        in_specs=vmem_specs(4),
        out_specs=vmem_specs(1)[0],
        out_shape=jax.ShapeDtypeStruct((*copies, 3 * cut + rows, half), BF),
        compiler_params=params(),
        cost_estimate=cost(10**8, 2 * 10**6),
        name="plane_join",
    )(*parts)


def plane_sum_kernel(x_ref, out_ref):
    out_ref[...] = sum(x_ref[k].astype(F32) for k in range(x_ref.shape[0])).astype(BF)


def plane_sum(parts):
    return pl.pallas_call(
        plane_sum_kernel,
        in_specs=vmem_specs(1),
        out_specs=vmem_specs(1)[0],
        out_shape=jax.ShapeDtypeStruct(parts.shape[1:], BF),
        compiler_params=params(),
        cost_estimate=cost(10**8, 2 * 10**6),
        name="plane_sum",
    )(parts)


def finish_kernel(per_plane, width, a_ref, half_ref, back_ref,
                  gi_ref, go_ref, wo_ref, in_ref, keep_ref, last_ref):
    seq = lax.axis_index("seq")
    plane = lax.div(seq, per_plane)
    blocks, pieces, cut, half = keep_ref.shape
    for k in range(pieces):
        for z in range(blocks):
            keep_ref[lax.bitwise_xor(plane, z), k] = a_ref[k, z * cut : (z + 1) * cut, :].astype(F32)
        last_ref[k] = a_ref[k, blocks * cut :, :].astype(F32)
    outs = []
    for j in range(blocks):
        block = jnp.concatenate([keep_ref[j, k] for k in range(pieces)], axis=0)
        gi_ref[j, :, 0, :] = block[:width]
        gi_ref[j, :, 1, :] = block[width : 2 * width]
        outs.append(block[2 * width : 3 * width].T)
    go_ref[...] = jnp.concatenate(outs, axis=1)
    wo_ref[: width // 2, :half] = last_ref[0]
    wo_ref[width // 2 :, :half] = last_ref[1]
    wo_ref[: width // 2, half:] = last_ref[2]
    wo_ref[width // 2 :, half:] = last_ref[3]
    count = half_ref.shape[0]
    me = lax.axis_index("tp")
    in_ref[pl.ds(pl.multiple_of(me * count, count), count), :] = half_ref[...]
    in_ref[pl.ds(pl.multiple_of((1 - me) * count, count), count), :] = back_ref[...]


def finish(sums, half_rows, other_rows, per_plane, width):
    half = sums.shape[2]
    model = 4 * width
    return pl.pallas_call(
        functools.partial(finish_kernel, per_plane, width),
        in_specs=vmem_specs(3),
        out_specs=vmem_specs(4),
        out_shape=[
            jax.ShapeDtypeStruct((4, width, 2, half), F32),
            jax.ShapeDtypeStruct((half, model), F32),
            jax.ShapeDtypeStruct((width, model), F32),
            jax.ShapeDtypeStruct((2 * half_rows.shape[0], model), BF),
        ],
        scratch_shapes=[pltpu.VMEM((4, 4, 3 * width // 4, half), F32), pltpu.VMEM((4, width // 2, half), F32)],
        compiler_params=params(),
        cost_estimate=cost(10**8, 6 * 10**6),
        name="finish",
    )(sums, half_rows, other_rows)


def in_unpack_kernel(place, turns, w_ref, gain_ref, *refs):
    tiles, (gi_ref, st_ref, gain_out, w1_ref, b1_ref, w2_ref, gain2_ref, keep_ref) = refs[:-8], refs[-8:]
    _, width, model = gi_ref.shape
    count, rows3, _ = keep_ref.shape
    small = None
    for ref, (turn,) in zip(tiles, turns):
        for z in range(4):
            keep_ref[source_of(place, turn, z)] = ref[z * rows3 : (z + 1) * rows3, :].astype(F32)
        part = ref[4 * rows3 :, :].astype(F32)
        small = part if small is None else small + part
    hidden = w2_ref.shape[0]
    more = small.shape[0]
    w2_ref[:more, :] = small[:, :LANES]
    w2_ref[more:, :] = small[: hidden - more, LANES:]
    rest = small[hidden - more : hidden - more + 8, LANES:]
    w1_ref[...] = rest[:5]
    b1_ref[...] = rest[5:6].reshape(-1)
    rest = small[hidden - more + 8 :, LANES:]
    for k in range(model // LANES):
        gain2_ref[k * LANES : (k + 1) * LANES] = rest[k : k + 1].reshape(-1)
    chans = rows3 // 3
    blocks = model // width
    per_block = count // blocks
    gains = []
    for j in range(blocks):
        acc = None
        for p in range(3):
            got = jnp.concatenate(
                [keep_ref[j * per_block + k, p * chans : (p + 1) * chans, :] for k in range(per_block)], axis=0
            )
            turned = got.T
            gi_ref[p, :, column(j, width)] = turned[:width]
            for k in range(3):
                st_ref[k, p : p + 1, column(j, width)] = turned[width + k : width + k + 1]
            part = turned[:width] * w_ref[p, :, column(j, width)].astype(F32)
            acc = part if acc is None else acc + part
        gains.append(jnp.sum(acc.T, axis=0, keepdims=True))
    gain_out[...] = (jnp.concatenate(gains, axis=1) / gain_ref[...].reshape(1, -1)).reshape(-1)


def in_unpack(tiles, turns, place, w, gain):
    rows3 = (tiles[0].shape[0] - SMALL_ROWS) // 4
    hidden = LANES
    count = 4 * len(tiles)
    _, width, model = w.shape
    return pl.pallas_call(
        functools.partial(in_unpack_kernel, place, turns),
        in_specs=vmem_specs(2 + len(tiles)),
        out_specs=vmem_specs(7),
        out_shape=[
            jax.ShapeDtypeStruct((3, width, model), F32),
            jax.ShapeDtypeStruct((3, 3, model), F32),
            jax.ShapeDtypeStruct((model,), F32),
            jax.ShapeDtypeStruct((5, hidden), F32),
            jax.ShapeDtypeStruct((hidden,), F32),
            jax.ShapeDtypeStruct((hidden, hidden), F32),
            jax.ShapeDtypeStruct((model,), F32),
        ],
        scratch_shapes=[pltpu.VMEM((count, rows3, 2 * LANES), F32)],
        compiler_params=params(),
        cost_estimate=cost(10**8, 4 * 10**6),
        name="in_unpack",
    )(w, gain, *tiles)


def mixer_back_kernel(by_source, pg_ref, mid_ref, x_ref, gain_ref, w_ref, in_ref):
    rows, model = mid_ref.shape
    width = w_ref.shape[1]
    blocks = model // width
    if by_source:
        pg = pg_ref[...].astype(F32)
        count, rows3, _ = pg.shape
        chans = rows3 // 3
        parts = [
            pg[:, p * chans : (p + 1) * chans, :].reshape(count * chans, rows).astype(BF) for p in range(3)
        ]
    else:
        parts = [pg_ref[p] for p in range(3)]
    grads = []
    for j in range(blocks):
        total = None
        for p in range(3):
            part = mm(w_ref[p, :, column(j, width)], parts[p][column(j, width)])
            total = part if total is None else total + part
        grads.append(total)
    n1_grad = jnp.concatenate(grads, axis=0).T
    xhat, r = norm_stats(own_part(x_ref, rows).astype(F32))
    in_ref[...] = (mid_ref[...] + norm_backward(n1_grad, gain_ref[...].reshape(1, -1), xhat, r)).astype(BF)


def mixer_back(pg, mid, x, gain, w, by_source):
    return pl.pallas_call(
        functools.partial(mixer_back_kernel, by_source),
        in_specs=vmem_specs(5),
        out_specs=vmem_specs(1)[0],
        out_shape=jax.ShapeDtypeStruct(mid.shape, BF),
        compiler_params=params(),
        cost_estimate=cost(3 * 10**9, 4 * 10**6),
        name="mixer_back",
    )(pg, mid, x, gain, w)


def after(x, *others):
    return lax.optimization_barrier((x,) + others)[0]


def permuted(x, axes, count, by):
    pairs = [(i, i + by) for i in range(count) if 0 <= i + by < count]
    return lax.ppermute(x, axes, pairs)


def swapped(x):
    return lax.ppermute(x, "tp", [(0, 1), (1, 0)])


def crossed(x, mask):
    devices = lax.axis_size("seq")
    return lax.ppermute(x, "seq", [(i, i ^ mask) for i in range(devices)])


def exchanged(x, axes, groups=None):
    return lax.all_to_all(x, axes, 0, 0, axis_index_groups=groups, tiled=True)


def gathered_over(x, count, groups=None):
    return exchanged(jnp.broadcast_to(x[None], (count,) + x.shape), "seq", groups)


def local(
    layer_input,
    mixer_gain,
    in_proj,
    short_taps,
    filter_w1,
    filter_b1,
    filter_w2,
    filter_w3,
    filter_decay,
    out_proj,
    glu_gain,
    glu_in,
    glu_out,
    out_grad,
):
    tok_rows, model = layer_input.shape
    width = in_proj.shape[0]
    blocks = model // width
    half = glu_out.shape[0]
    seq_devices = lax.axis_size("seq")
    tp_devices = lax.axis_size("tp")
    devices = seq_devices * tp_devices
    both = ("seq", "tp")
    rows = tok_rows // tp_devices
    seq_length = min(MIN_LEN, tok_rows * seq_devices)
    seqs = tok_rows * seq_devices // seq_length
    per_plane = seq_devices // blocks
    quick = per_plane == 4 and not SLOW_PATH
    place = (per_plane, quick)
    chans = model // devices
    chans_padded = -(-chans // GROUP) * GROUP
    spare = chans_padded - chans
    hidden = filter_w2.shape[0]
    tp_index = lax.axis_index("tp")
    linear = lax.axis_index("seq") * tp_devices + tp_index
    tables = transform_tables(seq_length)
    features = feature_table(seq_length)
    within = [[g * per_plane + r for r in range(per_plane)] for g in range(blocks)]

    halo = permuted(layer_input[tok_rows - 16 :], "seq", seq_devices, 1)

    w3t = filter_w3.T.reshape(tp_devices, chans, hidden)
    w3t = jnp.pad(w3t, ((0, 0), (0, spare), (0, 0))).reshape(tp_devices * chans_padded, hidden)
    decay = jnp.pad(filter_decay.reshape(tp_devices, chans), ((0, 0), (0, spare))).reshape(-1)
    lag_own, lag_other, *saved = filter_forward(features, filter_w1, filter_b1, filter_w2, w3t, decay)
    lag_back = swapped(lag_other)

    w_in = in_proj.transpose(1, 0, 2)
    conv_rows, sm2, *sent = mixer_in(
        layer_input, after(halo, lag_own), mixer_gain, w_in, short_taps, out_grad, per_plane, seq_length
    )

    def to_channels(x):
        out = exchanged(x.reshape(devices, chans, rows), both)
        return jnp.pad(out, ((0, 0), (0, spare), (0, 0)))

    def to_tokens(x):
        return exchanged(x[:, :chans], both).reshape(model, rows)

    conv_channels = to_channels(conv_rows)
    early = [sent[0]] + [crossed(sent[d], d * per_plane) for d in range(1, blocks)]
    glu_own = after(glu_in, conv_rows).transpose(0, 2, 1, 3)
    down_own = after(glu_out, conv_rows)
    glu_other = swapped(glu_own)
    down_other = swapped(down_own)
    spectrum = filter_spectrum(after(lag_own, glu_own), lag_back, tables)
    conv_out, signal_spec = conv_forward(after(conv_channels, spectrum), spectrum, tables, seqs)
    conv_tokens = to_tokens(conv_out)

    early = [after(x, conv_out) for x in early]
    rows_in = jnp.stack([x[:width] for x in early])
    if quick:
        plane_tiles = [rows_in] + [crossed(rows_in, d) for d in range(1, per_plane)]
        turns = [[(0, d)] for d in range(per_plane)]
    else:
        plane_tiles = [gathered_over(rows_in, per_plane, within).reshape(per_plane * blocks, width, rows)]
        turns = [[(0, r) for r in range(per_plane)]]
    gated_grad, mid, layer_output, extra, gain_sum, *sent = middle_part(
        conv_tokens, sm2, layer_input, out_grad, glu_gain, out_proj, glu_own, glu_other,
        down_own, down_other, per_plane
    )
    gated_channels = to_channels(gated_grad)
    across = lambda parts: [parts[0]] + [crossed(parts[d], d * per_plane) for d in range(1, blocks)]
    late = across(sent)
    extra_back = swapped(extra)
    plane_tiles = [after(x, gated_grad) for x in plane_tiles]
    tiles = plane_tiles + [swapped(x) for x in plane_tiles]
    turns = turns + [[(1, r) for _, r in t] for t in turns]
    turns = tuple(tuple(t) for t in turns)
    proj_channels, mixed_channels = channel_mixer(tiles, turns, place, w_in, short_taps, devices, seqs, chans)

    late = [after(x, proj_channels, gated_channels) for x in late]
    g_own, g_other = glu_grads(late, early, glu_own, glu_other, down_own, down_other, per_plane)
    g_back = swapped(g_other)
    if quick:
        sums = exchanged(plane_add(g_own, g_back, extra, extra_back, per_plane), "seq", within)

    pg, grad_spec, tap_sums = conv_backward(
        after(gated_channels, g_own), mixed_channels, proj_channels, conv_out, short_taps, spectrum, tables, seqs, chans
    )
    pg_sent = pg.reshape(devices, 3, chans_padded, rows)[:, :, :chans].reshape(devices, 3 * chans, rows)
    if quick:
        pg_sent = after(pg_sent, sums)
    pg_tokens = exchanged(pg_sent, both)
    if chans != chans_padded:
        pg_tokens = pg_tokens.reshape(devices, 3, chans, rows).transpose(1, 0, 2, 3).reshape(3, model, rows)

    if quick:
        glu_piece = plane_sum(after(sums, pg))
        glu_parts = across([glu_piece] * blocks)
        grad_spec = after(grad_spec, glu_piece)
    fg_own, fg_other = filter_grad_of(grad_spec, signal_spec, chans_padded, seq_length, tables, seqs)
    fg_back = swapped(fg_other)
    in_piece = in_grads(tiles, turns, place, pg, after(tap_sums, fg_own))
    in_piece, g3 = filter_backward(fg_own, fg_back, features, filter_w2, w3t, decay, saved, in_piece, gain_sum)
    g3_back = swapped(g3)
    if quick:
        in_parts = across([in_piece] * blocks)
        glu_parts = plane_join([after(x, in_piece) for x in glu_parts], 3 * width // per_plane, (per_plane,))
        glu_full = exchanged(glu_parts, "seq", within)
        pg_tokens = after(pg_tokens, glu_parts)
    input_half = mixer_back(pg_tokens, mid, layer_input, mixer_gain, w_in, chans == chans_padded)
    input_other = swapped(input_half)

    if quick:
        in_parts = plane_join([after(x, input_half) for x in in_parts], 3 * chans_padded)
        in_full = [in_parts] + [crossed(in_parts, d) for d in range(1, per_plane)]
        in_full = in_full + [swapped(x) for x in in_full]
        glu_in_grad, glu_out_grad, out_proj_grad, input_grad = finish(
            glu_full, input_half, input_other, per_plane, width
        )
        in_proj_grad, short_taps_grad, mixer_gain_grad, w1_grad, b1_grad, w2_grad, glu_gain_grad = in_unpack(
            [after(x, out_proj_grad) for x in in_full], turns, place, w_in, mixer_gain
        )
        in_proj_grad = in_proj_grad.transpose(1, 0, 2)
    else:
        total = (g_own + g_back.astype(F32)).astype(BF)
        piece = exchanged(total, "seq", within).reshape(per_plane, -1, half)
        piece = jnp.sum(piece.astype(F32), axis=0).astype(BF)
        full = gathered_over(piece, seq_devices).reshape(blocks, -1, half).astype(F32)
        glu_in_grad = full[:, : 2 * width].reshape(blocks, 2, width, half).transpose(0, 2, 1, 3)
        glu_out_grad = full[:, 2 * width :].transpose(2, 0, 1).reshape(half, model)
        total = (extra.astype(F32) + extra_back.astype(F32)).astype(BF)
        piece = exchanged(total, "seq").reshape(seq_devices, -1, model // 2)
        piece = jnp.sum(piece.astype(F32), axis=0).astype(BF)
        full = gathered_over(piece, seq_devices).reshape(2, width, model // 2).astype(F32)
        out_proj_grad = full.transpose(1, 0, 2).reshape(width, model)
        mine = gathered_over(in_piece, seq_devices)
        theirs = swapped(mine)
        pair = jnp.where(tp_index == 0, jnp.stack([mine, theirs], 1), jnp.stack([theirs, mine], 1)).astype(F32)
        pair = pair.reshape(devices, -1, 2 * LANES)
        small = jnp.sum(pair[:, 3 * chans_padded :], axis=0)
        small = jnp.concatenate([small[:, :LANES], small[:, LANES:]], axis=0)
        w1_grad, b1_grad, w2_grad = small[hidden : hidden + 5], small[hidden + 5], small[:hidden]
        glu_gain_grad = small[hidden + 8 : hidden + 8 + model // LANES].reshape(model)
        pair = pair[:, : 3 * chans_padded].reshape(devices, 3, chans_padded, 2 * LANES)[:, :, :chans]
        pair = pair.transpose(1, 0, 2, 3).reshape(3, model, 2 * LANES)
        in_proj_grad = pair[:, :, :width].transpose(2, 0, 1)
        short_taps_grad = pair[:, :, width : width + 3].transpose(2, 0, 1)
        products = in_proj_grad * in_proj.astype(F32)
        products = jnp.sum(products.reshape(width, 3, blocks, width), axis=(1, 3))
        mixer_gain_grad = products.T.reshape(model) / mixer_gain
        input_grad = jnp.where(
            tp_index == 0,
            jnp.concatenate([input_half, input_other], axis=0),
            jnp.concatenate([input_other, input_half], axis=0),
        )

    mine = g3[:chans] + g3_back[chans_padded : chans_padded + chans]
    theirs = g3[chans_padded : chans_padded + chans] + g3_back[:chans]
    g3_full = jnp.where(
        tp_index == 0, jnp.concatenate([mine, theirs], axis=0), jnp.concatenate([theirs, mine], axis=0)
    ).T
    return (
        layer_output,
        input_grad,
        mixer_gain_grad,
        in_proj_grad,
        short_taps_grad,
        w1_grad,
        b1_grad,
        w2_grad,
        g3_full,
        out_proj_grad,
        glu_gain_grad,
        glu_in_grad,
        glu_out_grad,
    )


def solution(mesh):
    placed = (
        P("seq", None),
        P(),
        P(),
        P(),
        P(),
        P(),
        P(),
        P(None, "seq"),
        P("seq"),
        P(),
        P(),
        P(None, None, None, "tp"),
        P("tp", None),
        P(("seq", "tp"), None),
    )
    return jax.shard_map(
        local,
        mesh=mesh,
        in_specs=placed,
        out_specs=(
            P(("seq", "tp"), None),
            P("seq", None),
            P(),
            P(),
            P(),
            P(),
            P(),
            P(),
            P(None, "seq"),
            P(),
            P(),
            P(None, None, None, "tp"),
            P("tp", None),
        ),
        check_vma=False,
    )
```

profile of v0, /device:TPU:0, one launch (start us, length us, event | category | flops | bytes accessed | tf_op | source)
XLA Modules:
  0.0 197.3 jit_solution(3351826434259973667)
XLA Ops:
  0.6 0.7 slice.27
  1.4 4.8 %collective-permute-start = (bf16[16,768]{1,0:T(8,128)(2,1)S(1)}, bf16[16,768]{1,0:T(8,128)(2,1)S(1)}, u32[]{:S(2)}, u32[]{:S(2)}) collective-permute-start(bf16[16,768]{1,0:T(8,128)(2,1)S(1)} %slice.27), channel_id=1, source_target_pairs={{0,2},{2,4},{4,6},{6,8},{8,10},{10,12},{12,14},{14,16},{16,18},{18... | collective-permute-start | bytes 73736 | tf_op jit(solution)/shard_map/ppermute | solution.py:1041
  6.2 8.5 %filter_forward.1 = (f32[24,4096]{1,0:T(8,128)}, f32[24,4096]{1,0:T(8,128)}, bf16[128,4096]{1,0:T(8,128)(2,1)}, bf16[128,4096]{1,0:T(8,128)(2,1)}, bf16[128,4096]{1,0:T(8,128)(2,1)}, /*index=5*/bf16[128,4096]{1,0:T(8,128)(2,1)}) custom-call(bf16[48,8192]{1,0:T(8,128)(2,1)} %constant.26.clone.feat_ref, f32[5,128]{1,0:T(8,128)} %w1_ref.1, f32[128]{0:T(128)} %b1_ref.1, ...), custom_call_target="tpu_custom_call" | custom-call | flops 400000000 | bytes 400000 | tf_op jit(solution)/shard_map/filter_forward/pallas_call | solution.py:223
  14.8 0.6 copy-done.37
  15.4 3.3 %mixer_in.1 = (bf16[768,128]{1,0:T(8,128)(2,1)}, f32[128,768]{1,0:T(8,128)}, bf16[384,128]{1,0:T(8,128)(2,1)}, bf16[384,128]{1,0:T(8,128)(2,1)}, bf16[384,128]{1,0:T(8,128)(2,1)}, /*index=5*/bf16[384,128]{1,0:T(8,128)(2,1)}) custom-call(bf16[256,768]{1,0:T(8,128)(2,1)} %x_ref.5, bf16[16,768]{1,0:T(8,128)(2,1)} %copy-done.37, f32[768]{0:T(1024)} %gain_ref.7, ...), custom_call_target="tpu_custom_call" | custom-call | flops 200000000 | bytes 200000 | tf_op jit(solution)/shard_map/mixer_in/pallas_call | solution.py:676
  19.0 0.7 copy-done.38
  19.7 5.2 %all-to-all-start = ((bf16[32,24,128]{2,1,0:T(8,128)(2,1)}), bf16[32,24,128]{2,1,0:T(8,128)(2,1)}, u32[]{:S(2)}, u32[]{:S(2)}) async-start(bf16[32,24,128]{2,1,0:T(8,128)(2,1)} %bitcast.2), calls=%async_computation | async-start | bytes 393216 | tf_op jit(solution)/shard_map/all_to_all | solution.py:1054
  24.9 1.8 collective-permute-start.4
  26.6 2.4 %collective-permute-start.5 = (bf16[384,128]{1,0:T(8,128)(2,1)}, bf16[384,128]{1,0:T(8,128)(2,1)}, u32[]{:S(2)}, u32[]{:S(2)}) collective-permute-start(bf16[384,128]{1,0:T(8,128)(2,1)} %get-tuple-element.113), channel_id=1, source_target_pairs={{0,16},{2,18},{4,20},{6,22},{8,24},{10,26},{12,28},{14,30},{16,0},... | collective-permute-start | bytes 294920 | tf_op jit(solution)/shard_map/ppermute | solution.py:1050
  29.3 4.4 %filter_spectrum.1.h_ref = f32[960,256]{1,0:T(8,128)} custom-call(f32[24,4096]{1,0:T(8,128)} %get-tuple-element.101.own_ref, f32[24,4096]{1,0:T(8,128)} %collective-permute-done.1.other_ref, bf16[640,512]{1,0:T(8,128)(2,1)} %constant.27.clone.fh, bf16[640,512]{1,0:T(8,128)(2,1)} %constant.28.clone.fl, f32[4,40,128]{2,1,0:T(8,128)} %constant.29.clone.tw, ...), custom_call_target="tpu_custom_call" | custom-call | flops 200000000 | bytes 200000 | tf_op jit(solution)/shard_map/filter_spectrum/pallas_call | solution.py:444
  34.2 5.4 %conv_forward.1 = (bf16[32,24,128]{2,1,0:T(8,128)(2,1)}, f32[960,256]{1,0:T(8,128)}) custom-call(bf16[32,24,128]{2,1,0:T(8,128)(2,1)} %all-to-all-done.x_ref, f32[960,256]{1,0:T(8,128)} %filter_spectrum.1.h_ref, bf16[640,512]{1,0:T(8,128)(2,1)} %constant.27.clone.fh, bf16[640,512]{1,0:T(8,128)(2,1)} %constant.28.clone.fl, f32[4,40,128]{2,1,0:T(8,128)} %constant.29.clone.tw, ...), custom_call_target="tpu_custom_call" | custom-call | flops 250000000 | bytes 300000 | tf_op jit(solution)/shard_map/conv_forward/pallas_call | solution.py:461
  39.6 5.7 %all-to-all-start.1 = ((bf16[32,24,128]{2,1,0:T(8,128)(2,1)}), bf16[32,24,128]{2,1,0:T(8,128)(2,1)}, u32[]{:S(2)}, u32[]{:S(2)}) async-start(bf16[32,24,128]{2,1,0:T(8,128)(2,1)} %get-tuple-element.104.y_ref), calls=%async_computation.1 | async-start | bytes 393216 | tf_op jit(solution)/shard_map/all_to_all | solution.py:1054
  45.3 0.8 slice_bitcast_fusion.2
  46.1 0.8 slice_bitcast_fusion
  47.0 0.7 pad_maximum_fusion.refs_0_
  47.7 2.4 %collective-permute-start.9 = (bf16[4,192,128]{2,1,0:T(8,128)(2,1)}, bf16[4,192,128]{2,1,0:T(8,128)(2,1)}, u32[]{:S(2)}, u32[]{:S(2)}) collective-permute-start(bf16[4,192,128]{2,1,0:T(8,128)(2,1)} %pad_maximum_fusion.refs_0_), channel_id=1, source_target_pairs={{0,6},{2,4},{4,2},{6,0},{8,14},{10,12},{12,10},{14,8},{16,22},{18,... | collective-permute-start | bytes 589832 | tf_op jit(solution)/shard_map/ppermute | solution.py:1050
  51.2 2.9 %all-to-all-done.1 = bf16[32,24,128]{2,1,0:T(8,128)(2,1)} async-done(((bf16[32,24,128]{2,1,0:T(8,128)(2,1)}), bf16[32,24,128]{2,1,0:T(8,128)(2,1)}, u32[]{:S(2)}, u32[]{:S(2)}) %all-to-all-start.1) | async-done | bytes 196640 | tf_op jit(solution)/shard_map/all_to_all | solution.py:1054
  54.1 1.0 copy-done.2
  55.1 7.8 %middle_part.1 = (bf16[768,128]{1,0:T(8,128)(2,1)}, f32[128,768]{1,0:T(8,128)}, bf16[128,768]{1,0:T(8,128)(2,1)}, bf16[384,384]{1,0:T(8,128)(2,1)}, f32[768]{0:T...) custom-call(bf16[768,128]{1,0:T(8,128)(2,1)} %bitcast.4.conv_ref, ...), custom_call_target="tpu_custom_call" | custom-call | flops 450000000 | bytes 300000 | tf_op jit(solution)/shard_map/middle_part/pallas_call | solution.py:761
  62.9 2.9 %all-to-all-start.2 = ((bf16[32,24,128]{2,1,0:T(8,128)(2,1)}), bf16[32,24,128]{2,1,0:T(8,128)(2,1)S(1)}, u32[]{:S(2)}, u32[]{:S(2)}) async-start(bf16[32,24,128]{2,1,0:T(8,128)(2,1)} %bitcast.26), calls=%async_computation.2 | async-start | bytes 393216 | tf_op jit(solution)/shard_map/all_to_all | solution.py:1054
  66.9 3.6 %collective-permute-start.16 = (bf16[192,128]{1,0:T(8,128)(2,1)}, bf16[192,128]{1,0:T(8,128)(2,1)S(1)}, u32[]{:S(2)}, u32[]{:S(2)}) collective-permute-start(bf16[192,128]{1,0:T(8,128)(2,1)} %get-tuple-element.128), channel_id=1, source_target_pairs={{0,24},{2,26},{4,28},{6,30},{8,16},{10,18},{12,20},{14,22},{16,8},... | collective-permute-start | bytes 147464 | tf_op jit(solution)/shard_map/ppermute | solution.py:1050
  70.5 1.2 collective-permute-start.14
  71.7 0.7 copy-done.11
  72.4 0.7 copy-done.12
  73.1 4.9 %channel_mixer.1 = (f32[32,72,128]{2,1,0:T(8,128)}, f32[32,72,128]{2,1,0:T(8,128)}) custom-call(bf16[3,192,768]{2,1,0:T(8,128)(2,1)} %bitcast.20, f32[3,3,768]{2,1,0:T(4,128)} %taps_ref.5, bf16[4,192,128]{2,1,0:T(8,128)(2,1)} %pad_maximum_fusion.refs_0_, bf16[4,192,128]{2,1,0:T(8,128)(2,1)} %collective-permute-done.7.refs_1_, ...), custom_call_target="tpu_custom_call" | custom-call | flops 150000000 | bytes 300000 | tf_op jit(solution)/shard_map/channel_mixer/pallas_call | solution.py:567
  78.7 6.1 %glu_grads.1 = (f32[576,384]{1,0:T(8,128)}, bf16[576,384]{1,0:T(8,128)(2,1)}) custom-call(bf16[192,128]{1,0:T(8,128)(2,1)} %get-tuple-element.123.za, bf16[192,128]{1,0:T(8,128)(2,1)} %copy-done.35, bf16[192,128]{1,0:T(8,128)(2,1)} %copy-done.34, bf16[192,128]{1,0:T(8,128)(2,1)} %copy-done.33, bf16[384,128]{1,0:T(8,128)(2,1)} %get-tuple-element.110.oa, ...), custom_call_target="tpu_custom_call" | custom-call | flops 450000000 | bytes 200000 | tf_op jit(solution)/shard_map/glu_grads/pallas_call | solution.py:806
  85.3 1.7 collective-permute-done.18.theirs_ref
  87.0 0.7 copy-done.17
  87.9 2.5 %plane_add.1 = bf16[4,240,384]{2,1,0:T(8,128)(2,1)} custom-call(f32[576,384]{1,0:T(8,128)} %get-tuple-element.130.own_ref, bf16[576,384]{1,0:T(8,128)(2,1)} %copy-done.14, bf16[384,384]{1,0:T(8,128)(2,1)} %get-tuple-element.132.mine_ref, bf16[384,384]{1,0:T(8,128)(2,1)} %copy-done.17), custom_call_target="tpu_custom_call" | custom-call | flops 5000000 | bytes 100000 | tf_op jit(solution)/shard_map/plane_add/pallas_call | solution.py:833
  90.4 3.7 %all-to-all-start.3 = ((bf16[4,240,384]{2,1,0:T(8,128)(2,1)}), bf16[4,240,384]{2,1,0:T(8,128)(2,1)S(1)}, u32[]{:S(2)}, u32[]{:S(2)}) async-start(bf16[4,240,384]{2,1,0:T(8,128)(2,1)} %plane_add.1), calls=%async_computation.3 | async-start | bytes 1474560 | tf_op jit(solution)/shard_map/all_to_all | solution.py:1054
  94.0 7.9 %conv_backward.1 = (bf16[32,72,128]{2,1,0:T(8,128)(2,1)}, f32[960,256]{1,0:T(8,128)}, f32[72,128]{1,0:T(8,128)}) custom-call(bf16[32,24,128]{2,1,0:T(8,128)(2,1)} %copy-done.8, f32[32,72,128]{2,1,0:T(8,128)} %get-tuple-element.134.sm_ref, f32[32,72,128]{2,1,0:T(8,128)} %get-tuple-element.122.p_ref, bf16[32,24,128]{2,1,0:T(8,128)(2,1)} %get-tuple-element.104.y_ref, ...), custom_call_target="tpu_custom_call" | custom-call | flops 350000000 | bytes 450000 | tf_op jit(solution)/shard_map/conv_backward/pallas_call | solution.py:478
  102.0 2.7 %all-to-all-done.3.x_ref = bf16[4,240,384]{2,1,0:T(8,128)(2,1)S(1)} async-done(((bf16[4,240,384]{2,1,0:T(8,128)(2,1)}), bf16[4,240,384]{2,1,0:T(8,128)(2,1)S(1)}, u32[]{:S(2)}, u32[]{:S(2)}) %all-to-all-start.3) | async-done | bytes 737312 | tf_op jit(solution)/shard_map/all_to_all | solution.py:1054
  104.7 4.7 %all-to-all-start.5 = ((bf16[32,72,128]{2,1,0:T(8,128)(2,1)}), bf16[32,72,128]{2,1,0:T(8,128)(2,1)S(1)}, u32[]{:S(2)}, u32[]{:S(2)}) async-start(bf16[32,72,128]{2,1,0:T(8,128)(2,1)} %get-tuple-element.154.pg_ref), calls=%async_computation.5 | async-start | bytes 1179648 | tf_op jit(solution)/shard_map/all_to_all | solution.py:1054
  109.4 1.9 plane_sum.1.a0
  111.3 5.0 %filter_grad.1 = (f32[24,4096]{1,0:T(8,128)}, f32[24,4096]{1,0:T(8,128)}) custom-call(f32[960,256]{1,0:T(8,128)} %get-tuple-element.138.spec_ref, f32[960,256]{1,0:T(8,128)} %get-tuple-element.139.saved_ref, f32[4,40,128]{2,1,0:T(8,128)} %constant.29.clone.tw, bf16[256,256]{1,0:T(8,128)(2,1)} %constant.32.clone.ih, bf16[256,256]{1,0:T(8,128)(2,1)} %constant.33.clone.il, ...), custom_call_target="tpu_custom_call" | custom-call | flops 250000000 | bytes 300000 | tf_op jit(solution)/shard_map/filter_grad/pallas_call | solution.py:496
  116.3 3.5 %collective-permute-start.22 = (bf16[240,384]{1,0:T(8,128)(2,1)S(1)}, bf16[240,384]{1,0:T(8,128)(2,1)S(1)}, u32[]{:S(2)}, u32[]{:S(2)}) collective-permute-start(bf16[240,384]{1,0:T(8,128)(2,1)S(1)} %copy-done.13), channel_id=1, source_target_pairs={{0,24},{2,26},{4,28},{6,30},{8,16},{10,18},{12,20},{14,22},{16,8},... | collective-permute-start | bytes 552968 | tf_op jit(solution)/shard_map/ppermute | solution.py:1050
  119.9 0.9 collective-permute-start.20
  120.7 2.9 %in_grads.1.piece_ref = bf16[72,256]{1,0:T(8,128)(2,1)} custom-call(bf16[32,72,128]{2,1,0:T(8,128)(2,1)} %get-tuple-element.154.pg_ref, f32[72,128]{1,0:T(8,128)} %get-tuple-element.147.st_ref, bf16[4,192,128]{2,1,0:T(8,128)(2,1)} %pad_maximum_fusion.refs_0_, bf16[4,192,128]{2,1,0:T(8,128)(2,1)} %collective-permute-done.7.refs_1_, ...), custom_call_target="tpu_custom_call" | custom-call | flops 150000000 | bytes 200000 | tf_op jit(solution)/shard_map/in_grads/pallas_call | solution.py:596
  123.7 0.7 copy-done.15
  124.4 6.6 %filter_backward.1 = (bf16[144,256]{1,0:T(8,128)(2,1)}, f32[48,128]{1,0:T(8,128)}) custom-call(f32[24,4096]{1,0:T(8,128)} %get-tuple-element.140.own_ref, f32[24,4096]{1,0:T(8,128)} %copy-done.15, bf16[48,8192]{1,0:T(8,128)(2,1)} %constant.26.clone.feat_ref, f32[128,128]{1,0:T(8,128)} %w2_ref.3, f32[48,128]{1,0:T(8,128)} %bitcast.28, f32[48]{0:T(128)} %decay_ref.3, ...), custom_call_target="tpu_custom_call" | custom-call | flops 400000000 | bytes 400000 | tf_op jit(solution)/shard_map/filter_backward/pallas_call | solution.py:267
  131.0 10.4 %collective-permute-done.21.a2 = bf16[240,384]{1,0:T(8,128)(2,1)S(1)} collective-permute-done((bf16[240,384]{1,0:T(8,128)(2,1)S(1)}, bf16[240,384]{1,0:T(8,128)(2,1)S(1)}, u32[]{:S(2)}, u32[]{:S(2)}) %collective-permute-start.21) | collective-permute-done | bytes 184352 | tf_op jit(solution)/shard_map/ppermute | solution.py:1050
  141.4 0.7 copy-done.27
  142.1 0.7 copy-done.28
  142.7 2.7 %plane_join.2 = bf16[4,672,384]{2,1,0:T(8,128)(2,1)} custom-call(bf16[240,384]{1,0:T(8,128)(2,1)} %plane_sum.1.a0, bf16[240,384]{1,0:T(8,128)(2,1)} %copy-done.28, bf16[240,384]{1,0:T(8,128)(2,1)} %copy-done.27, bf16[240,384]{1,0:T(8,128)(2,1)} %copy-done.26), custom_call_target="tpu_custom_call" | custom-call | flops 5000000 | bytes 100000 | tf_op jit(solution)/shard_map/plane_join/pallas_call | solution.py:860
  145.4 0.8 copy-done.4
  146.3 3.7 %all-to-all-start.4 = ((bf16[4,672,384]{2,1,0:T(8,128)(2,1)}), bf16[4,672,384]{2,1,0:T(8,128)(2,1)S(1)}, u32[]{:S(2)}, u32[]{:S(2)}) async-start(bf16[4,672,384]{2,1,0:T(8,128)(2,1)} %plane_join.2), calls=%async_computation.4 | async-start | bytes 4128768 | tf_op jit(solution)/shard_map/all_to_all | solution.py:1054
  149.9 1.5 collective-permute-start.26
  151.4 2.9 %collective-permute-start.24 = (bf16[144,256]{1,0:T(8,128)(2,1)S(1)}, bf16[144,256]{1,0:T(8,128)(2,1)S(1)}, u32[]{:S(2)}, u32[]{:S(2)}) collective-permute-start(bf16[144,256]{1,0:T(8,128)(2,1)S(1)} %copy-done.29), channel_id=1, source_target_pairs={{0,8},{2,10},{4,12},{6,14},{8,0},{10,2},{12,4},{14,6},{16,24},{18,... | collective-permute-start | bytes 221192 | tf_op jit(solution)/shard_map/ppermute | solution.py:1050
  154.3 3.0 %mixer_back.1.half_ref = bf16[128,768]{1,0:T(8,128)(2,1)} custom-call(bf16[32,72,128]{2,1,0:T(8,128)(2,1)} %copy-done.4, f32[128,768]{1,0:T(8,128)} %get-tuple-element.156.mid_ref, bf16[256,768]{1,0:T(8,128)(2,1)} %x_ref.5, f32[768]{0:T(1024)} %gain_ref.7, bf16[3,192,768]{2,1,0:T(8,128)(2,1)} %bitcast.21), custom_call_target="tpu_custom_call" | custom-call | flops 150000000 | bytes 200000 | tf_op jit(solution)/shard_map/mixer_back/pallas_call | solution.py:1024
  157.3 1.4 collective-permute-done.25.a2
  158.7 0.6 copy-done.31
  159.3 0.6 copy-done.32
  160.0 1.7 plane_join.3.refs_0_
  161.7 2.5 %collective-permute-start.29 = (bf16[360,256]{1,0:T(8,128)(2,1)}, bf16[360,256]{1,0:T(8,128)(2,1)S(1)}, u32[]{:S(2)}, u32[]{:S(2)}) collective-permute-start(bf16[360,256]{1,0:T(8,128)(2,1)} %plane_join.3.refs_0_), channel_id=1, source_target_pairs={{0,6},{2,4},{4,2},{6,0},{8,14},{10,12},{12,10},{14,8},{16,22},{18,... | collective-permute-start | bytes 552968 | tf_op jit(solution)/shard_map/ppermute | solution.py:1050
  165.7 0.8 collective-permute-done.34
  166.6 14.1 %collective-permute-done.29.refs_3_ = bf16[360,256]{1,0:T(8,128)(2,1)S(1)} collective-permute-done((bf16[360,256]{1,0:T(8,128)(2,1)}, bf16[360,256]{1,0:T(8,128)(2,1)S(1)}, u32[]{:S(2)}, u32[]{:S(2)}) %collective-permute-start.29) | collective-permute-done | bytes 184352 | tf_op jit(solution)/shard_map/ppermute | solution.py:1050
  180.8 1.5 collective-permute-done.28.refs_2_
  182.8 0.8 slice_add_fusion.1
  183.6 0.6 fusion
  184.2 0.7 copy-done.18
  184.9 1.3 copy-done.1
  186.1 4.8 %finish.1 = (f32[4,192,2,384]{3,2,1,0:T(2,128)}, f32[384,768]{1,0:T(8,128)}, f32[192,768]{1,0:T(8,128)}, bf16[256,768]{1,0:T(8,128)(2,1)}) custom-call(bf16[4,672,384]{2,1,0:T(8,128)(2,1)} %copy-done.1, bf16[128,768]{1,0:T(8,128)(2,1)} %mixer_back.1.half_ref, bf16[128,768]{1,0:T(8,128)(2,1)} %copy-done.18), custom_call_target="tpu_custom_call" | custom-call | flops 5000000 | bytes 300000 | tf_op jit(solution)/shard_map/finish/pallas_call | solution.py:916
  191.7 0.7 copy-done.22
  192.4 4.9 %in_unpack.1 = (f32[3,192,768]{2,1,0:T(8,128)}, f32[3,3,768]{2,1,0:T(4,128)}, f32[768]{0:T(1024)}, f32[5,128]{1,0:T(8,128)}, f32[128]{0:T(128)}, /*index=5*/f32[128,128]{1,0:T(8,128)}, f32[768]{0:T(1024)}) custom-call(bf16[3,192,768]{2,1,0:T(8,128)(2,1)} %bitcast.22, f32[768]{0:T(1024)} %gain_ref.7, bf16[360,256]{1,0:T(8,128)(2,1)} %plane_join.3.refs_0_, ...), custom_call_target="tpu_custom_call" | custom-call | flops 5000000 | bytes 200000 | tf_op jit(solution)/shard_map/in_unpack/pallas_call | solution.py:978
  (121 shorter events, 7.6 us)
Async XLA Ops:
  1.4 13.4 %collective-permute-start = (bf16[16,768]{1,0:T(8,128)(2,1)S(1)}, bf16[16,768]{1,0:T(8,128)(2,1)S(1)}, u32[]{:S(2)}, u32[]{:S(2)}) collective-permute-start(bf16[16,768]{1,0:T(8,128)(2,1)S(1)} %slice.27), channel_id=1, source_target_pairs={{0,2},{2,4},{4,6},{6,8},{8,10},{10,12},{12,14},{14,16},{16,18},{18... | collective-permute-start | bytes 73736 | tf_op jit(solution)/shard_map/ppermute | solution.py:1041
  6.2 12.5 %copy-start.7 = (bf16[4,192,2,384]{3,2,1,0:T(2,128)(2,1)S(1)}, bf16[4,192,2,384]{3,2,1,0:T(2,128)(2,1)}, u32[]{:S(2)}) copy-start(bf16[4,192,2,384]{3,2,1,0:T(2,128)(2,1)} %param.35) | copy-start | bytes 3538948
  18.7 1.0 copy-start.38
  18.7 10.6 %copy-start.5 = (bf16[384,768]{1,0:T(8,128)(2,1)S(1)}, bf16[384,768]{1,0:T(8,128)(2,1)}, u32[]{:S(2)}) copy-start(bf16[384,768]{1,0:T(8,128)(2,1)} %da_ref.1) | copy-start | bytes 1769476
  18.9 14.8 %copy-start = (bf16[4,192,2,384]{3,1,2,0:T(8,128)(2,1)}, bf16[4,192,2,384]{3,1,2,0:T(8,128)(2,1)S(1)}, u32[]{:S(2)}) copy-start(bf16[4,192,2,384]{3,1,2,0:T(8,128)(2,1)S(1)} %copy.39) | copy-start | bytes 3538948
  18.9 35.2 %collective-permute-start.2 = (bf16[4,2,192,384]{3,2,1,0:T(8,128)(2,1)S(1)}, bf16[4,2,192,384]{3,2,1,0:T(8,128)(2,1)S(1)}, u32[]{:S(2)}, u32[]{:S(2)}) collective-permute-start(bf16[4,2,192,384]{3,2,1,0:T(8,128)(2,1)S(1)} %bitcast.23), channel_id=1, source_target_pairs={{0,1},{1,0},{2,3},{3,2},{4,5},{5,4},{6,7},{7,6},{8,9},{9,8},{10,11... | collective-permute-start | bytes 3538952 | tf_op jit(solution)/shard_map/ppermute | solution.py:1045
  19.7 9.6 %collective-permute-start.1 = (f32[24,4096]{1,0:T(8,128)S(1)}, f32[24,4096]{1,0:T(8,128)}, u32[]{:S(2)}, u32[]{:S(2)}) collective-permute-start(f32[24,4096]{1,0:T(8,128)S(1)} %copy-done.38), channel_id=1, source_target_pairs={{0,1},{1,0},{2,3},{3,2},{4,5},{5,4},{6,7},{7,6},{8,9},{9,8},{10,11... | collective-permute-start | bytes 1179656 | tf_op jit(solution)/shard_map/ppermute | solution.py:1045
  19.7 14.5 %all-to-all-start = ((bf16[32,24,128]{2,1,0:T(8,128)(2,1)}), bf16[32,24,128]{2,1,0:T(8,128)(2,1)}, u32[]{:S(2)}, u32[]{:S(2)}) async-start(bf16[32,24,128]{2,1,0:T(8,128)(2,1)} %bitcast.2), calls=%async_computation | async-start | bytes 393216 | tf_op jit(solution)/shard_map/all_to_all | solution.py:1054
  24.9 20.4 %collective-permute-start.4 = (bf16[384,128]{1,0:T(8,128)(2,1)}, bf16[384,128]{1,0:T(8,128)(2,1)}, u32[]{:S(2)}, u32[]{:S(2)}) collective-permute-start(bf16[384,128]{1,0:T(8,128)(2,1)} %get-tuple-element.111), channel_id=1, source_target_pairs={{0,8},{2,10},{4,12},{6,14},{8,0},{10,2},{12,4},{14,6},{16,24},{18,... | collective-permute-start | bytes 294920 | tf_op jit(solution)/shard_map/ppermute | solution.py:1050
  26.6 19.5 %collective-permute-start.5 = (bf16[384,128]{1,0:T(8,128)(2,1)}, bf16[384,128]{1,0:T(8,128)(2,1)}, u32[]{:S(2)}, u32[]{:S(2)}) collective-permute-start(bf16[384,128]{1,0:T(8,128)(2,1)} %get-tuple-element.113), channel_id=1, source_target_pairs={{0,16},{2,18},{4,20},{6,22},{8,24},{10,26},{12,28},{14,30},{16,0},... | collective-permute-start | bytes 294920 | tf_op jit(solution)/shard_map/ppermute | solution.py:1050
  29.1 17.1 %collective-permute-start.6 = (bf16[384,128]{1,0:T(8,128)(2,1)}, bf16[384,128]{1,0:T(8,128)(2,1)}, u32[]{:S(2)}, u32[]{:S(2)}) collective-permute-start(bf16[384,128]{1,0:T(8,128)(2,1)} %get-tuple-element.115), channel_id=1, source_target_pairs={{0,24},{2,26},{4,28},{6,30},{8,16},{10,18},{12,20},{14,22},{16,8},... | collective-permute-start | bytes 294920 | tf_op jit(solution)/shard_map/ppermute | solution.py:1050
  29.3 21.8 %collective-permute-start.3 = (bf16[384,768]{1,0:T(8,128)(2,1)S(1)}, bf16[384,768]{1,0:T(8,128)(2,1)S(1)}, u32[]{:S(2)}, u32[]{:S(2)}) collective-permute-start(bf16[384,768]{1,0:T(8,128)(2,1)S(1)} %copy-done.5), channel_id=1, source_target_pairs={{0,1},{1,0},{2,3},{3,2},{4,5},{5,4},{6,7},{7,6},{8,9},{9,8},{10,11... | collective-permute-start | bytes 1769480 | tf_op jit(solution)/shard_map/ppermute | solution.py:1045
  39.6 14.5 %all-to-all-start.1 = ((bf16[32,24,128]{2,1,0:T(8,128)(2,1)}), bf16[32,24,128]{2,1,0:T(8,128)(2,1)}, u32[]{:S(2)}, u32[]{:S(2)}) async-start(bf16[32,24,128]{2,1,0:T(8,128)(2,1)} %get-tuple-element.104.y_ref), calls=%async_computation.1 | async-start | bytes 393216 | tf_op jit(solution)/shard_map/all_to_all | solution.py:1054
  47.7 18.1 %collective-permute-start.9 = (bf16[4,192,128]{2,1,0:T(8,128)(2,1)}, bf16[4,192,128]{2,1,0:T(8,128)(2,1)}, u32[]{:S(2)}, u32[]{:S(2)}) collective-permute-start(bf16[4,192,128]{2,1,0:T(8,128)(2,1)} %pad_maximum_fusion.refs_0_), channel_id=1, source_target_pairs={{0,6},{2,4},{4,2},{6,0},{8,14},{10,12},{12,10},{14,8},{16,22},{18,... | collective-permute-start | bytes 589832 | tf_op jit(solution)/shard_map/ppermute | solution.py:1050
  50.1 16.0 %collective-permute-start.8 = (bf16[4,192,128]{2,1,0:T(8,128)(2,1)}, bf16[4,192,128]{2,1,0:T(8,128)(2,1)}, u32[]{:S(2)}, u32[]{:S(2)}) collective-permute-start(bf16[4,192,128]{2,1,0:T(8,128)(2,1)} %pad_maximum_fusion.refs_0_), channel_id=1, source_target_pairs={{0,4},{2,6},{4,0},{6,2},{8,12},{10,14},{12,8},{14,10},{16,20},{18,... | collective-permute-start | bytes 589832 | tf_op jit(solution)/shard_map/ppermute | solution.py:1050
  50.7 15.7 %collective-permute-start.7 = (bf16[4,192,128]{2,1,0:T(8,128)(2,1)}, bf16[4,192,128]{2,1,0:T(8,128)(2,1)}, u32[]{:S(2)}, u32[]{:S(2)}) collective-permute-start(bf16[4,192,128]{2,1,0:T(8,128)(2,1)} %pad_maximum_fusion.refs_0_), channel_id=1, source_target_pairs={{0,2},{2,0},{4,6},{6,4},{8,10},{10,8},{12,14},{14,12},{16,18},{18,... | collective-permute-start | bytes 589832 | tf_op jit(solution)/shard_map/ppermute | solution.py:1050
  51.2 2.9 %copy-start.6 = (bf16[384,768]{1,0:T(8,128)(2,1)}, bf16[384,768]{1,0:T(8,128)(2,1)S(1)}, u32[]{:S(2)}) copy-start(bf16[384,768]{1,0:T(8,128)(2,1)S(1)} %collective-permute-done.3.db_ref) | copy-start | bytes 1769476
  54.1 1.0 copy-start.2
  62.9 15.1 %all-to-all-start.2 = ((bf16[32,24,128]{2,1,0:T(8,128)(2,1)}), bf16[32,24,128]{2,1,0:T(8,128)(2,1)S(1)}, u32[]{:S(2)}, u32[]{:S(2)}) async-start(bf16[32,24,128]{2,1,0:T(8,128)(2,1)} %bitcast.26), calls=%async_computation.2 | async-start | bytes 393216 | tf_op jit(solution)/shard_map/all_to_all | solution.py:1054
  65.8 4.7 %collective-permute-start.13 = (bf16[4,192,128]{2,1,0:T(8,128)(2,1)}, bf16[4,192,128]{2,1,0:T(8,128)(2,1)S(1)}, u32[]{:S(2)}, u32[]{:S(2)}) collective-permute-start(bf16[4,192,128]{2,1,0:T(8,128)(2,1)} %collective-permute-done.9.refs_3_), channel_id=1, source_target_pairs={{0,1},{1,0},{2,3},{3,2},{4,5},{5,4},{6,7},{7,6},{8,9},{9,8},{10,11... | collective-permute-start | bytes 589832 | tf_op jit(solution)/shard_map/ppermute | solution.py:1045
  66.1 4.4 %collective-permute-start.12 = (bf16[4,192,128]{2,1,0:T(8,128)(2,1)}, bf16[4,192,128]{2,1,0:T(8,128)(2,1)S(1)}, u32[]{:S(2)}, u32[]{:S(2)}) collective-permute-start(bf16[4,192,128]{2,1,0:T(8,128)(2,1)} %collective-permute-done.8.refs_2_), channel_id=1, source_target_pairs={{0,1},{1,0},{2,3},{3,2},{4,5},{5,4},{6,7},{7,6},{8,9},{9,8},{10,11... | collective-permute-start | bytes 589832 | tf_op jit(solution)/shard_map/ppermute | solution.py:1045
  66.4 5.3 %collective-permute-start.11 = (bf16[4,192,128]{2,1,0:T(8,128)(2,1)}, bf16[4,192,128]{2,1,0:T(8,128)(2,1)S(1)}, u32[]{:S(2)}, u32[]{:S(2)}) collective-permute-start(bf16[4,192,128]{2,1,0:T(8,128)(2,1)} %collective-permute-done.7.refs_1_), channel_id=1, source_target_pairs={{0,1},{1,0},{2,3},{3,2},{4,5},{5,4},{6,7},{7,6},{8,9},{9,8},{10,11... | collective-permute-start | bytes 589832 | tf_op jit(solution)/shard_map/ppermute | solution.py:1045
  66.6 5.1 %collective-permute-start.10 = (bf16[4,192,128]{2,1,0:T(8,128)(2,1)}, bf16[4,192,128]{2,1,0:T(8,128)(2,1)S(1)}, u32[]{:S(2)}, u32[]{:S(2)}) collective-permute-start(bf16[4,192,128]{2,1,0:T(8,128)(2,1)} %pad_maximum_fusion.refs_0_), channel_id=1, source_target_pairs={{0,1},{1,0},{2,3},{3,2},{4,5},{5,4},{6,7},{7,6},{8,9},{9,8},{10,11... | collective-permute-start | bytes 589832 | tf_op jit(solution)/shard_map/ppermute | solution.py:1045
  66.9 11.0 %collective-permute-start.16 = (bf16[192,128]{1,0:T(8,128)(2,1)}, bf16[192,128]{1,0:T(8,128)(2,1)S(1)}, u32[]{:S(2)}, u32[]{:S(2)}) collective-permute-start(bf16[192,128]{1,0:T(8,128)(2,1)} %get-tuple-element.128), channel_id=1, source_target_pairs={{0,24},{2,26},{4,28},{6,30},{8,16},{10,18},{12,20},{14,22},{16,8},... | collective-permute-start | bytes 147464 | tf_op jit(solution)/shard_map/ppermute | solution.py:1050
  70.5 1.2 copy-start.9
  70.5 7.5 %collective-permute-start.15 = (bf16[192,128]{1,0:T(8,128)(2,1)}, bf16[192,128]{1,0:T(8,128)(2,1)S(1)}, u32[]{:S(2)}, u32[]{:S(2)}) collective-permute-start(bf16[192,128]{1,0:T(8,128)(2,1)} %get-tuple-element.126), channel_id=1, source_target_pairs={{0,16},{2,18},{4,20},{6,22},{8,24},{10,26},{12,28},{14,30},{16,0},... | collective-permute-start | bytes 147464 | tf_op jit(solution)/shard_map/ppermute | solution.py:1050
  70.5 1.2 copy-start.10
  70.5 7.4 %collective-permute-start.14 = (bf16[192,128]{1,0:T(8,128)(2,1)}, bf16[192,128]{1,0:T(8,128)(2,1)S(1)}, u32[]{:S(2)}, u32[]{:S(2)}) collective-permute-start(bf16[192,128]{1,0:T(8,128)(2,1)} %get-tuple-element.124), channel_id=1, source_target_pairs={{0,8},{2,10},{4,12},{6,14},{8,0},{10,2},{12,4},{14,6},{16,24},{18,... | collective-permute-start | bytes 147464 | tf_op jit(solution)/shard_map/ppermute | solution.py:1050
  78.0 6.8 %copy-start.8 = (bf16[32,24,128]{2,1,0:T(8,128)(2,1)}, bf16[32,24,128]{2,1,0:T(8,128)(2,1)S(1)}, u32[]{:S(2)}) copy-start(bf16[32,24,128]{2,1,0:T(8,128)(2,1)S(1)} %all-to-all-done.2.g_ref) | copy-start | bytes 589828
  78.7 6.2 %copy-start.16 = (bf16[384,384]{1,0:T(8,128)(2,1)S(1)}, bf16[384,384]{1,0:T(8,128)(2,1)}, u32[]{:S(2)}) copy-start(bf16[384,384]{1,0:T(8,128)(2,1)} %get-tuple-element.132.mine_ref) | copy-start | bytes 884740
  84.8 2.3 %collective-permute-start.17 = (bf16[576,384]{1,0:T(8,128)(2,1)}, bf16[576,384]{1,0:T(8,128)(2,1)S(1)}, u32[]{:S(2)}, u32[]{:S(2)}) collective-permute-start(bf16[576,384]{1,0:T(8,128)(2,1)} %get-tuple-element.131), channel_id=1, source_target_pairs={{0,1},{1,0},{2,3},{3,2},{4,5},{5,4},{6,7},{7,6},{8,9},{9,8},{10,11... | collective-permute-start | bytes 1327112 | tf_op jit(solution)/shard_map/ppermute | solution.py:1045
  84.8 2.2 %collective-permute-start.18 = (bf16[384,384]{1,0:T(8,128)(2,1)S(1)}, bf16[384,384]{1,0:T(8,128)(2,1)S(1)}, u32[]{:S(2)}, u32[]{:S(2)}) collective-permute-start(bf16[384,384]{1,0:T(8,128)(2,1)S(1)} %copy-done.16), channel_id=1, source_target_pairs={{0,1},{1,0},{2,3},{3,2},{4,5},{5,4},{6,7},{7,6},{8,9},{9,8},{10,11... | collective-permute-start | bytes 884744 | tf_op jit(solution)/shard_map/ppermute | solution.py:1045
  87.0 0.9 copy-start.14
  90.4 14.3 %all-to-all-start.3 = ((bf16[4,240,384]{2,1,0:T(8,128)(2,1)}), bf16[4,240,384]{2,1,0:T(8,128)(2,1)S(1)}, u32[]{:S(2)}, u32[]{:S(2)}) async-start(bf16[4,240,384]{2,1,0:T(8,128)(2,1)} %plane_add.1), calls=%async_computation.3 | async-start | bytes 1474560 | tf_op jit(solution)/shard_map/all_to_all | solution.py:1054
  104.7 4.7 %copy-start.3 = (bf16[4,240,384]{2,1,0:T(8,128)(2,1)}, bf16[4,240,384]{2,1,0:T(8,128)(2,1)S(1)}, u32[]{:S(2)}) copy-start(bf16[4,240,384]{2,1,0:T(8,128)(2,1)S(1)} %all-to-all-done.3.x_ref) | copy-start | bytes 2211844
  104.7 40.7 %all-to-all-start.5 = ((bf16[32,72,128]{2,1,0:T(8,128)(2,1)}), bf16[32,72,128]{2,1,0:T(8,128)(2,1)S(1)}, u32[]{:S(2)}, u32[]{:S(2)}) async-start(bf16[32,72,128]{2,1,0:T(8,128)(2,1)} %get-tuple-element.154.pg_ref), calls=%async_computation.5 | async-start | bytes 1179648 | tf_op jit(solution)/shard_map/all_to_all | solution.py:1054
  111.3 5.0 %copy-start.13 = (bf16[240,384]{1,0:T(8,128)(2,1)S(1)}, bf16[240,384]{1,0:T(8,128)(2,1)}, u32[]{:S(2)}) copy-start(bf16[240,384]{1,0:T(8,128)(2,1)} %plane_sum.1.a0) | copy-start | bytes 552964
  116.3 7.4 %collective-permute-start.19 = (f32[24,4096]{1,0:T(8,128)}, f32[24,4096]{1,0:T(8,128)S(1)}, u32[]{:S(2)}, u32[]{:S(2)}) collective-permute-start(f32[24,4096]{1,0:T(8,128)} %get-tuple-element.141), channel_id=1, source_target_pairs={{0,1},{1,0},{2,3},{3,2},{4,5},{5,4},{6,7},{7,6},{8,9},{9,8},{10,11... | collective-permute-start | bytes 1179656 | tf_op jit(solution)/shard_map/ppermute | solution.py:1045
  116.3 14.7 %collective-permute-start.22 = (bf16[240,384]{1,0:T(8,128)(2,1)S(1)}, bf16[240,384]{1,0:T(8,128)(2,1)S(1)}, u32[]{:S(2)}, u32[]{:S(2)}) collective-permute-start(bf16[240,384]{1,0:T(8,128)(2,1)S(1)} %copy-done.13), channel_id=1, source_target_pairs={{0,24},{2,26},{4,28},{6,30},{8,16},{10,18},{12,20},{14,22},{16,8},... | collective-permute-start | bytes 552968 | tf_op jit(solution)/shard_map/ppermute | solution.py:1050
  119.9 21.5 %collective-permute-start.21 = (bf16[240,384]{1,0:T(8,128)(2,1)S(1)}, bf16[240,384]{1,0:T(8,128)(2,1)S(1)}, u32[]{:S(2)}, u32[]{:S(2)}) collective-permute-start(bf16[240,384]{1,0:T(8,128)(2,1)S(1)} %copy-done.13), channel_id=1, source_target_pairs={{0,16},{2,18},{4,20},{6,22},{8,24},{10,26},{12,28},{14,30},{16,0},... | collective-permute-start | bytes 552968 | tf_op jit(solution)/shard_map/ppermute | solution.py:1050
  119.9 21.5 %collective-permute-start.20 = (bf16[240,384]{1,0:T(8,128)(2,1)S(1)}, bf16[240,384]{1,0:T(8,128)(2,1)S(1)}, u32[]{:S(2)}, u32[]{:S(2)}) collective-permute-start(bf16[240,384]{1,0:T(8,128)(2,1)S(1)} %copy-done.13), channel_id=1, source_target_pairs={{0,8},{2,10},{4,12},{6,14},{8,0},{10,2},{12,4},{14,6},{16,24},{18,... | collective-permute-start | bytes 552968 | tf_op jit(solution)/shard_map/ppermute | solution.py:1050
  131.0 10.4 %copy-start.26 = (bf16[240,384]{1,0:T(8,128)(2,1)}, bf16[240,384]{1,0:T(8,128)(2,1)S(1)}, u32[]{:S(2)}) copy-start(bf16[240,384]{1,0:T(8,128)(2,1)S(1)} %collective-permute-done.22.a3) | copy-start | bytes 552964
  145.4 4.5 %copy-start.29 = (bf16[144,256]{1,0:T(8,128)(2,1)S(1)}, bf16[144,256]{1,0:T(8,128)(2,1)}, u32[]{:S(2)}) copy-start(bf16[144,256]{1,0:T(8,128)(2,1)} %get-tuple-element.158.a0) | copy-start | bytes 221188
  145.4 0.8 copy-start.4
  146.3 37.9 %all-to-all-start.4 = ((bf16[4,672,384]{2,1,0:T(8,128)(2,1)}), bf16[4,672,384]{2,1,0:T(8,128)(2,1)S(1)}, u32[]{:S(2)}, u32[]{:S(2)}) async-start(bf16[4,672,384]{2,1,0:T(8,128)(2,1)} %plane_join.2), calls=%async_computation.4 | async-start | bytes 4128768 | tf_op jit(solution)/shard_map/all_to_all | solution.py:1054
  149.9 7.4 %collective-permute-start.26 = (bf16[144,256]{1,0:T(8,128)(2,1)S(1)}, bf16[144,256]{1,0:T(8,128)(2,1)S(1)}, u32[]{:S(2)}, u32[]{:S(2)}) collective-permute-start(bf16[144,256]{1,0:T(8,128)(2,1)S(1)} %copy-done.29), channel_id=1, source_target_pairs={{0,24},{2,26},{4,28},{6,30},{8,16},{10,18},{12,20},{14,22},{16,8},... | collective-permute-start | bytes 221192 | tf_op jit(solution)/shard_map/ppermute | solution.py:1050
  151.4 7.3 %collective-permute-start.25 = (bf16[144,256]{1,0:T(8,128)(2,1)S(1)}, bf16[144,256]{1,0:T(8,128)(2,1)S(1)}, u32[]{:S(2)}, u32[]{:S(2)}) collective-permute-start(bf16[144,256]{1,0:T(8,128)(2,1)S(1)} %copy-done.29), channel_id=1, source_target_pairs={{0,16},{2,18},{4,20},{6,22},{8,24},{10,26},{12,28},{14,30},{16,0},... | collective-permute-start | bytes 221192 | tf_op jit(solution)/shard_map/ppermute | solution.py:1050
  151.4 7.3 %collective-permute-start.24 = (bf16[144,256]{1,0:T(8,128)(2,1)S(1)}, bf16[144,256]{1,0:T(8,128)(2,1)S(1)}, u32[]{:S(2)}, u32[]{:S(2)}) collective-permute-start(bf16[144,256]{1,0:T(8,128)(2,1)S(1)} %copy-done.29), channel_id=1, source_target_pairs={{0,8},{2,10},{4,12},{6,14},{8,0},{10,2},{12,4},{14,6},{16,24},{18,... | collective-permute-start | bytes 221192 | tf_op jit(solution)/shard_map/ppermute | solution.py:1050
  154.3 10.8 %copy-start.36 = (f32[48,128]{1,0:T(8,128)S(1)}, f32[48,128]{1,0:T(8,128)}, u32[]{:S(2)}) copy-start(f32[48,128]{1,0:T(8,128)} %get-tuple-element.177) | copy-start | bytes 73732
  157.3 1.4 copy-start.30
  161.7 19.1 %collective-permute-start.29 = (bf16[360,256]{1,0:T(8,128)(2,1)}, bf16[360,256]{1,0:T(8,128)(2,1)S(1)}, u32[]{:S(2)}, u32[]{:S(2)}) collective-permute-start(bf16[360,256]{1,0:T(8,128)(2,1)} %plane_join.3.refs_0_), channel_id=1, source_target_pairs={{0,6},{2,4},{4,2},{6,0},{8,14},{10,12},{12,10},{14,8},{16,22},{18,... | collective-permute-start | bytes 552968 | tf_op jit(solution)/shard_map/ppermute | solution.py:1050
  164.2 18.1 %collective-permute-start.28 = (bf16[360,256]{1,0:T(8,128)(2,1)}, bf16[360,256]{1,0:T(8,128)(2,1)S(1)}, u32[]{:S(2)}, u32[]{:S(2)}) collective-permute-start(bf16[360,256]{1,0:T(8,128)(2,1)} %plane_join.3.refs_0_), channel_id=1, source_target_pairs={{0,4},{2,6},{4,0},{6,2},{8,12},{10,14},{12,8},{14,10},{16,20},{18,... | collective-permute-start | bytes 552968 | tf_op jit(solution)/shard_map/ppermute | solution.py:1050
  164.8 17.6 %collective-permute-start.27 = (bf16[360,256]{1,0:T(8,128)(2,1)}, bf16[360,256]{1,0:T(8,128)(2,1)S(1)}, u32[]{:S(2)}, u32[]{:S(2)}) collective-permute-start(bf16[360,256]{1,0:T(8,128)(2,1)} %plane_join.3.refs_0_), channel_id=1, source_target_pairs={{0,2},{2,0},{4,6},{6,4},{8,10},{10,8},{12,14},{14,12},{16,18},{18,... | collective-permute-start | bytes 552968 | tf_op jit(solution)/shard_map/ppermute | solution.py:1050
  165.2 1.3 collective-permute-start.34
  165.2 19.0 %collective-permute-start.23 = (bf16[128,768]{1,0:T(8,128)(2,1)}, bf16[128,768]{1,0:T(8,128)(2,1)S(1)}, u32[]{:S(2)}, u32[]{:S(2)}) collective-permute-start(bf16[128,768]{1,0:T(8,128)(2,1)} %mixer_back.1.half_ref), channel_id=1, source_target_pairs={{0,1},{1,0},{2,3},{3,2},{4,5},{5,4},{6,7},{7,6},{8,9},{9,8},{10,11... | collective-permute-start | bytes 589832 | tf_op jit(solution)/shard_map/ppermute | solution.py:1045
  166.5 24.5 %collective-permute-start.30 = (bf16[360,256]{1,0:T(8,128)(2,1)}, bf16[360,256]{1,0:T(8,128)(2,1)S(1)}, u32[]{:S(2)}, u32[]{:S(2)}) collective-permute-start(bf16[360,256]{1,0:T(8,128)(2,1)} %plane_join.3.refs_0_), channel_id=1, source_target_pairs={{0,1},{1,0},{2,3},{3,2},{4,5},{5,4},{6,7},{7,6},{8,9},{9,8},{10,11... | collective-permute-start | bytes 552968 | tf_op jit(solution)/shard_map/ppermute | solution.py:1045
  180.7 10.3 %copy-start.19 = (bf16[360,256]{1,0:T(8,128)(2,1)}, bf16[360,256]{1,0:T(8,128)(2,1)S(1)}, u32[]{:S(2)}) copy-start(bf16[360,256]{1,0:T(8,128)(2,1)S(1)} %collective-permute-done.29.refs_3_) | copy-start | bytes 552964
  180.7 10.2 %collective-permute-start.33 = (bf16[360,256]{1,0:T(8,128)(2,1)S(1)}, bf16[360,256]{1,0:T(8,128)(2,1)S(1)}, u32[]{:S(2)}, u32[]{:S(2)}) collective-permute-start(bf16[360,256]{1,0:T(8,128)(2,1)S(1)} %collective-permute-done.29.refs_3_), channel_id=1, source_target_pairs={{0,1},{1,0},{2,3},{3,2},{4,5},{5,4},{6,7},{7,6},{8,9},{9,8},{10,11... | collective-permute-start | bytes 552968 | tf_op jit(solution)/shard_map/ppermute | solution.py:1045
  182.3 8.7 %copy-start.20 = (bf16[360,256]{1,0:T(8,128)(2,1)}, bf16[360,256]{1,0:T(8,128)(2,1)S(1)}, u32[]{:S(2)}) copy-start(bf16[360,256]{1,0:T(8,128)(2,1)S(1)} %collective-permute-done.28.refs_2_) | copy-start | bytes 552964
  182.3 8.7 %collective-permute-start.32 = (bf16[360,256]{1,0:T(8,128)(2,1)S(1)}, bf16[360,256]{1,0:T(8,128)(2,1)S(1)}, u32[]{:S(2)}, u32[]{:S(2)}) collective-permute-start(bf16[360,256]{1,0:T(8,128)(2,1)S(1)} %collective-permute-done.28.refs_2_), channel_id=1, source_target_pairs={{0,1},{1,0},{2,3},{3,2},{4,5},{5,4},{6,7},{7,6},{8,9},{9,8},{10,11... | collective-permute-start | bytes 552968 | tf_op jit(solution)/shard_map/ppermute | solution.py:1045
  182.4 8.7 %copy-start.21 = (bf16[360,256]{1,0:T(8,128)(2,1)}, bf16[360,256]{1,0:T(8,128)(2,1)S(1)}, u32[]{:S(2)}) copy-start(bf16[360,256]{1,0:T(8,128)(2,1)S(1)} %collective-permute-done.27.refs_1_) | copy-start | bytes 552964
  182.4 8.6 %collective-permute-start.31 = (bf16[360,256]{1,0:T(8,128)(2,1)S(1)}, bf16[360,256]{1,0:T(8,128)(2,1)S(1)}, u32[]{:S(2)}, u32[]{:S(2)}) collective-permute-start(bf16[360,256]{1,0:T(8,128)(2,1)S(1)} %collective-permute-done.27.refs_1_), channel_id=1, source_target_pairs={{0,1},{1,0},{2,3},{3,2},{4,5},{5,4},{6,7},{7,6},{8,9},{9,8},{10,11... | collective-permute-start | bytes 552968 | tf_op jit(solution)/shard_map/ppermute | solution.py:1045
  184.9 1.3 copy-start.1
  191.0 0.8 copy-start.25
  (16 other events, 10.7 us)
where the time goes:
time: 199 us; the launch traced here: 197 us
  Pallas kernels  84.1 us (42%)
  starting transfers between devices  58.5 us (29%)
  waiting for transfers between devices  36.2 us (18%)
  local copies, waits for them, and re-layouts  15.3 us (8%)
  other arithmetic  2.09 us (1%)
    ppermute x18, waiting for transfers between devices, crossed(): return lax.ppermute(x, 'seq', [(i, i ^ mask) for i in range(devices)])  27.5 us
    all_to_all x6, starting transfers between devices, exchanged(): return lax.all_to_all(x, axes, 0, 0, axis_index_groups=groups, tiled=True)  25.8 us
    ppermute x18, starting transfers between devices, crossed(): return lax.ppermute(x, 'seq', [(i, i ^ mask) for i in range(devices)])  25 us
    unnamed x78, local copies, waits for them, and re-layouts  12.7 us
    pallas_call x1, Pallas kernels, filter_forward(): pl.pallas_call(filter_forward_kernel, in_specs=vmem_specs(6), out_specs=v...  8.52 us
    pallas_call x1, Pallas kernels, conv_backward(): pl.pallas_call(functools.partial(conv_backward_kernel, padded, seqs, real...  7.92 us
    pallas_call x1, Pallas kernels, middle_part(): pl.pallas_call(functools.partial(middle_kernel, per_plane), in_specs=vmem...  7.8 us
    pallas_call x1, Pallas kernels, filter_backward(): pl.pallas_call(filter_backward_kernel, in_specs=vmem_specs(12), out_specs...  6.58 us
  transfers between devices with their start and end apart: 41, of which 10 were waited for; matrix products, arithmetic and copies ran while one was open for 2% of the time, Pallas kernels for 34%

commit v1 on v0

--- a/solution.py
+++ b/solution.py
@@ -17,7 +17,6 @@
 GROUP = 8
 FILTER_LANES = 2048
 SMALL_ROWS = 72
-VMEM_BYTES = 60 * 1024 * 1024
 BF = jnp.bfloat16
 F32 = jnp.float32
 
@@ -32,8 +31,8 @@
     return [pl.BlockSpec(memory_space=pltpu.VMEM)] * count
 
 
-def params(flops=0):
-    return pltpu.CompilerParams(vmem_limit_bytes=VMEM_BYTES)
+def params(mib=60):
+    return pltpu.CompilerParams(vmem_limit_bytes=mib * 1024 * 1024)
 
 
 def cost(flops, bytes_accessed=0, transcendentals=0):
@@ -83,6 +82,8 @@
     return {
         "forward": split_np(forward),
         "backward": split_np(backward),
+        "forward_used": split_np(forward[:, : first // 2 * GROUP]),
+        "backward_used": split_np(backward[: first // 2 * GROUP]),
         "twiddle": twiddle,
         "second": split_np(second),
         "inverse": split_np(second.T),
@@ -232,52 +233,6 @@
     )(features, w1, b1, w2, w3t, decay)
 
 
-def filter_backward_kernel(own_ref, other_ref, feat_ref, w2_ref, w3_ref, decay_ref, a_ref, ac_ref, b_ref, bc_ref, piece_ref, gain_ref, out_ref, g3_ref):
-    length = own_ref.shape[1]
-    width = min(FILTER_LANES, length)
-    begin = lax.axis_index("tp") * length
-    w2 = stacked_weights(w2_ref[...])
-    w3 = split(own_first(w3_ref))
-    decay = decay_columns(decay_ref)
-    g1 = g2 = g3 = 0.0
-    for lo in range(0, length, width):
-        lanes = slice(lo, lo + width)
-        start = pl.multiple_of(begin + lo, LANES)
-        grad = jnp.concatenate([own_ref[:, lanes], other_ref[:, lanes]], axis=0)
-        wh, wl = split(grad * lag_decay(decay, start, width, length))
-        second = b_ref[:, lanes]
-        g3 += mm_nt(wh, second) + mm_nt(wl, second)
-        pre2 = mm3_tn(w3, (wh, wl)) * bc_ref[:, lanes].astype(F32)
-        ph = pre2.astype(BF)
-        g2 += mm_nt(a_ref[:, lanes], ph)
-        pre1 = stacked_product(w2, pre2) * ac_ref[:, lanes].astype(F32)
-        g1 += mm_nt(feat_ref[:8, pl.ds(start, width)], pre1.astype(BF))
-    rows3 = piece_ref.shape[0]
-    more = out_ref.shape[0] - rows3
-    gains = [gain_ref[k * LANES : (k + 1) * LANES].reshape(1, LANES) for k in range(gain_ref.shape[0] // LANES)]
-    gains += [jnp.zeros((8 - len(gains), LANES), F32)]
-    right = jnp.concatenate([g2[more:], g1] + gains, axis=0)
-    small = jnp.concatenate([g2[:more], right], axis=1)
-    out_ref[...] = jnp.concatenate([piece_ref[...].astype(F32), small], axis=0).astype(BF)
-    g3_ref[...] = g3
-
-
-def filter_backward(own, other, features, w2, w3t, decay, saved, piece, gain):
-    hidden = w2.shape[0]
-    return pl.pallas_call(
-        filter_backward_kernel,
-        in_specs=vmem_specs(12),
-        out_specs=vmem_specs(2),
-        out_shape=[
-            jax.ShapeDtypeStruct((piece.shape[0] + SMALL_ROWS, 2 * hidden), BF),
-            jax.ShapeDtypeStruct((w3t.shape[0], hidden), F32),
-        ],
-        compiler_params=params(),
-        cost_estimate=cost(8 * 10**9, 8 * 10**6),
-        name="filter_backward",
-    )(own, other, features, w2, w3t, decay, *saved, piece, gain)
-
-
 def inner_spectrum(a, twiddle_ref, second, padded, columns):
     tc, ts = twiddle_ref[0], twiddle_ref[1]
     parts = []
@@ -379,13 +334,15 @@
     y_ref[...] = filtered(spec, h_ref, seqs, False, tw, ih, il, bh, bl, padded, x.shape).astype(BF)
 
 
-def conv_backward_kernel(padded, seqs, real, g_ref, sm_ref, p_ref, y_ref, taps_ref, h_ref, fh, fl, tw, sh, sl, ih, il, bh, bl,
-                         pg_ref, spec_ref, st_ref, icg_ref):
+def conv_backward_kernel(padded, seqs, real, g_ref, sm_ref, p_ref, y_ref, saved_ref, taps_ref, h_ref, fh, fl, tw, sh, sl, ih, il, bh, bl,
+                         pg_ref, cross_ref, st_ref, icg_ref):
     count, chans, _ = g_ref.shape
     gated = g_ref[...].astype(F32)
     conv_grad = gated * sm_ref[:, 2 * chans :, :]
     spec = signal_spectrum(conv_grad, seqs, fh, fl, tw, sh, sl, padded)
-    spec_ref[...] = spec
+    cross = product(spec, saved_ref[...], True)
+    height = cross_ref.shape[0]
+    cross_ref[...] = sum(cross[q * height : (q + 1) * height] for q in range(seqs))
     icg = filtered(spec, h_ref, seqs, True, tw, ih, il, bh, bl, padded, g_ref.shape)
     icg_ref[...] = icg.astype(BF).astype(F32)
     per_seq = count // seqs
@@ -417,28 +374,6 @@
     st_ref[...] = out
 
 
-def filter_grad_kernel(padded, seqs, spec_ref, saved_ref, tw, ih, il, bh, bl, own_ref, other_ref):
-    groups = own_ref.shape[0] // GROUP
-    rows = own_ref.shape[1] // LANES
-    used = rows * GROUP
-    height = groups * GROUP * padded
-    total = None
-    for q in range(seqs):
-        part = product(spec_ref[q * height : (q + 1) * height, :], saved_ref[q * height : (q + 1) * height, :], True)
-        total = part if total is None else total + part
-    me = lax.axis_index("tp")
-    halves = []
-    for half in (me, 1 - me):
-        begin = pl.multiple_of(half * used, LANES)
-        halves.append((bh[pl.ds(begin, used), :], bl[pl.ds(begin, used), :]))
-    for out_ref, y in zip((own_ref, other_ref), signal_of(total, (ih[...], il[...]), tw, halves, padded, groups)):
-        for g in range(groups):
-            for n in range(rows):
-                out_ref[g * GROUP : (g + 1) * GROUP, n * LANES : (n + 1) * LANES] = y[
-                    n * GROUP : (n + 1) * GROUP, g * LANES : (g + 1) * LANES
-                ]
-
-
 def filter_spectrum(own, other, tables):
     padded = tables["padded"]
     return pl.pallas_call(
@@ -453,7 +388,7 @@
 
 
 def transforms(tables):
-    return (*tables["forward"], tables["twiddle"], *tables["second"], *tables["inverse"], *tables["backward"])
+    return (*tables["forward_used"], tables["twiddle"], *tables["second"], *tables["inverse"], *tables["backward_used"])
 
 
 def conv_forward(x, spectrum, tables, seqs):
@@ -472,36 +407,23 @@
     )(x, spectrum, *transforms(tables))
 
 
-def conv_backward(gated, mixed, proj, conv_out, taps, spectrum, tables, seqs, real):
+def conv_backward(gated, mixed, proj, conv_out, saved, taps, spectrum, tables, seqs, real):
     padded = tables["padded"]
     count, chans, _ = gated.shape
     return pl.pallas_call(
         functools.partial(conv_backward_kernel, padded, seqs, real),
-        in_specs=vmem_specs(15),
+        in_specs=vmem_specs(16),
         out_specs=vmem_specs(3),
         out_shape=[
             jax.ShapeDtypeStruct((count, 3 * chans, LANES), BF),
-            jax.ShapeDtypeStruct((seqs * chans * padded, 2 * LANES), F32),
+            jax.ShapeDtypeStruct((chans * padded, 2 * LANES), F32),
             jax.ShapeDtypeStruct((3 * chans, LANES), F32),
         ],
         scratch_shapes=[pltpu.VMEM(gated.shape, F32)],
         compiler_params=params(),
         cost_estimate=cost(7 * 10**9, 9 * 10**6),
         name="conv_backward",
-    )(gated, mixed, proj, conv_out, taps, spectrum, *transforms(tables))
-
-
-def filter_grad_of(spec, saved, channels, seq_length, tables, seqs):
-    padded = tables["padded"]
-    return pl.pallas_call(
-        functools.partial(filter_grad_kernel, padded, seqs),
-        in_specs=vmem_specs(7),
-        out_specs=vmem_specs(2),
-        out_shape=[jax.ShapeDtypeStruct((channels, seq_length), F32)] * 2,
-        compiler_params=params(),
-        cost_estimate=cost(5 * 10**9, 6 * 10**6),
-        name="filter_grad",
-    )(spec, saved, tables["twiddle"], *tables["inverse"], *tables["backward"])
+    )(gated, mixed, proj, conv_out, saved, taps, spectrum, *transforms(tables))
 
 
 def source_of(place, turn, group):
@@ -575,8 +497,9 @@
     )(w, taps, *tiles)
 
 
-def in_grad_kernel(place, turns, pg_ref, st_ref, *refs):
-    tiles, (out_ref, keep_ref) = refs[:-2], refs[-2:]
+def channel_grads_kernel(place, turns, padded, count, pg_ref, st_ref, own_ref, other_ref, tw, ih, il, bh, bl, feat_ref, w2_ref,
+                         w3_ref, decay_ref, gain_ref, a_ref, ac_ref, b_ref, bc_ref, *refs):
+    tiles, (out_ref, g3_ref, keep_ref, lag_ref) = refs[:count], refs[count:]
     total = None
     for ref, turn_list in zip(tiles, turns):
         for q, turn in enumerate(turn_list):
@@ -584,25 +507,73 @@
             g = jnp.concatenate([pg_ref[source_of(place, turn, z)] for z in range(4)], axis=1)
             part = mm_nt(g, x)
             total = part if total is None else total + part
-    width = total.shape[1]
+    rows3, width = total.shape
     keep_ref[...] = jnp.zeros_like(keep_ref)
-    keep_ref[:, :width] = total
-    keep_ref[:, width : width + 3] = st_ref[:, :3]
+    keep_ref[:rows3, :width] = total
+    keep_ref[:rows3, width : width + 3] = st_ref[:, :3]
+
+    length = lag_ref.shape[1]
+    rows = length // LANES
+    used = rows * GROUP
+    channels = lag_ref.shape[0] // 2
+    groups = channels // GROUP
+    begin = pl.multiple_of(lax.axis_index("tp") * used, LANES)
+    back = (bh[pl.ds(begin, used), :], bl[pl.ds(begin, used), :])
+    for half, ref in enumerate((own_ref, other_ref)):
+        (y,) = signal_of(ref[...], (ih[...], il[...]), tw, [back], padded, groups)
+        for g in range(groups):
+            base = half * channels + g * GROUP
+            for n in range(rows):
+                lag_ref[base : base + GROUP, n * LANES : (n + 1) * LANES] = y[
+                    n * GROUP : (n + 1) * GROUP, g * LANES : (g + 1) * LANES
+                ]
+
+    span = min(FILTER_LANES, length)
+    begin = lax.axis_index("tp") * length
+    w2 = stacked_weights(w2_ref[...])
+    w3 = split(own_first(w3_ref))
+    decay = decay_columns(decay_ref)
+    g1 = g2 = g3 = 0.0
+    for lo in range(0, length, span):
+        lanes = slice(lo, lo + span)
+        start = pl.multiple_of(begin + lo, LANES)
+        wh, wl = split(lag_ref[:, lanes] * lag_decay(decay, start, span, length))
+        second = b_ref[:, lanes]
+        g3 += mm_nt(wh, second) + mm_nt(wl, second)
+        pre2 = mm3_tn(w3, (wh, wl)) * bc_ref[:, lanes].astype(F32)
+        g2 += mm_nt(a_ref[:, lanes], pre2.astype(BF))
+        pre1 = stacked_product(w2, pre2) * ac_ref[:, lanes].astype(F32)
+        g1 += mm_nt(feat_ref[:8, pl.ds(start, span)], pre1.astype(BF))
+    g3_ref[...] = g3
+    more = out_ref.shape[0] - rows3
+    gains = [gain_ref[k * LANES : (k + 1) * LANES].reshape(1, LANES) for k in range(gain_ref.shape[0] // LANES)]
+    gains += [jnp.zeros((8 - len(gains), LANES), F32)]
+    keep_ref[rows3:, :LANES] = g2[:more]
+    keep_ref[rows3:, LANES:] = jnp.concatenate([g2[more:], g1] + gains, axis=0)
     out_ref[...] = keep_ref[...].astype(BF)
 
 
-def in_grads(tiles, turns, place, pg, st):
+def channel_grads(tiles, turns, place, pg, st, own, other, tables, features, w2, w3t, decay, gain, saved):
     rows3 = pg.shape[1]
-    return pl.pallas_call(
-        functools.partial(in_grad_kernel, place, turns),
-        in_specs=vmem_specs(2 + len(tiles)),
-        out_specs=vmem_specs(1)[0],
-        out_shape=jax.ShapeDtypeStruct((rows3, 2 * LANES), BF),
-        scratch_shapes=[pltpu.VMEM((rows3, 2 * LANES), F32)],
+    hidden = w2.shape[0]
+    length = features.shape[1] // 2
+    return pl.pallas_call(
+        functools.partial(channel_grads_kernel, place, turns, tables["padded"], len(tiles)),
+        in_specs=vmem_specs(18 + len(tiles)),
+        out_specs=vmem_specs(2),
+        out_shape=[
+            jax.ShapeDtypeStruct((rows3 + SMALL_ROWS, 2 * LANES), BF),
+            jax.ShapeDtypeStruct((w3t.shape[0], hidden), F32),
+        ],
+        scratch_shapes=[
+            pltpu.VMEM((rows3 + SMALL_ROWS, 2 * LANES), F32),
+            pltpu.VMEM((w3t.shape[0], length), F32),
+        ],
         compiler_params=params(),
-        cost_estimate=cost(3 * 10**9, 4 * 10**6),
-        name="in_grads",
-    )(pg, st, *tiles)
+        cost_estimate=cost(8 * 10**9, 8 * 10**6),
+        name="channel_grads",
+    )(pg, st, own, other, tables["twiddle"], *tables["inverse"], *tables["backward"], features, w2, w3t, decay, gain,
+      *saved, *tiles)
 
 
 def erf_parts(g):
@@ -680,7 +651,7 @@
         out_shape=[jax.ShapeDtypeStruct((model, rows), BF), jax.ShapeDtypeStruct((rows, model), F32)]
         + [jax.ShapeDtypeStruct((2 * width, rows), BF)] * 4,
         scratch_shapes=[pltpu.VMEM((model // width, 2 * width, rows), BF)],
-        compiler_params=params(),
+        compiler_params=params(24),
         cost_estimate=cost(4 * 10**9, 4 * 10**6),
         name="mixer_in",
     )(x, halo, gain, w, taps, og)
@@ -811,7 +782,7 @@
             jax.ShapeDtypeStruct((3 * width, half), F32),
             jax.ShapeDtypeStruct((3 * width, half), BF),
         ],
-        compiler_params=params(),
+        compiler_params=params(40),
         cost_estimate=cost(9 * 10**9, 4 * 10**6),
         name="glu_grads",
     )(*z_parts, *o_parts, ga, gb, da, db)
@@ -835,7 +806,7 @@
         in_specs=vmem_specs(4),
         out_specs=vmem_specs(1)[0],
         out_shape=jax.ShapeDtypeStruct((count, rows, half), BF),
-        compiler_params=params(),
+        compiler_params=params(8),
         cost_estimate=cost(10**8, 2 * 10**6),
         name="plane_add",
     )(own, other, mine, theirs)
@@ -862,7 +833,7 @@
         in_specs=vmem_specs(4),
         out_specs=vmem_specs(1)[0],
         out_shape=jax.ShapeDtypeStruct((*copies, 3 * cut + rows, half), BF),
-        compiler_params=params(),
+        compiler_params=params(8),
         cost_estimate=cost(10**8, 2 * 10**6),
         name="plane_join",
     )(*parts)
@@ -878,7 +849,7 @@
         in_specs=vmem_specs(1),
         out_specs=vmem_specs(1)[0],
         out_shape=jax.ShapeDtypeStruct(parts.shape[1:], BF),
-        compiler_params=params(),
+        compiler_params=params(8),
         cost_estimate=cost(10**8, 2 * 10**6),
         name="plane_sum",
     )(parts)
@@ -924,20 +895,21 @@
             jax.ShapeDtypeStruct((2 * half_rows.shape[0], model), BF),
         ],
         scratch_shapes=[pltpu.VMEM((4, 4, 3 * width // 4, half), F32), pltpu.VMEM((4, width // 2, half), F32)],
-        compiler_params=params(),
+        compiler_params=params(32),
         cost_estimate=cost(10**8, 6 * 10**6),
         name="finish",
     )(sums, half_rows, other_rows)
 
 
-def in_unpack_kernel(place, turns, w_ref, gain_ref, *refs):
+def in_unpack_kernel(place, w_ref, gain_ref, *refs):
     tiles, (gi_ref, st_ref, gain_out, w1_ref, b1_ref, w2_ref, gain2_ref, keep_ref) = refs[:-8], refs[-8:]
     _, width, model = gi_ref.shape
     count, rows3, _ = keep_ref.shape
     small = None
-    for ref, (turn,) in zip(tiles, turns):
-        for z in range(4):
-            keep_ref[source_of(place, turn, z)] = ref[z * rows3 : (z + 1) * rows3, :].astype(F32)
+    for k, ref in enumerate(tiles):
+        half, z = divmod(k, 4)
+        for inner in range(4):
+            keep_ref[source_of(place, (half, inner), z)] = ref[inner * rows3 : (inner + 1) * rows3, :].astype(F32)
         part = ref[4 * rows3 :, :].astype(F32)
         small = part if small is None else small + part
     hidden = w2_ref.shape[0]
@@ -970,13 +942,13 @@
     gain_out[...] = (jnp.concatenate(gains, axis=1) / gain_ref[...].reshape(1, -1)).reshape(-1)
 
 
-def in_unpack(tiles, turns, place, w, gain):
+def in_unpack(tiles, place, w, gain):
     rows3 = (tiles[0].shape[0] - SMALL_ROWS) // 4
     hidden = LANES
     count = 4 * len(tiles)
     _, width, model = w.shape
     return pl.pallas_call(
-        functools.partial(in_unpack_kernel, place, turns),
+        functools.partial(in_unpack_kernel, place),
         in_specs=vmem_specs(2 + len(tiles)),
         out_specs=vmem_specs(7),
         out_shape=[
@@ -989,7 +961,7 @@
             jax.ShapeDtypeStruct((model,), F32),
         ],
         scratch_shapes=[pltpu.VMEM((count, rows3, 2 * LANES), F32)],
-        compiler_params=params(),
+        compiler_params=params(24),
         cost_estimate=cost(10**8, 4 * 10**6),
         name="in_unpack",
     )(w, gain, *tiles)
@@ -1026,7 +998,7 @@
         in_specs=vmem_specs(5),
         out_specs=vmem_specs(1)[0],
         out_shape=jax.ShapeDtypeStruct(mid.shape, BF),
-        compiler_params=params(),
+        compiler_params=params(16),
         cost_estimate=cost(3 * 10**9, 4 * 10**6),
         name="mixer_back",
     )(pg, mid, x, gain, w)
@@ -1156,8 +1128,9 @@
     if quick:
         sums = exchanged(plane_add(g_own, g_back, extra, extra_back, per_plane), "seq", within)
 
-    pg, grad_spec, tap_sums = conv_backward(
-        after(gated_channels, g_own), mixed_channels, proj_channels, conv_out, short_taps, spectrum, tables, seqs, chans
+    pg, cross, tap_sums = conv_backward(
+        after(gated_channels, g_own), mixed_channels, proj_channels, conv_out, signal_spec, short_taps, spectrum, tables,
+        seqs, chans
     )
     pg_sent = pg.reshape(devices, 3, chans_padded, rows)[:, :, :chans].reshape(devices, 3 * chans, rows)
     if quick:
@@ -1169,29 +1142,29 @@
     if quick:
         glu_piece = plane_sum(after(sums, pg))
         glu_parts = across([glu_piece] * blocks)
-        grad_spec = after(grad_spec, glu_piece)
-    fg_own, fg_other = filter_grad_of(grad_spec, signal_spec, chans_padded, seq_length, tables, seqs)
-    fg_back = swapped(fg_other)
-    in_piece = in_grads(tiles, turns, place, pg, after(tap_sums, fg_own))
-    in_piece, g3 = filter_backward(fg_own, fg_back, features, filter_w2, w3t, decay, saved, in_piece, gain_sum)
+        tap_sums = after(tap_sums, glu_piece)
+    cross_back = swapped(cross)
+    in_piece, g3 = channel_grads(
+        tiles, turns, place, pg, tap_sums, cross, cross_back, tables, features, filter_w2, w3t, decay, gain_sum, saved
+    )
     g3_back = swapped(g3)
     if quick:
-        in_parts = across([in_piece] * blocks)
+        in_parts = [in_piece] + [crossed(in_piece, d) for d in range(1, per_plane)]
         glu_parts = plane_join([after(x, in_piece) for x in glu_parts], 3 * width // per_plane, (per_plane,))
-        glu_full = exchanged(glu_parts, "seq", within)
-        pg_tokens = after(pg_tokens, glu_parts)
+        glu_full = exchanged(after(glu_parts, *in_parts), "seq", within)
+        in_parts = plane_join([after(x, glu_parts) for x in in_parts], 3 * chans_padded)
+        in_full = across([in_parts] * blocks)
+        pg_tokens = after(pg_tokens, in_parts)
     input_half = mixer_back(pg_tokens, mid, layer_input, mixer_gain, w_in, chans == chans_padded)
     input_other = swapped(input_half)
 
     if quick:
-        in_parts = plane_join([after(x, input_half) for x in in_parts], 3 * chans_padded)
-        in_full = [in_parts] + [crossed(in_parts, d) for d in range(1, per_plane)]
         in_full = in_full + [swapped(x) for x in in_full]
+        in_proj_grad, short_taps_grad, mixer_gain_grad, w1_grad, b1_grad, w2_grad, glu_gain_grad = in_unpack(
+            [after(x, input_half) for x in in_full], place, w_in, mixer_gain
+        )
         glu_in_grad, glu_out_grad, out_proj_grad, input_grad = finish(
-            glu_full, input_half, input_other, per_plane, width
-        )
-        in_proj_grad, short_taps_grad, mixer_gain_grad, w1_grad, b1_grad, w2_grad, glu_gain_grad = in_unpack(
-            [after(x, out_proj_grad) for x in in_full], turns, place, w_in, mixer_gain
+            after(glu_full, glu_gain_grad), input_half, input_other, per_plane, width
         )
         in_proj_grad = in_proj_grad.transpose(1, 0, 2)
     else:

time: 199 us -> 175 us (0.88)
  Pallas kernels: 84.1 us -> 67.4 us
  waiting for transfers between devices: 36.2 us -> 33 us
  local copies, waits for them, and re-layouts: 15.3 us -> 12.7 us
    pallas_call x4 -> x2, Pallas kernels: 19.3 us -> 15.2 us  [the longest x1 10.8 us: channel_grads(): pl.pallas_call(functools.partial(channel_grads_kernel, place, turns, tabl...]
    unnamed x78 -> x70, local copies, waits for them, and re-layouts: 12.7 us -> 10 us
    ppermute x18, waiting for transfers between devices: 27.5 us -> 25 us  [crossed(): return lax.ppermute(x, 'seq', [(i, i ^ mask) for i in range(devices)])]
    pallas_call x1, Pallas kernels: 3 us -> 0.71 us  [mixer_back(): pl.pallas_call(functools.partial(mixer_back_kernel, by_source), in_specs=...]
    pallas_call x1, Pallas kernels: 6.09 us -> 3.89 us  [glu_grads(): pl.pallas_call(functools.partial(glu_grad_kernel, per_plane), in_specs=vm...]
    pallas_call x2, Pallas kernels: 4.37 us -> 2.21 us  [plane_join(): pl.pallas_call(functools.partial(plane_join_kernel, cut), in_specs=vmem_s...]
  transfers between devices with their start and end apart: 41 -> 41, of which waited for: 10 -> 8; matrix products, arithmetic and copies ran while one was open for 2% -> 2% of each run, Pallas kernels for 34% -> 33%
where the time goes in v1:
time: 175 us; the launch traced here: 173 us
  Pallas kernels  67.4 us (39%)
  starting transfers between devices  57.3 us (33%)
  waiting for transfers between devices  33 us (19%)
  local copies, waits for them, and re-layouts  12.7 us (7%)
  other arithmetic  2.09 us (1%)
    ppermute x18, starting transfers between devices, crossed(): return lax.ppermute(x, 'seq', [(i, i ^ mask) for i in range(devices)])  25.2 us
    ppermute x18, waiting for transfers between devices, crossed(): return lax.ppermute(x, 'seq', [(i, i ^ mask) for i in range(devices)])  25 us
    all_to_all x6, starting transfers between devices, exchanged(): return lax.all_to_all(x, axes, 0, 0, axis_index_groups=groups, tiled=True)  24.3 us
    pallas_call x1, Pallas kernels, channel_grads(): pl.pallas_call(functools.partial(channel_grads_kernel, place, turns, tabl...  10.8 us
    unnamed x70, local copies, waits for them, and re-layouts  10 us
    pallas_call x1, Pallas kernels, filter_forward(): pl.pallas_call(filter_forward_kernel, in_specs=vmem_specs(6), out_specs=v...  8.42 us
    pallas_call x1, Pallas kernels, conv_backward(): pl.pallas_call(functools.partial(conv_backward_kernel, padded, seqs, real...  7.94 us
    pallas_call x1, Pallas kernels, middle_part(): pl.pallas_call(functools.partial(middle_kernel, per_plane), in_specs=vmem...  7.87 us
  transfers between devices with their start and end apart: 41, of which 8 were waited for; matrix products, arithmetic and copies ran while one was open for 2% of the time, Pallas kernels for 33%

profile of v1, /device:TPU:0, one launch (start us, length us, event | category | flops | bytes accessed | tf_op | source)
XLA Modules:
  0.0 173.5 jit_solution(4313156036652989928)
XLA Ops:
  0.7 0.8 slice.27
  1.5 4.8 %collective-permute-start = (bf16[16,768]{1,0:T(8,128)(2,1)S(1)}, bf16[16,768]{1,0:T(8,128)(2,1)S(1)}, u32[]{:S(2)}, u32[]{:S(2)}) collective-permute-start(bf16[16,768]{1,0:T(8,128)(2,1)S(1)} %slice.27), channel_id=1, source_target_pairs={{0,2},{2,4},{4,6},{6,8},{8,10},{10,12},{12,14},{14,16},{16,18},{18... | collective-permute-start | bytes 73736 | tf_op jit(solution)/shard_map/ppermute | solution.py:1013
  6.4 8.4 %filter_forward.1 = (f32[24,4096]{1,0:T(8,128)}, f32[24,4096]{1,0:T(8,128)}, bf16[128,4096]{1,0:T(8,128)(2,1)}, bf16[128,4096]{1,0:T(8,128)(2,1)}, bf16[128,4096]{1,0:T(8,128)(2,1)}, /*index=5*/bf16[128,4096]{1,0:T(8,128)(2,1)}) custom-call(bf16[48,8192]{1,0:T(8,128)(2,1)} %constant.34.clone.feat_ref, f32[5,128]{1,0:T(8,128)} %w1_ref.1, f32[128]{0:T(128)} %b1_ref.1, ...), custom_call_target="tpu_custom_call" | custom-call | flops 400000000 | bytes 400000 | tf_op jit(solution)/shard_map/filter_forward/pallas_call | solution.py:224
  14.9 1.9 %mixer_in.1 = (bf16[768,128]{1,0:T(8,128)(2,1)}, f32[128,768]{1,0:T(8,128)S(1)}, bf16[384,128]{1,0:T(8,128)(2,1)S(1)}, bf16[384,128]{1,0:T(8,128)(2,1)}, bf16[38...) custom-call(bf16[256,768]{1,0:T(8,128)(2,1)S(1)} %copy-done.6, bf16[16,768]{1,0:T(8,128)(2,1)S(1)} %collective-permute-done.halo_ref, ...), custom_call_target="tpu_custom_call" | custom-call | flops 200000000 | bytes 200000 | tf_op jit(solution)/shard_map/mixer_in/pallas_call | solution.py:647
  16.9 0.6 copy-done.16
  17.5 0.4 copy-done.34
  18.0 5.1 %all-to-all-start = ((bf16[32,24,128]{2,1,0:T(8,128)(2,1)}), bf16[32,24,128]{2,1,0:T(8,128)(2,1)}, u32[]{:S(2)}, u32[]{:S(2)}) async-start(bf16[32,24,128]{2,1,0:T(8,128)(2,1)} %bitcast.2), calls=%async_computation | async-start | bytes 393216 | tf_op jit(solution)/shard_map/all_to_all | solution.py:1026
  23.1 1.8 %collective-permute-start.4 = (bf16[384,128]{1,0:T(8,128)(2,1)}, bf16[384,128]{1,0:T(8,128)(2,1)}, u32[]{:S(2)}, u32[]{:S(2)}) collective-permute-start(bf16[384,128]{1,0:T(8,128)(2,1)} %get-tuple-element.110), channel_id=1, source_target_pairs={{0,8},{2,10},{4,12},{6,14},{8,0},{10,2},{12,4},{14,6},{16,24},{18,... | collective-permute-start | bytes 294920 | tf_op jit(solution)/shard_map/ppermute | solution.py:1022
  24.9 2.4 %collective-permute-start.5 = (bf16[384,128]{1,0:T(8,128)(2,1)}, bf16[384,128]{1,0:T(8,128)(2,1)}, u32[]{:S(2)}, u32[]{:S(2)}) collective-permute-start(bf16[384,128]{1,0:T(8,128)(2,1)} %get-tuple-element.112), channel_id=1, source_target_pairs={{0,16},{2,18},{4,20},{6,22},{8,24},{10,26},{12,28},{14,30},{16,0},... | collective-permute-start | bytes 294920 | tf_op jit(solution)/shard_map/ppermute | solution.py:1022
  27.6 4.2 %filter_spectrum.1.h_ref = f32[960,256]{1,0:T(8,128)} custom-call(f32[24,4096]{1,0:T(8,128)} %get-tuple-element.100.own_ref, f32[24,4096]{1,0:T(8,128)} %collective-permute-done.1.other_ref, bf16[640,512]{1,0:T(8,128)(2,1)} %constant.35.clone.fh, bf16[640,512]{1,0:T(8,128)(2,1)} %constant.36.clone.fl, f32[4,40,128]{2,1,0:T(8,128)} %constant.37.clone.tw, ...), custom_call_target="tpu_custom_call" | custom-call | flops 200000000 | bytes 200000 | tf_op jit(solution)/shard_map/filter_spectrum/pallas_call | solution.py:379
  31.8 0.6 all-to-all-done.x_ref
  32.4 5.0 %conv_forward.1 = (bf16[32,24,128]{2,1,0:T(8,128)(2,1)}, f32[960,256]{1,0:T(8,128)}) custom-call(bf16[32,24,128]{2,1,0:T(8,128)(2,1)} %all-to-all-done.x_ref, f32[960,256]{1,0:T(8,128)} %filter_spectrum.1.h_ref, bf16[640,256]{1,0:T(8,128)(2,1)} %constant.40.clone.fh, bf16[640,256]{1,0:T(8,128)(2,1)} %constant.41.clone.fl, f32[4,40,128]{2,1,0:T(8,128)} %constant.37.clone.tw, ...), custom_call_target="tpu_custom_call" | custom-call | flops 250000000 | bytes 300000 | tf_op jit(solution)/shard_map/conv_forward/pallas_call | solution.py:396
  37.4 5.6 %all-to-all-start.1 = ((bf16[32,24,128]{2,1,0:T(8,128)(2,1)}), bf16[32,24,128]{2,1,0:T(8,128)(2,1)}, u32[]{:S(2)}, u32[]{:S(2)}) async-start(bf16[32,24,128]{2,1,0:T(8,128)(2,1)} %get-tuple-element.103.y_ref), calls=%async_computation.1 | async-start | bytes 393216 | tf_op jit(solution)/shard_map/all_to_all | solution.py:1026
  43.0 0.8 slice_bitcast_fusion.2
  43.8 0.8 slice_bitcast_fusion
  44.7 0.7 pad_maximum_fusion.refs_0_
  45.4 2.4 %collective-permute-start.9 = (bf16[4,192,128]{2,1,0:T(8,128)(2,1)}, bf16[4,192,128]{2,1,0:T(8,128)(2,1)}, u32[]{:S(2)}, u32[]{:S(2)}) collective-permute-start(bf16[4,192,128]{2,1,0:T(8,128)(2,1)} %pad_maximum_fusion.refs_0_), channel_id=1, source_target_pairs={{0,6},{2,4},{4,2},{6,0},{8,14},{10,12},{12,10},{14,8},{16,22},{18,... | collective-permute-start | bytes 589832 | tf_op jit(solution)/shard_map/ppermute | solution.py:1022
  47.8 0.6 collective-permute-start.8
  48.4 0.5 collective-permute-start.7
  48.9 2.9 %all-to-all-done.1 = bf16[32,24,128]{2,1,0:T(8,128)(2,1)} async-done(((bf16[32,24,128]{2,1,0:T(8,128)(2,1)}), bf16[32,24,128]{2,1,0:T(8,128)(2,1)}, u32[]{:S(2)}, u32[]{:S(2)}) %all-to-all-start.1) | async-done | bytes 196640 | tf_op jit(solution)/shard_map/all_to_all | solution.py:1026
  51.8 1.0 copy-done.4
  52.8 7.9 %middle_part.1 = (bf16[768,128]{1,0:T(8,128)(2,1)}, f32[128,768]{1,0:T(8,128)}, bf16[128,768]{1,0:T(8,128)(2,1)}, bf16[384,384]{1,0:T(8,128)(2,1)}, f32[768]{0:T...) custom-call(bf16[768,128]{1,0:T(8,128)(2,1)} %bitcast.4.conv_ref, ...), custom_call_target="tpu_custom_call" | custom-call | flops 450000000 | bytes 300000 | tf_op jit(solution)/shard_map/middle_part/pallas_call | solution.py:732
  60.7 2.9 %all-to-all-start.2 = ((bf16[32,24,128]{2,1,0:T(8,128)(2,1)}), bf16[32,24,128]{2,1,0:T(8,128)(2,1)S(1)}, u32[]{:S(2)}, u32[]{:S(2)}) async-start(bf16[32,24,128]{2,1,0:T(8,128)(2,1)} %bitcast.26), calls=%async_computation.2 | async-start | bytes 393216 | tf_op jit(solution)/shard_map/all_to_all | solution.py:1026
  64.7 3.6 %collective-permute-start.16 = (bf16[192,128]{1,0:T(8,128)(2,1)}, bf16[192,128]{1,0:T(8,128)(2,1)S(1)}, u32[]{:S(2)}, u32[]{:S(2)}) collective-permute-start(bf16[192,128]{1,0:T(8,128)(2,1)} %get-tuple-element.127), channel_id=1, source_target_pairs={{0,24},{2,26},{4,28},{6,30},{8,16},{10,18},{12,20},{14,22},{16,8},... | collective-permute-start | bytes 147464 | tf_op jit(solution)/shard_map/ppermute | solution.py:1022
  68.4 1.2 collective-permute-start.14
  69.6 4.9 %channel_mixer.1 = (f32[32,72,128]{2,1,0:T(8,128)}, f32[32,72,128]{2,1,0:T(8,128)}) custom-call(bf16[3,192,768]{2,1,0:T(8,128)(2,1)} %bitcast.19, f32[3,3,768]{2,1,0:T(4,128)} %taps_ref.5, bf16[4,192,128]{2,1,0:T(8,128)(2,1)} %pad_maximum_fusion.refs_0_, bf16[4,192,128]{2,1,0:T(8,128)(2,1)} %collective-permute-done.7.refs_1_, ...), custom_call_target="tpu_custom_call" | custom-call | flops 150000000 | bytes 300000 | tf_op jit(solution)/shard_map/channel_mixer/pallas_call | solution.py:489
  74.5 1.3 collective-permute-done.15.zc
  75.8 1.1 copy-done.13
  76.9 3.9 %glu_grads.1 = (f32[576,384]{1,0:T(8,128)S(1)}, bf16[576,384]{1,0:T(8,128)(2,1)S(1)}) custom-call(bf16[192,128]{1,0:T(8,128)(2,1)S(1)} %copy-done.26, bf16[192,128]{1,0:T(8,128)(2,1)S(1)} %collective-permute-done.14.zb, bf16[192,128]{1,0:T(8,128)(2,1)S(1)} %collective-permute-done.15.zc, bf16[192,128]{1,0:T(8,128)(2,1)S(1)} %collective-permute-done.16.zd, ...), custom_call_target="tpu_custom_call" | custom-call | flops 450000000 | bytes 200000 | tf_op jit(solution)/shard_map/glu_grads/pallas_call | solution.py:777
  80.9 0.5 collective-permute-start.18
  81.4 1.7 collective-permute-done.18.theirs_ref
  83.1 1.0 plane_add.1
  84.1 3.7 %all-to-all-start.3 = ((bf16[4,240,384]{2,1,0:T(8,128)(2,1)}), bf16[4,240,384]{2,1,0:T(8,128)(2,1)S(1)}, u32[]{:S(2)}, u32[]{:S(2)}) async-start(bf16[4,240,384]{2,1,0:T(8,128)(2,1)} %plane_add.1), calls=%async_computation.3 | async-start | bytes 1474560 | tf_op jit(solution)/shard_map/all_to_all | solution.py:1026
  87.7 7.9 %conv_backward.1 = (bf16[32,72,128]{2,1,0:T(8,128)(2,1)}, f32[960,256]{1,0:T(8,128)}, f32[72,128]{1,0:T(8,128)}) custom-call(bf16[32,24,128]{2,1,0:T(8,128)(2,1)} %copy-done.31, f32[32,72,128]{2,1,0:T(8,128)} %get-tuple-element.133.sm_ref, f32[32,72,128]{2,1,0:T(8,128)} %get-tuple-element.121.p_ref, bf16[32,24,128]{2,1,0:T(8,128)(2,1)} %get-tuple-element.103.y_ref, ...), custom_call_target="tpu_custom_call" | custom-call | flops 350000000 | bytes 450000 | tf_op jit(solution)/shard_map/conv_backward/pallas_call | solution.py:413
  95.7 2.7 %all-to-all-done.3.x_ref = bf16[4,240,384]{2,1,0:T(8,128)(2,1)S(1)} async-done(((bf16[4,240,384]{2,1,0:T(8,128)(2,1)}), bf16[4,240,384]{2,1,0:T(8,128)(2,1)S(1)}, u32[]{:S(2)}, u32[]{:S(2)}) %all-to-all-start.3) | async-done | bytes 737312 | tf_op jit(solution)/shard_map/all_to_all | solution.py:1026
  98.4 3.4 %all-to-all-start.5 = ((bf16[32,72,128]{2,1,0:T(8,128)(2,1)}), bf16[32,72,128]{2,1,0:T(8,128)(2,1)S(1)}, u32[]{:S(2)}, u32[]{:S(2)}) async-start(bf16[32,72,128]{2,1,0:T(8,128)(2,1)} %get-tuple-element.155.pg_ref), calls=%async_computation.5 | async-start | bytes 1179648 | tf_op jit(solution)/shard_map/all_to_all | solution.py:1026
  102.1 3.6 %collective-permute-start.22 = (bf16[240,384]{1,0:T(8,128)(2,1)S(1)}, bf16[240,384]{1,0:T(8,128)(2,1)S(1)}, u32[]{:S(2)}, u32[]{:S(2)}) collective-permute-start(bf16[240,384]{1,0:T(8,128)(2,1)S(1)} %plane_sum.1.a0), channel_id=1, source_target_pairs={{0,24},{2,26},{4,28},{6,30},{8,16},{10,18},{12,20},{14,22},{16,8},... | collective-permute-start | bytes 552968 | tf_op jit(solution)/shard_map/ppermute | solution.py:1022
  105.7 0.9 collective-permute-start.20
  106.5 0.9 copy-done.30
  107.5 10.8 %channel_grads.1 = (bf16[144,256]{1,0:T(8,128)(2,1)}, f32[48,128]{1,0:T(8,128)}) custom-call(bf16[32,72,128]{2,1,0:T(8,128)(2,1)} %get-tuple-element.155.pg_ref, f32[72,128]{1,0:T(8,128)} %get-tuple-element.138.st_ref, f32[960,256]{1,0:T(8,128)} %get-tuple-element.139.own_ref, f32[960,256]{1,0:T(8,128)} %copy-done.30, f32[4,40,128]{2,1,0:T(8,128)} %constant.37.clone.tw, ...), custom_call_target="tpu_custom_call" | custom-call | flops 400000000 | bytes 400000 | tf_op jit(solution)/shard_map/channel_grads/pallas_call | solution.py:560
  118.3 2.6 %collective-permute-start.25 = (bf16[144,256]{1,0:T(8,128)(2,1)}, bf16[144,256]{1,0:T(8,128)(2,1)S(1)}, u32[]{:S(2)}, u32[]{:S(2)}) collective-permute-start(bf16[144,256]{1,0:T(8,128)(2,1)} %get-tuple-element.151.a0), channel_id=1, source_target_pairs={{0,6},{2,4},{4,2},{6,0},{8,14},{10,12},{12,10},{14,8},{16,22},{18,... | collective-permute-start | bytes 221192 | tf_op jit(solution)/shard_map/ppermute | solution.py:1022
  121.0 0.6 collective-permute-start.24
  121.9 12.0 %collective-permute-done.21.a2 = bf16[240,384]{1,0:T(8,128)(2,1)S(1)} collective-permute-done((bf16[240,384]{1,0:T(8,128)(2,1)S(1)}, bf16[240,384]{1,0:T(8,128)(2,1)S(1)}, u32[]{:S(2)}, u32[]{:S(2)}) %collective-permute-start.21) | collective-permute-done | bytes 184352 | tf_op jit(solution)/shard_map/ppermute | solution.py:1022
  133.9 1.5 plane_join.2
  135.4 0.6 copy-done.22
  136.0 0.6 copy-done.24
  136.7 0.8 copy-done.8
  137.5 3.7 %all-to-all-start.4 = ((bf16[4,672,384]{2,1,0:T(8,128)(2,1)}), bf16[4,672,384]{2,1,0:T(8,128)(2,1)S(1)}, u32[]{:S(2)}, u32[]{:S(2)}) async-start(bf16[4,672,384]{2,1,0:T(8,128)(2,1)} %plane_join.2), calls=%async_computation.4 | async-start | bytes 4128768 | tf_op jit(solution)/shard_map/all_to_all | solution.py:1026
  141.1 0.9 copy-done.23
  142.0 0.9 copy-done.25
  142.9 0.7 plane_join.3.refs_0_
  143.6 1.4 collective-permute-start.28
  145.0 3.0 %collective-permute-start.26 = (bf16[360,256]{1,0:T(8,128)(2,1)}, bf16[360,256]{1,0:T(8,128)(2,1)}, u32[]{:S(2)}, u32[]{:S(2)}) collective-permute-start(bf16[360,256]{1,0:T(8,128)(2,1)} %plane_join.3.refs_0_), channel_id=1, source_target_pairs={{0,8},{2,10},{4,12},{6,14},{8,0},{10,2},{12,4},{14,6},{16,24},{18,... | collective-permute-start | bytes 552968 | tf_op jit(solution)/shard_map/ppermute | solution.py:1022
  148.0 0.5 collective-permute-start.29
  148.5 4.9 %collective-permute-done.28.refs_3_ = bf16[360,256]{1,0:T(8,128)(2,1)} collective-permute-done((bf16[360,256]{1,0:T(8,128)(2,1)}, bf16[360,256]{1,0:T(8,128)(2,1)}, u32[]{:S(2)}, u32[]{:S(2)}) %collective-permute-start.28) | collective-permute-done | bytes 184352 | tf_op jit(solution)/shard_map/ppermute | solution.py:1022
  153.4 6.8 %collective-permute-done.27.refs_2_ = bf16[360,256]{1,0:T(8,128)(2,1)} collective-permute-done((bf16[360,256]{1,0:T(8,128)(2,1)}, bf16[360,256]{1,0:T(8,128)(2,1)}, u32[]{:S(2)}, u32[]{:S(2)}) %collective-permute-start.27) | collective-permute-done | bytes 184352 | tf_op jit(solution)/shard_map/ppermute | solution.py:1022
  160.2 0.5 collective-permute-start.30
  160.8 1.1 copy-done.9
  161.8 1.0 copy-done.15
  162.8 0.7 mixer_back.1.half_ref
  163.6 0.8 slice_add_fusion.1
  164.4 0.6 fusion
  165.0 4.4 %in_unpack.1 = (f32[3,192,768]{2,1,0:T(8,128)}, f32[3,3,768]{2,1,0:T(4,128)}, f32[768]{0:T(1024)}, f32[5,128]{1,0:T(8,128)}, f32[128]{0:T(128)}, /*index=5*/f32[128,128]{1,0:T(8,128)}, f32[768]{0:T(1024)}) custom-call(bf16[3,192,768]{2,1,0:T(8,128)(2,1)S(1)} %bitcast.22, f32[768]{0:T(1024)S(1)} %copy-done.27, bf16[360,256]{1,0:T(8,128)(2,1)} %plane_join.3.refs_0_, ...), custom_call_target="tpu_custom_call" | custom-call | flops 5000000 | bytes 200000 | tf_op jit(solution)/shard_map/in_unpack/pallas_call | solution.py:950
  169.4 4.0 %finish.1 = (f32[4,192,2,384]{3,2,1,0:T(2,128)}, f32[384,768]{1,0:T(8,128)}, f32[192,768]{1,0:T(8,128)}, bf16[256,768]{1,0:T(8,128)(2,1)}) custom-call(bf16[4,672,384]{2,1,0:T(8,128)(2,1)S(1)} %all-to-all-done.4.a_ref, bf16[128,768]{1,0:T(8,128)(2,1)S(1)} %mixer_back.1.half_ref, bf16[128,768]{1,0:T(8,128)(2,1)} %collective-permute-done.33.back_ref), custom_call_target="tpu_custom_call" | custom-call | flops 5000000 | bytes 300000 | tf_op jit(solution)/shard_map/finish/pallas_call | solution.py:887
  (111 shorter events, 2.6 us)
Async XLA Ops:
  0.6 14.2 %copy-start.6 = (bf16[256,768]{1,0:T(8,128)(2,1)S(1)}, bf16[256,768]{1,0:T(8,128)(2,1)}, u32[]{:S(2)}) copy-start(bf16[256,768]{1,0:T(8,128)(2,1)} %x_ref.5) | copy-start | bytes 1179652
  0.7 14.2 %copy-start = (bf16[192,3,768]{2,0,1:T(8,128)(2,1)S(1)}, bf16[192,3,768]{2,0,1:T(8,128)(2,1)}, u32[]{:S(2)}) copy-start(bf16[192,3,768]{2,0,1:T(8,128)(2,1)} %param.30) | copy-start | bytes 2654212
  0.7 14.2 %copy-start.27 = (f32[768]{0:T(1024)S(1)}, f32[768]{0:T(1024)}, u32[]{:S(2)}) copy-start(f32[768]{0:T(1024)} %gain_ref.7) | copy-start | bytes 9220
  0.7 14.2 %copy-start.17 = (f32[3,3,768]{2,1,0:T(4,128)S(1)}, f32[3,3,768]{2,1,0:T(4,128)}, u32[]{:S(2)}) copy-start(f32[3,3,768]{2,1,0:T(4,128)} %taps_ref.5) | copy-start | bytes 82948
  0.7 14.2 %copy-start.14 = (bf16[128,768]{1,0:T(8,128)(2,1)S(1)}, bf16[128,768]{1,0:T(8,128)(2,1)}, u32[]{:S(2)}) copy-start(bf16[128,768]{1,0:T(8,128)(2,1)} %og_ref.3) | copy-start | bytes 589828
  1.5 13.3 %collective-permute-start = (bf16[16,768]{1,0:T(8,128)(2,1)S(1)}, bf16[16,768]{1,0:T(8,128)(2,1)S(1)}, u32[]{:S(2)}, u32[]{:S(2)}) collective-permute-start(bf16[16,768]{1,0:T(8,128)(2,1)S(1)} %slice.27), channel_id=1, source_target_pairs={{0,2},{2,4},{4,6},{6,8},{8,10},{10,12},{12,14},{14,16},{16,18},{18... | collective-permute-start | bytes 73736 | tf_op jit(solution)/shard_map/ppermute | solution.py:1013
  14.8 1.9 %copy-start.28 = (bf16[4,192,2,384]{3,2,1,0:T(2,128)(2,1)S(1)}, bf16[4,192,2,384]{3,2,1,0:T(2,128)(2,1)}, u32[]{:S(2)}) copy-start(bf16[4,192,2,384]{3,2,1,0:T(2,128)(2,1)} %param.39) | copy-start | bytes 3538948
  16.7 1.2 copy-start.34
  16.7 10.8 %copy-start.10 = (bf16[384,768]{1,0:T(8,128)(2,1)S(1)}, bf16[384,768]{1,0:T(8,128)(2,1)}, u32[]{:S(2)}) copy-start(bf16[384,768]{1,0:T(8,128)(2,1)} %da_ref.1) | copy-start | bytes 1769476
  17.5 14.3 %copy-start.2 = (bf16[4,192,2,384]{3,1,2,0:T(8,128)(2,1)}, bf16[4,192,2,384]{3,1,2,0:T(8,128)(2,1)S(1)}, u32[]{:S(2)}) copy-start(bf16[4,192,2,384]{3,1,2,0:T(8,128)(2,1)S(1)} %copy.43) | copy-start | bytes 3538948
  17.5 34.3 %collective-permute-start.2 = (bf16[4,2,192,384]{3,2,1,0:T(8,128)(2,1)S(1)}, bf16[4,2,192,384]{3,2,1,0:T(8,128)(2,1)S(1)}, u32[]{:S(2)}, u32[]{:S(2)}) collective-permute-start(bf16[4,2,192,384]{3,2,1,0:T(8,128)(2,1)S(1)} %bitcast.23), channel_id=1, source_target_pairs={{0,1},{1,0},{2,3},{3,2},{4,5},{5,4},{6,7},{7,6},{8,9},{9,8},{10,11... | collective-permute-start | bytes 3538952 | tf_op jit(solution)/shard_map/ppermute | solution.py:1017
  17.9 9.6 %collective-permute-start.1 = (f32[24,4096]{1,0:T(8,128)S(1)}, f32[24,4096]{1,0:T(8,128)}, u32[]{:S(2)}, u32[]{:S(2)}) collective-permute-start(f32[24,4096]{1,0:T(8,128)S(1)} %copy-done.34), channel_id=1, source_target_pairs={{0,1},{1,0},{2,3},{3,2},{4,5},{5,4},{6,7},{7,6},{8,9},{9,8},{10,11... | collective-permute-start | bytes 1179656 | tf_op jit(solution)/shard_map/ppermute | solution.py:1017
  18.0 14.4 %all-to-all-start = ((bf16[32,24,128]{2,1,0:T(8,128)(2,1)}), bf16[32,24,128]{2,1,0:T(8,128)(2,1)}, u32[]{:S(2)}, u32[]{:S(2)}) async-start(bf16[32,24,128]{2,1,0:T(8,128)(2,1)} %bitcast.2), calls=%async_computation | async-start | bytes 393216 | tf_op jit(solution)/shard_map/all_to_all | solution.py:1026
  23.1 19.9 %collective-permute-start.4 = (bf16[384,128]{1,0:T(8,128)(2,1)}, bf16[384,128]{1,0:T(8,128)(2,1)}, u32[]{:S(2)}, u32[]{:S(2)}) collective-permute-start(bf16[384,128]{1,0:T(8,128)(2,1)} %get-tuple-element.110), channel_id=1, source_target_pairs={{0,8},{2,10},{4,12},{6,14},{8,0},{10,2},{12,4},{14,6},{16,24},{18,... | collective-permute-start | bytes 294920 | tf_op jit(solution)/shard_map/ppermute | solution.py:1022
  24.9 19.0 %collective-permute-start.5 = (bf16[384,128]{1,0:T(8,128)(2,1)}, bf16[384,128]{1,0:T(8,128)(2,1)}, u32[]{:S(2)}, u32[]{:S(2)}) collective-permute-start(bf16[384,128]{1,0:T(8,128)(2,1)} %get-tuple-element.112), channel_id=1, source_target_pairs={{0,16},{2,18},{4,20},{6,22},{8,24},{10,26},{12,28},{14,30},{16,0},... | collective-permute-start | bytes 294920 | tf_op jit(solution)/shard_map/ppermute | solution.py:1022
  27.3 16.6 %collective-permute-start.6 = (bf16[384,128]{1,0:T(8,128)(2,1)}, bf16[384,128]{1,0:T(8,128)(2,1)}, u32[]{:S(2)}, u32[]{:S(2)}) collective-permute-start(bf16[384,128]{1,0:T(8,128)(2,1)} %get-tuple-element.114), channel_id=1, source_target_pairs={{0,24},{2,26},{4,28},{6,30},{8,16},{10,18},{12,20},{14,22},{16,8},... | collective-permute-start | bytes 294920 | tf_op jit(solution)/shard_map/ppermute | solution.py:1022
  27.6 21.3 %collective-permute-start.3 = (bf16[384,768]{1,0:T(8,128)(2,1)S(1)}, bf16[384,768]{1,0:T(8,128)(2,1)S(1)}, u32[]{:S(2)}, u32[]{:S(2)}) collective-permute-start(bf16[384,768]{1,0:T(8,128)(2,1)S(1)} %copy-done.10), channel_id=1, source_target_pairs={{0,1},{1,0},{2,3},{3,2},{4,5},{5,4},{6,7},{7,6},{8,9},{9,8},{10,11... | collective-permute-start | bytes 1769480 | tf_op jit(solution)/shard_map/ppermute | solution.py:1017
  37.4 14.4 %all-to-all-start.1 = ((bf16[32,24,128]{2,1,0:T(8,128)(2,1)}), bf16[32,24,128]{2,1,0:T(8,128)(2,1)}, u32[]{:S(2)}, u32[]{:S(2)}) async-start(bf16[32,24,128]{2,1,0:T(8,128)(2,1)} %get-tuple-element.103.y_ref), calls=%async_computation.1 | async-start | bytes 393216 | tf_op jit(solution)/shard_map/all_to_all | solution.py:1026
  45.4 18.2 %collective-permute-start.9 = (bf16[4,192,128]{2,1,0:T(8,128)(2,1)}, bf16[4,192,128]{2,1,0:T(8,128)(2,1)}, u32[]{:S(2)}, u32[]{:S(2)}) collective-permute-start(bf16[4,192,128]{2,1,0:T(8,128)(2,1)} %pad_maximum_fusion.refs_0_), channel_id=1, source_target_pairs={{0,6},{2,4},{4,2},{6,0},{8,14},{10,12},{12,10},{14,8},{16,22},{18,... | collective-permute-start | bytes 589832 | tf_op jit(solution)/shard_map/ppermute | solution.py:1022
  47.8 16.1 %collective-permute-start.8 = (bf16[4,192,128]{2,1,0:T(8,128)(2,1)}, bf16[4,192,128]{2,1,0:T(8,128)(2,1)}, u32[]{:S(2)}, u32[]{:S(2)}) collective-permute-start(bf16[4,192,128]{2,1,0:T(8,128)(2,1)} %pad_maximum_fusion.refs_0_), channel_id=1, source_target_pairs={{0,4},{2,6},{4,0},{6,2},{8,12},{10,14},{12,8},{14,10},{16,20},{18,... | collective-permute-start | bytes 589832 | tf_op jit(solution)/shard_map/ppermute | solution.py:1022
  48.4 15.8 %collective-permute-start.7 = (bf16[4,192,128]{2,1,0:T(8,128)(2,1)}, bf16[4,192,128]{2,1,0:T(8,128)(2,1)}, u32[]{:S(2)}, u32[]{:S(2)}) collective-permute-start(bf16[4,192,128]{2,1,0:T(8,128)(2,1)} %pad_maximum_fusion.refs_0_), channel_id=1, source_target_pairs={{0,2},{2,0},{4,6},{6,4},{8,10},{10,8},{12,14},{14,12},{16,18},{18,... | collective-permute-start | bytes 589832 | tf_op jit(solution)/shard_map/ppermute | solution.py:1022
  48.9 2.9 %copy-start.12 = (bf16[384,768]{1,0:T(8,128)(2,1)}, bf16[384,768]{1,0:T(8,128)(2,1)S(1)}, u32[]{:S(2)}) copy-start(bf16[384,768]{1,0:T(8,128)(2,1)S(1)} %collective-permute-done.3.db_ref) | copy-start | bytes 1769476
  52.8 23.0 %copy-start.11 = (bf16[384,768]{1,0:T(8,128)(2,1)S(1)}, bf16[384,768]{1,0:T(8,128)(2,1)}, u32[]{:S(2)}) copy-start(bf16[384,768]{1,0:T(8,128)(2,1)} %da_ref.1) | copy-start | bytes 1769476
  60.7 15.1 %copy-start.26 = (bf16[192,128]{1,0:T(8,128)(2,1)S(1)}, bf16[192,128]{1,0:T(8,128)(2,1)}, u32[]{:S(2)}) copy-start(bf16[192,128]{1,0:T(8,128)(2,1)} %get-tuple-element.122.za) | copy-start | bytes 147460
  60.7 13.8 %all-to-all-start.2 = ((bf16[32,24,128]{2,1,0:T(8,128)(2,1)}), bf16[32,24,128]{2,1,0:T(8,128)(2,1)S(1)}, u32[]{:S(2)}, u32[]{:S(2)}) async-start(bf16[32,24,128]{2,1,0:T(8,128)(2,1)} %bitcast.26), calls=%async_computation.2 | async-start | bytes 393216 | tf_op jit(solution)/shard_map/all_to_all | solution.py:1026
  63.6 4.7 %collective-permute-start.13 = (bf16[4,192,128]{2,1,0:T(8,128)(2,1)}, bf16[4,192,128]{2,1,0:T(8,128)(2,1)S(1)}, u32[]{:S(2)}, u32[]{:S(2)}) collective-permute-start(bf16[4,192,128]{2,1,0:T(8,128)(2,1)} %collective-permute-done.9.refs_3_), channel_id=1, source_target_pairs={{0,1},{1,0},{2,3},{3,2},{4,5},{5,4},{6,7},{7,6},{8,9},{9,8},{10,11... | collective-permute-start | bytes 589832 | tf_op jit(solution)/shard_map/ppermute | solution.py:1017
  63.9 4.4 %collective-permute-start.12 = (bf16[4,192,128]{2,1,0:T(8,128)(2,1)}, bf16[4,192,128]{2,1,0:T(8,128)(2,1)S(1)}, u32[]{:S(2)}, u32[]{:S(2)}) collective-permute-start(bf16[4,192,128]{2,1,0:T(8,128)(2,1)} %collective-permute-done.8.refs_2_), channel_id=1, source_target_pairs={{0,1},{1,0},{2,3},{3,2},{4,5},{5,4},{6,7},{7,6},{8,9},{9,8},{10,11... | collective-permute-start | bytes 589832 | tf_op jit(solution)/shard_map/ppermute | solution.py:1017
  64.2 5.4 %collective-permute-start.11 = (bf16[4,192,128]{2,1,0:T(8,128)(2,1)}, bf16[4,192,128]{2,1,0:T(8,128)(2,1)}, u32[]{:S(2)}, u32[]{:S(2)}) collective-permute-start(bf16[4,192,128]{2,1,0:T(8,128)(2,1)} %collective-permute-done.7.refs_1_), channel_id=1, source_target_pairs={{0,1},{1,0},{2,3},{3,2},{4,5},{5,4},{6,7},{7,6},{8,9},{9,8},{10,11... | collective-permute-start | bytes 589832 | tf_op jit(solution)/shard_map/ppermute | solution.py:1017
  64.4 5.2 %collective-permute-start.10 = (bf16[4,192,128]{2,1,0:T(8,128)(2,1)}, bf16[4,192,128]{2,1,0:T(8,128)(2,1)}, u32[]{:S(2)}, u32[]{:S(2)}) collective-permute-start(bf16[4,192,128]{2,1,0:T(8,128)(2,1)} %pad_maximum_fusion.refs_0_), channel_id=1, source_target_pairs={{0,1},{1,0},{2,3},{3,2},{4,5},{5,4},{6,7},{7,6},{8,9},{9,8},{10,11... | collective-permute-start | bytes 589832 | tf_op jit(solution)/shard_map/ppermute | solution.py:1017
  64.7 9.8 %collective-permute-start.16 = (bf16[192,128]{1,0:T(8,128)(2,1)}, bf16[192,128]{1,0:T(8,128)(2,1)S(1)}, u32[]{:S(2)}, u32[]{:S(2)}) collective-permute-start(bf16[192,128]{1,0:T(8,128)(2,1)} %get-tuple-element.127), channel_id=1, source_target_pairs={{0,24},{2,26},{4,28},{6,30},{8,16},{10,18},{12,20},{14,22},{16,8},... | collective-permute-start | bytes 147464 | tf_op jit(solution)/shard_map/ppermute | solution.py:1022
  68.3 1.3 copy-start.32
  68.3 7.5 %collective-permute-start.15 = (bf16[192,128]{1,0:T(8,128)(2,1)}, bf16[192,128]{1,0:T(8,128)(2,1)S(1)}, u32[]{:S(2)}, u32[]{:S(2)}) collective-permute-start(bf16[192,128]{1,0:T(8,128)(2,1)} %get-tuple-element.125), channel_id=1, source_target_pairs={{0,16},{2,18},{4,20},{6,22},{8,24},{10,26},{12,28},{14,30},{16,0},... | collective-permute-start | bytes 147464 | tf_op jit(solution)/shard_map/ppermute | solution.py:1022
  68.3 1.3 copy-start.33
  68.3 7.4 %copy-start.3 = (bf16[4,192,2,384]{3,1,2,0:T(8,128)(2,1)S(1)}, bf16[4,192,2,384]{3,1,2,0:T(8,128)(2,1)}, u32[]{:S(2)}) copy-start(bf16[4,192,2,384]{3,1,2,0:T(8,128)(2,1)} %copy-done.2) | copy-start | bytes 3538948
  68.3 7.4 %copy-start.5 = (bf16[4,2,192,384]{3,2,1,0:T(8,128)(2,1)S(1)}, bf16[4,2,192,384]{3,2,1,0:T(8,128)(2,1)}, u32[]{:S(2)}) copy-start(bf16[4,2,192,384]{3,2,1,0:T(8,128)(2,1)} %copy-done.4) | copy-start | bytes 3538948
  68.3 7.4 %copy-start.20 = (bf16[384,128]{1,0:T(8,128)(2,1)S(1)}, bf16[384,128]{1,0:T(8,128)(2,1)}, u32[]{:S(2)}) copy-start(bf16[384,128]{1,0:T(8,128)(2,1)} %copy-done.19) | copy-start | bytes 294916
  68.4 7.4 %collective-permute-start.14 = (bf16[192,128]{1,0:T(8,128)(2,1)}, bf16[192,128]{1,0:T(8,128)(2,1)S(1)}, u32[]{:S(2)}, u32[]{:S(2)}) collective-permute-start(bf16[192,128]{1,0:T(8,128)(2,1)} %get-tuple-element.123), channel_id=1, source_target_pairs={{0,8},{2,10},{4,12},{6,14},{8,0},{10,2},{12,4},{14,6},{16,24},{18,... | collective-permute-start | bytes 147464 | tf_op jit(solution)/shard_map/ppermute | solution.py:1022
  74.5 6.3 %copy-start.31 = (bf16[32,24,128]{2,1,0:T(8,128)(2,1)}, bf16[32,24,128]{2,1,0:T(8,128)(2,1)S(1)}, u32[]{:S(2)}) copy-start(bf16[32,24,128]{2,1,0:T(8,128)(2,1)S(1)} %all-to-all-done.2.g_ref) | copy-start | bytes 589828
  76.9 4.0 %copy-start.18 = (bf16[384,384]{1,0:T(8,128)(2,1)S(1)}, bf16[384,384]{1,0:T(8,128)(2,1)}, u32[]{:S(2)}) copy-start(bf16[384,384]{1,0:T(8,128)(2,1)} %get-tuple-element.131.mine_ref) | copy-start | bytes 884740
  80.8 2.3 %collective-permute-start.17 = (bf16[576,384]{1,0:T(8,128)(2,1)S(1)}, bf16[576,384]{1,0:T(8,128)(2,1)S(1)}, u32[]{:S(2)}, u32[]{:S(2)}) collective-permute-start(bf16[576,384]{1,0:T(8,128)(2,1)S(1)} %get-tuple-element.130), channel_id=1, source_target_pairs={{0,1},{1,0},{2,3},{3,2},{4,5},{5,4},{6,7},{7,6},{8,9},{9,8},{10,11... | collective-permute-start | bytes 1327112 | tf_op jit(solution)/shard_map/ppermute | solution.py:1017
  80.9 2.2 %collective-permute-start.18 = (bf16[384,384]{1,0:T(8,128)(2,1)S(1)}, bf16[384,384]{1,0:T(8,128)(2,1)S(1)}, u32[]{:S(2)}, u32[]{:S(2)}) collective-permute-start(bf16[384,384]{1,0:T(8,128)(2,1)S(1)} %copy-done.18), channel_id=1, source_target_pairs={{0,1},{1,0},{2,3},{3,2},{4,5},{5,4},{6,7},{7,6},{8,9},{9,8},{10,11... | collective-permute-start | bytes 884744 | tf_op jit(solution)/shard_map/ppermute | solution.py:1017
  84.1 14.3 %all-to-all-start.3 = ((bf16[4,240,384]{2,1,0:T(8,128)(2,1)}), bf16[4,240,384]{2,1,0:T(8,128)(2,1)S(1)}, u32[]{:S(2)}, u32[]{:S(2)}) async-start(bf16[4,240,384]{2,1,0:T(8,128)(2,1)} %plane_add.1), calls=%async_computation.3 | async-start | bytes 1474560 | tf_op jit(solution)/shard_map/all_to_all | solution.py:1026
  95.7 6.2 %copy-start.29 = (f32[960,256]{1,0:T(8,128)S(1)}, f32[960,256]{1,0:T(8,128)}, u32[]{:S(2)}) copy-start(f32[960,256]{1,0:T(8,128)} %get-tuple-element.139.own_ref) | copy-start | bytes 2949124
  98.4 38.2 %all-to-all-start.5 = ((bf16[32,72,128]{2,1,0:T(8,128)(2,1)}), bf16[32,72,128]{2,1,0:T(8,128)(2,1)S(1)}, u32[]{:S(2)}, u32[]{:S(2)}) async-start(bf16[32,72,128]{2,1,0:T(8,128)(2,1)} %get-tuple-element.155.pg_ref), calls=%async_computation.5 | async-start | bytes 1179648 | tf_op jit(solution)/shard_map/all_to_all | solution.py:1026
  101.9 4.7 %collective-permute-start.19 = (f32[960,256]{1,0:T(8,128)S(1)}, f32[960,256]{1,0:T(8,128)S(1)}, u32[]{:S(2)}, u32[]{:S(2)}) collective-permute-start(f32[960,256]{1,0:T(8,128)S(1)} %copy-done.29), channel_id=1, source_target_pairs={{0,1},{1,0},{2,3},{3,2},{4,5},{5,4},{6,7},{7,6},{8,9},{9,8},{10,11... | collective-permute-start | bytes 2949128 | tf_op jit(solution)/shard_map/ppermute | solution.py:1017
  102.1 19.5 %collective-permute-start.22 = (bf16[240,384]{1,0:T(8,128)(2,1)S(1)}, bf16[240,384]{1,0:T(8,128)(2,1)S(1)}, u32[]{:S(2)}, u32[]{:S(2)}) collective-permute-start(bf16[240,384]{1,0:T(8,128)(2,1)S(1)} %plane_sum.1.a0), channel_id=1, source_target_pairs={{0,24},{2,26},{4,28},{6,30},{8,16},{10,18},{12,20},{14,22},{16,8},... | collective-permute-start | bytes 552968 | tf_op jit(solution)/shard_map/ppermute | solution.py:1022
  105.7 28.2 %collective-permute-start.21 = (bf16[240,384]{1,0:T(8,128)(2,1)S(1)}, bf16[240,384]{1,0:T(8,128)(2,1)S(1)}, u32[]{:S(2)}, u32[]{:S(2)}) collective-permute-start(bf16[240,384]{1,0:T(8,128)(2,1)S(1)} %plane_sum.1.a0), channel_id=1, source_target_pairs={{0,16},{2,18},{4,20},{6,22},{8,24},{10,26},{12,28},{14,30},{16,0},... | collective-permute-start | bytes 552968 | tf_op jit(solution)/shard_map/ppermute | solution.py:1022
  105.7 28.2 %collective-permute-start.20 = (bf16[240,384]{1,0:T(8,128)(2,1)S(1)}, bf16[240,384]{1,0:T(8,128)(2,1)S(1)}, u32[]{:S(2)}, u32[]{:S(2)}) collective-permute-start(bf16[240,384]{1,0:T(8,128)(2,1)S(1)} %plane_sum.1.a0), channel_id=1, source_target_pairs={{0,8},{2,10},{4,12},{6,14},{8,0},{10,2},{12,4},{14,6},{16,24},{18,... | collective-permute-start | bytes 552968 | tf_op jit(solution)/shard_map/ppermute | solution.py:1022
  118.3 17.0 %collective-permute-start.25 = (bf16[144,256]{1,0:T(8,128)(2,1)}, bf16[144,256]{1,0:T(8,128)(2,1)S(1)}, u32[]{:S(2)}, u32[]{:S(2)}) collective-permute-start(bf16[144,256]{1,0:T(8,128)(2,1)} %get-tuple-element.151.a0), channel_id=1, source_target_pairs={{0,6},{2,4},{4,2},{6,0},{8,14},{10,12},{12,10},{14,8},{16,22},{18,... | collective-permute-start | bytes 221192 | tf_op jit(solution)/shard_map/ppermute | solution.py:1022
  121.0 14.4 %collective-permute-start.24 = (bf16[144,256]{1,0:T(8,128)(2,1)}, bf16[144,256]{1,0:T(8,128)(2,1)S(1)}, u32[]{:S(2)}, u32[]{:S(2)}) collective-permute-start(bf16[144,256]{1,0:T(8,128)(2,1)} %get-tuple-element.151.a0), channel_id=1, source_target_pairs={{0,4},{2,6},{4,0},{6,2},{8,12},{10,14},{12,8},{14,10},{16,20},{18,... | collective-permute-start | bytes 221192 | tf_op jit(solution)/shard_map/ppermute | solution.py:1022
  121.5 14.5 %collective-permute-start.23 = (bf16[144,256]{1,0:T(8,128)(2,1)}, bf16[144,256]{1,0:T(8,128)(2,1)S(1)}, u32[]{:S(2)}, u32[]{:S(2)}) collective-permute-start(bf16[144,256]{1,0:T(8,128)(2,1)} %get-tuple-element.151.a0), channel_id=1, source_target_pairs={{0,2},{2,0},{4,6},{6,4},{8,10},{10,8},{12,14},{14,12},{16,18},{18,... | collective-permute-start | bytes 221192 | tf_op jit(solution)/shard_map/ppermute | solution.py:1022
  135.4 5.8 %copy-start.21 = (bf16[144,256]{1,0:T(8,128)(2,1)S(1)}, bf16[144,256]{1,0:T(8,128)(2,1)}, u32[]{:S(2)}) copy-start(bf16[144,256]{1,0:T(8,128)(2,1)} %get-tuple-element.151.a0) | copy-start | bytes 221188
  135.4 25.4 %copy-start.1 = (bf16[192,3,768]{2,0,1:T(8,128)(2,1)S(1)}, bf16[192,3,768]{2,0,1:T(8,128)(2,1)}, u32[]{:S(2)}) copy-start(bf16[192,3,768]{2,0,1:T(8,128)(2,1)} %param.30) | copy-start | bytes 2654212
  135.4 25.4 %copy-start.7 = (bf16[256,768]{1,0:T(8,128)(2,1)S(1)}, bf16[256,768]{1,0:T(8,128)(2,1)}, u32[]{:S(2)}) copy-start(bf16[256,768]{1,0:T(8,128)(2,1)} %x_ref.5) | copy-start | bytes 1179652
  137.5 32.0 %all-to-all-start.4 = ((bf16[4,672,384]{2,1,0:T(8,128)(2,1)}), bf16[4,672,384]{2,1,0:T(8,128)(2,1)S(1)}, u32[]{:S(2)}, u32[]{:S(2)}) async-start(bf16[4,672,384]{2,1,0:T(8,128)(2,1)} %plane_join.2), calls=%async_computation.4 | async-start | bytes 4128768 | tf_op jit(solution)/shard_map/all_to_all | solution.py:1026
  143.6 9.8 %collective-permute-start.28 = (bf16[360,256]{1,0:T(8,128)(2,1)}, bf16[360,256]{1,0:T(8,128)(2,1)}, u32[]{:S(2)}, u32[]{:S(2)}) collective-permute-start(bf16[360,256]{1,0:T(8,128)(2,1)} %plane_join.3.refs_0_), channel_id=1, source_target_pairs={{0,24},{2,26},{4,28},{6,30},{8,16},{10,18},{12,20},{14,22},{16,8},... | collective-permute-start | bytes 552968 | tf_op jit(solution)/shard_map/ppermute | solution.py:1022
  145.0 15.2 %collective-permute-start.27 = (bf16[360,256]{1,0:T(8,128)(2,1)}, bf16[360,256]{1,0:T(8,128)(2,1)}, u32[]{:S(2)}, u32[]{:S(2)}) collective-permute-start(bf16[360,256]{1,0:T(8,128)(2,1)} %plane_join.3.refs_0_), channel_id=1, source_target_pairs={{0,16},{2,18},{4,20},{6,22},{8,24},{10,26},{12,28},{14,30},{16,0},... | collective-permute-start | bytes 552968 | tf_op jit(solution)/shard_map/ppermute | solution.py:1022
  145.0 15.2 %collective-permute-start.26 = (bf16[360,256]{1,0:T(8,128)(2,1)}, bf16[360,256]{1,0:T(8,128)(2,1)}, u32[]{:S(2)}, u32[]{:S(2)}) collective-permute-start(bf16[360,256]{1,0:T(8,128)(2,1)} %plane_join.3.refs_0_), channel_id=1, source_target_pairs={{0,8},{2,10},{4,12},{6,14},{8,0},{10,2},{12,4},{14,6},{16,24},{18,... | collective-permute-start | bytes 552968 | tf_op jit(solution)/shard_map/ppermute | solution.py:1022
  148.0 15.5 %collective-permute-start.34 = (f32[48,128]{1,0:T(8,128)}, f32[48,128]{1,0:T(8,128)}, u32[]{:S(2)}, u32[]{:S(2)}) collective-permute-start(f32[48,128]{1,0:T(8,128)} %get-tuple-element.175), channel_id=1, source_target_pairs={{0,1},{1,0},{2,3},{3,2},{4,5},{5,4},{6,7},{7,6},{8,9},{9,8},{10,11... | collective-permute-start | bytes 73736 | tf_op jit(solution)/shard_map/ppermute | solution.py:1017
  148.0 17.0 %collective-permute-start.29 = (bf16[360,256]{1,0:T(8,128)(2,1)}, bf16[360,256]{1,0:T(8,128)(2,1)S(1)}, u32[]{:S(2)}, u32[]{:S(2)}) collective-permute-start(bf16[360,256]{1,0:T(8,128)(2,1)} %plane_join.3.refs_0_), channel_id=1, source_target_pairs={{0,1},{1,0},{2,3},{3,2},{4,5},{5,4},{6,7},{7,6},{8,9},{9,8},{10,11... | collective-permute-start | bytes 552968 | tf_op jit(solution)/shard_map/ppermute | solution.py:1017
  153.4 11.6 %collective-permute-start.32 = (bf16[360,256]{1,0:T(8,128)(2,1)}, bf16[360,256]{1,0:T(8,128)(2,1)S(1)}, u32[]{:S(2)}, u32[]{:S(2)}) collective-permute-start(bf16[360,256]{1,0:T(8,128)(2,1)} %collective-permute-done.28.refs_3_), channel_id=1, source_target_pairs={{0,1},{1,0},{2,3},{3,2},{4,5},{5,4},{6,7},{7,6},{8,9},{9,8},{10,11... | collective-permute-start | bytes 552968 | tf_op jit(solution)/shard_map/ppermute | solution.py:1017
  160.2 4.8 %collective-permute-start.31 = (bf16[360,256]{1,0:T(8,128)(2,1)}, bf16[360,256]{1,0:T(8,128)(2,1)S(1)}, u32[]{:S(2)}, u32[]{:S(2)}) collective-permute-start(bf16[360,256]{1,0:T(8,128)(2,1)} %collective-permute-done.27.refs_2_), channel_id=1, source_target_pairs={{0,1},{1,0},{2,3},{3,2},{4,5},{5,4},{6,7},{7,6},{8,9},{9,8},{10,11... | collective-permute-start | bytes 552968 | tf_op jit(solution)/shard_map/ppermute | solution.py:1017
  160.2 4.8 %collective-permute-start.30 = (bf16[360,256]{1,0:T(8,128)(2,1)}, bf16[360,256]{1,0:T(8,128)(2,1)S(1)}, u32[]{:S(2)}, u32[]{:S(2)}) collective-permute-start(bf16[360,256]{1,0:T(8,128)(2,1)} %collective-permute-done.26.refs_1_), channel_id=1, source_target_pairs={{0,1},{1,0},{2,3},{3,2},{4,5},{5,4},{6,7},{7,6},{8,9},{9,8},{10,11... | collective-permute-start | bytes 552968 | tf_op jit(solution)/shard_map/ppermute | solution.py:1017
  163.6 5.9 %collective-permute-start.33 = (bf16[128,768]{1,0:T(8,128)(2,1)S(1)}, bf16[128,768]{1,0:T(8,128)(2,1)}, u32[]{:S(2)}, u32[]{:S(2)}) collective-permute-start(bf16[128,768]{1,0:T(8,128)(2,1)S(1)} %mixer_back.1.half_ref), channel_id=1, source_target_pairs={{0,1},{1,0},{2,3},{3,2},{4,5},{5,4},{6,7},{7,6},{8,9},{9,8},{10,11... | collective-permute-start | bytes 589832 | tf_op jit(solution)/shard_map/ppermute | solution.py:1017
  (12 other events, 10.5 us)

commit v2 on v1

--- a/solution.py
+++ b/solution.py
@@ -678,7 +678,7 @@
 
 
 def middle_kernel(per_plane, conv_ref, sm2_ref, x_ref, og_ref, gain_ref, wo_ref, ga_ref, gb_ref, da_ref, db_ref,
-                  gg_ref, mid_ref, out_ref, wo_out, gain_out, z0, z1, z2, z3, keep_ref):
+                  gg_ref, mid_ref, out_ref, wo_own, wo_other, gain_out, z0, z1, z2, z3, keep_ref):
     width = wo_ref.shape[0]
     blocks = wo_ref.shape[1] // width
     conv = conv_ref[...].astype(F32).T
@@ -715,9 +715,11 @@
     gain_out[...] = jnp.sum(n2_grad * xhat, axis=0, keepdims=True).reshape(-1)
     weight = jnp.concatenate(
         [mm_tn(gated_low[:, column(j, width)], bg[:, column(j, width)]) for j in range(blocks)], axis=1
-    ).astype(BF)
-    lanes = wo_out.shape[1]
-    wo_out[...] = jnp.concatenate([weight[:, :lanes], weight[:, lanes:]], axis=0)
+    )
+    lanes = wo_own.shape[1]
+    first = lax.axis_index("tp") == 0
+    wo_own[...] = jnp.where(first, weight[:, :lanes], weight[:, lanes:]).astype(BF)
+    wo_other[...] = jnp.where(first, weight[:, lanes:], weight[:, :lanes]).astype(BF)
     turned = normed.T.astype(BF)
     for j in range(blocks):
         keep_ref[j] = turned[column(j, width)]
@@ -732,12 +734,13 @@
     return pl.pallas_call(
         functools.partial(middle_kernel, per_plane),
         in_specs=vmem_specs(10),
-        out_specs=vmem_specs(9),
+        out_specs=vmem_specs(10),
         out_shape=[
             jax.ShapeDtypeStruct((model, rows), BF),
             jax.ShapeDtypeStruct((rows, model), F32),
             jax.ShapeDtypeStruct((rows, model), BF),
-            jax.ShapeDtypeStruct((2 * width, model // 2), BF),
+            jax.ShapeDtypeStruct((width, model // 2), BF),
+            jax.ShapeDtypeStruct((width, model // 2), BF),
             jax.ShapeDtypeStruct((model,), F32),
         ]
         + [jax.ShapeDtypeStruct((width, rows), BF)] * 4,
@@ -856,14 +859,13 @@
 
 
 def finish_kernel(per_plane, width, a_ref, half_ref, back_ref,
-                  gi_ref, go_ref, wo_ref, in_ref, keep_ref, last_ref):
+                  gi_ref, go_ref, in_ref, keep_ref):
     seq = lax.axis_index("seq")
     plane = lax.div(seq, per_plane)
     blocks, pieces, cut, half = keep_ref.shape
     for k in range(pieces):
         for z in range(blocks):
             keep_ref[lax.bitwise_xor(plane, z), k] = a_ref[k, z * cut : (z + 1) * cut, :].astype(F32)
-        last_ref[k] = a_ref[k, blocks * cut :, :].astype(F32)
     outs = []
     for j in range(blocks):
         block = jnp.concatenate([keep_ref[j, k] for k in range(pieces)], axis=0)
@@ -871,10 +873,6 @@
         gi_ref[j, :, 1, :] = block[width : 2 * width]
         outs.append(block[2 * width : 3 * width].T)
     go_ref[...] = jnp.concatenate(outs, axis=1)
-    wo_ref[: width // 2, :half] = last_ref[0]
-    wo_ref[width // 2 :, :half] = last_ref[1]
-    wo_ref[: width // 2, half:] = last_ref[2]
-    wo_ref[width // 2 :, half:] = last_ref[3]
     count = half_ref.shape[0]
     me = lax.axis_index("tp")
     in_ref[pl.ds(pl.multiple_of(me * count, count), count), :] = half_ref[...]
@@ -887,18 +885,40 @@
     return pl.pallas_call(
         functools.partial(finish_kernel, per_plane, width),
         in_specs=vmem_specs(3),
-        out_specs=vmem_specs(4),
+        out_specs=vmem_specs(3),
         out_shape=[
             jax.ShapeDtypeStruct((4, width, 2, half), F32),
             jax.ShapeDtypeStruct((half, model), F32),
-            jax.ShapeDtypeStruct((width, model), F32),
             jax.ShapeDtypeStruct((2 * half_rows.shape[0], model), BF),
         ],
-        scratch_shapes=[pltpu.VMEM((4, 4, 3 * width // 4, half), F32), pltpu.VMEM((4, width // 2, half), F32)],
+        scratch_shapes=[pltpu.VMEM((4, 4, 3 * width // 4, half), F32)],
         compiler_params=params(32),
         cost_estimate=cost(10**8, 6 * 10**6),
         name="finish",
     )(sums, half_rows, other_rows)
+
+
+def out_unpack_kernel(mine_ref, theirs_ref, wo_ref):
+    first = lax.axis_index("tp") == 0
+    mine, theirs = mine_ref[...].astype(F32), theirs_ref[...].astype(F32)
+    left, right = jnp.where(first, mine, theirs), jnp.where(first, theirs, mine)
+    _, cut, lanes = left.shape
+    for k in range(left.shape[0]):
+        wo_ref[k * cut : (k + 1) * cut, :lanes] = left[k]
+        wo_ref[k * cut : (k + 1) * cut, lanes:] = right[k]
+
+
+def out_unpack(mine, theirs):
+    count, rows, lanes = mine.shape
+    return pl.pallas_call(
+        out_unpack_kernel,
+        in_specs=vmem_specs(2),
+        out_specs=vmem_specs(1)[0],
+        out_shape=jax.ShapeDtypeStruct((count * rows, 2 * lanes), F32),
+        compiler_params=params(8),
+        cost_estimate=cost(10**8, 10**6),
+        name="out_unpack",
+    )(mine, theirs)
 
 
 def in_unpack_kernel(place, w_ref, gain_ref, *refs):
@@ -1108,14 +1128,14 @@
     else:
         plane_tiles = [gathered_over(rows_in, per_plane, within).reshape(per_plane * blocks, width, rows)]
         turns = [[(0, r) for r in range(per_plane)]]
-    gated_grad, mid, layer_output, extra, gain_sum, *sent = middle_part(
+    gated_grad, mid, layer_output, extra, extra_other, gain_sum, *sent = middle_part(
         conv_tokens, sm2, layer_input, out_grad, glu_gain, out_proj, glu_own, glu_other,
         down_own, down_other, per_plane
     )
     gated_channels = to_channels(gated_grad)
     across = lambda parts: [parts[0]] + [crossed(parts[d], d * per_plane) for d in range(1, blocks)]
     late = across(sent)
-    extra_back = swapped(extra)
+    extra_back = swapped(extra_other)
     plane_tiles = [after(x, gated_grad) for x in plane_tiles]
     tiles = plane_tiles + [swapped(x) for x in plane_tiles]
     turns = turns + [[(1, r) for _, r in t] for t in turns]
@@ -1151,21 +1171,25 @@
     if quick:
         in_parts = [in_piece] + [crossed(in_piece, d) for d in range(1, per_plane)]
         glu_parts = plane_join([after(x, in_piece) for x in glu_parts], 3 * width // per_plane, (per_plane,))
-        glu_full = exchanged(after(glu_parts, *in_parts), "seq", within)
-        in_parts = plane_join([after(x, glu_parts) for x in in_parts], 3 * chans_padded)
-        in_full = across([in_parts] * blocks)
-        pg_tokens = after(pg_tokens, in_parts)
+        pg_tokens = after(pg_tokens, glu_parts)
     input_half = mixer_back(pg_tokens, mid, layer_input, mixer_gain, w_in, chans == chans_padded)
     input_other = swapped(input_half)
 
     if quick:
+        in_parts = plane_join([after(x, input_half) for x in in_parts], 3 * chans_padded)
+        in_full = across([in_parts] * blocks)
+        glu_full = exchanged(after(glu_parts, in_parts), "seq", within)
         in_full = in_full + [swapped(x) for x in in_full]
         in_proj_grad, short_taps_grad, mixer_gain_grad, w1_grad, b1_grad, w2_grad, glu_gain_grad = in_unpack(
-            [after(x, input_half) for x in in_full], place, w_in, mixer_gain
+            in_full, place, w_in, mixer_gain
         )
-        glu_in_grad, glu_out_grad, out_proj_grad, input_grad = finish(
-            after(glu_full, glu_gain_grad), input_half, input_other, per_plane, width
+        glu_full = after(glu_full, glu_gain_grad)
+        out_mine = glu_full[:, 3 * width :, :]
+        out_theirs = swapped(out_mine)
+        glu_in_grad, glu_out_grad, input_grad = finish(
+            after(glu_full, out_mine), input_half, input_other, per_plane, width
         )
+        out_proj_grad = out_unpack(out_mine, after(out_theirs, glu_out_grad))
         in_proj_grad = in_proj_grad.transpose(1, 0, 2)
     else:
         total = (g_own + g_back.astype(F32)).astype(BF)
@@ -1175,10 +1199,13 @@
         glu_in_grad = full[:, : 2 * width].reshape(blocks, 2, width, half).transpose(0, 2, 1, 3)
         glu_out_grad = full[:, 2 * width :].transpose(2, 0, 1).reshape(half, model)
         total = (extra.astype(F32) + extra_back.astype(F32)).astype(BF)
-        piece = exchanged(total, "seq").reshape(seq_devices, -1, model // 2)
+        piece = exchanged(total.reshape(seq_devices, -1), "seq")
         piece = jnp.sum(piece.astype(F32), axis=0).astype(BF)
-        full = gathered_over(piece, seq_devices).reshape(2, width, model // 2).astype(F32)
-        out_proj_grad = full.transpose(1, 0, 2).reshape(width, model)
+        mine = gathered_over(piece, seq_devices).reshape(width, model // 2).astype(F32)
+        theirs = swapped(mine)
+        out_proj_grad = jnp.where(
+            tp_index == 0, jnp.concatenate([mine, theirs], axis=1), jnp.concatenate([theirs, mine], axis=1)
+        )
         mine = gathered_over(in_piece, seq_devices)
         theirs = swapped(mine)
         pair = jnp.where(tp_index == 0, jnp.stack([mine, theirs], 1), jnp.stack([theirs, mine], 1)).astype(F32)

time: 175 us -> 165 us (0.943)
  waiting for transfers between devices: 33 us -> 28.7 us
  local copies, waits for them, and re-layouts: 12.7 us -> 9.77 us
  Pallas kernels: 67.4 us -> 65.1 us
    unnamed x70 -> x68, local copies, waits for them, and re-layouts: 10 us -> 7.09 us
    ppermute x18, waiting for transfers between devices: 25 us -> 22.3 us  [crossed(): return lax.ppermute(x, 'seq', [(i, i ^ mask) for i in range(devices)])]
    pallas_call x2, Pallas kernels: 2.21 us -> 0.2 us  [plane_join(): pl.pallas_call(functools.partial(plane_join_kernel, cut), in_specs=vmem_s...]
  transfers between devices with their start and end apart: 41 -> 42, of which waited for: 8 -> 10; matrix products, arithmetic and copies ran while one was open for 2% -> 2% of each run, Pallas kernels for 33% -> 35%
where the time goes in v2:
time: 165 us; the launch traced here: 164 us
  Pallas kernels  65.1 us (39%)
  starting transfers between devices  57.9 us (35%)
  waiting for transfers between devices  28.7 us (17%)
  local copies, waits for them, and re-layouts  9.77 us (6%)
    ppermute x18, starting transfers between devices, crossed(): return lax.ppermute(x, 'seq', [(i, i ^ mask) for i in range(devices)])  25.2 us
    all_to_all x6, starting transfers between devices, exchanged(): return lax.all_to_all(x, axes, 0, 0, axis_index_groups=groups, tiled=True)  24.7 us
    ppermute x18, waiting for transfers between devices, crossed(): return lax.ppermute(x, 'seq', [(i, i ^ mask) for i in range(devices)])  22.3 us
    pallas_call x1, Pallas kernels, channel_grads(): pl.pallas_call(functools.partial(channel_grads_kernel, place, turns, tabl...  10.9 us
    pallas_call x1, Pallas kernels, filter_forward(): pl.pallas_call(filter_forward_kernel, in_specs=vmem_specs(6), out_specs=v...  8.4 us
    pallas_call x1, Pallas kernels, conv_backward(): pl.pallas_call(functools.partial(conv_backward_kernel, padded, seqs, real...  7.94 us
    pallas_call x1, Pallas kernels, middle_part(): pl.pallas_call(functools.partial(middle_kernel, per_plane), in_specs=vmem...  7.84 us
    unnamed x68, local copies, waits for them, and re-layouts  7.09 us
  transfers between devices with their start and end apart: 42, of which 10 were waited for; matrix products, arithmetic and copies ran while one was open for 2% of the time, Pallas kernels for 35%

profile of v2, /device:TPU:0, one launch (start us, length us, event | category | flops | bytes accessed | tf_op | source)
XLA Modules:
  0.0 164.0 jit_solution(14533670973893446919)
XLA Ops:
  0.7 0.8 slice.30
  1.5 4.8 %collective-permute-start = (bf16[16,768]{1,0:T(8,128)(2,1)S(1)}, bf16[16,768]{1,0:T(8,128)(2,1)S(1)}, u32[]{:S(2)}, u32[]{:S(2)}) collective-permute-start(bf16[16,768]{1,0:T(8,128)(2,1)S(1)} %slice.30), channel_id=1, source_target_pairs={{0,2},{2,4},{4,6},{6,8},{8,10},{10,12},{12,14},{14,16},{16,18},{18... | collective-permute-start | bytes 73736 | tf_op jit(solution)/shard_map/ppermute | solution.py:1033
  6.4 8.4 %filter_forward.1 = (f32[24,4096]{1,0:T(8,128)}, f32[24,4096]{1,0:T(8,128)}, bf16[128,4096]{1,0:T(8,128)(2,1)}, bf16[128,4096]{1,0:T(8,128)(2,1)}, bf16[128,4096]{1,0:T(8,128)(2,1)}, /*index=5*/bf16[128,4096]{1,0:T(8,128)(2,1)}) custom-call(bf16[48,8192]{1,0:T(8,128)(2,1)} %constant.34.clone.feat_ref, f32[5,128]{1,0:T(8,128)} %w1_ref.1, f32[128]{0:T(128)} %b1_ref.1, ...), custom_call_target="tpu_custom_call" | custom-call | flops 400000000 | bytes 400000 | tf_op jit(solution)/shard_map/filter_forward/pallas_call | solution.py:224
  14.8 1.9 %mixer_in.1 = (bf16[768,128]{1,0:T(8,128)(2,1)}, f32[128,768]{1,0:T(8,128)S(1)}, bf16[384,128]{1,0:T(8,128)(2,1)S(1)}, bf16[384,128]{1,0:T(8,128)(2,1)}, bf16[38...) custom-call(bf16[256,768]{1,0:T(8,128)(2,1)S(1)} %copy-done.7, bf16[16,768]{1,0:T(8,128)(2,1)S(1)} %collective-permute-done.halo_ref, ...), custom_call_target="tpu_custom_call" | custom-call | flops 200000000 | bytes 200000 | tf_op jit(solution)/shard_map/mixer_in/pallas_call | solution.py:647
  16.9 0.6 copy-done.15
  17.5 0.4 copy-done.32
  18.0 5.1 %all-to-all-start = ((bf16[32,24,128]{2,1,0:T(8,128)(2,1)}), bf16[32,24,128]{2,1,0:T(8,128)(2,1)}, u32[]{:S(2)}, u32[]{:S(2)}) async-start(bf16[32,24,128]{2,1,0:T(8,128)(2,1)} %bitcast.2), calls=%async_computation | async-start | bytes 393216 | tf_op jit(solution)/shard_map/all_to_all | solution.py:1046
  23.1 1.8 %collective-permute-start.4 = (bf16[384,128]{1,0:T(8,128)(2,1)}, bf16[384,128]{1,0:T(8,128)(2,1)}, u32[]{:S(2)}, u32[]{:S(2)}) collective-permute-start(bf16[384,128]{1,0:T(8,128)(2,1)} %get-tuple-element.104), channel_id=1, source_target_pairs={{0,8},{2,10},{4,12},{6,14},{8,0},{10,2},{12,4},{14,6},{16,24},{18,... | collective-permute-start | bytes 294920 | tf_op jit(solution)/shard_map/ppermute | solution.py:1042
  24.9 2.4 %collective-permute-start.5 = (bf16[384,128]{1,0:T(8,128)(2,1)}, bf16[384,128]{1,0:T(8,128)(2,1)}, u32[]{:S(2)}, u32[]{:S(2)}) collective-permute-start(bf16[384,128]{1,0:T(8,128)(2,1)} %get-tuple-element.106), channel_id=1, source_target_pairs={{0,16},{2,18},{4,20},{6,22},{8,24},{10,26},{12,28},{14,30},{16,0},... | collective-permute-start | bytes 294920 | tf_op jit(solution)/shard_map/ppermute | solution.py:1042
  27.3 0.3 collective-permute-start.6
  27.5 4.3 %filter_spectrum.1.h_ref = f32[960,256]{1,0:T(8,128)} custom-call(f32[24,4096]{1,0:T(8,128)} %get-tuple-element.94.own_ref, f32[24,4096]{1,0:T(8,128)} %collective-permute-done.1.other_ref, bf16[640,512]{1,0:T(8,128)(2,1)} %constant.35.clone.fh, bf16[640,512]{1,0:T(8,128)(2,1)} %constant.36.clone.fl, f32[4,40,128]{2,1,0:T(8,128)} %constant.37.clone.tw, ...), custom_call_target="tpu_custom_call" | custom-call | flops 200000000 | bytes 200000 | tf_op jit(solution)/shard_map/filter_spectrum/pallas_call | solution.py:379
  31.8 0.6 all-to-all-done.x_ref
  32.4 5.0 %conv_forward.1 = (bf16[32,24,128]{2,1,0:T(8,128)(2,1)}, f32[960,256]{1,0:T(8,128)}) custom-call(bf16[32,24,128]{2,1,0:T(8,128)(2,1)} %all-to-all-done.x_ref, f32[960,256]{1,0:T(8,128)} %filter_spectrum.1.h_ref, bf16[640,256]{1,0:T(8,128)(2,1)} %constant.40.clone.fh, bf16[640,256]{1,0:T(8,128)(2,1)} %constant.41.clone.fl, f32[4,40,128]{2,1,0:T(8,128)} %constant.37.clone.tw, ...), custom_call_target="tpu_custom_call" | custom-call | flops 250000000 | bytes 300000 | tf_op jit(solution)/shard_map/conv_forward/pallas_call | solution.py:396
  37.4 5.6 %all-to-all-start.1 = ((bf16[32,24,128]{2,1,0:T(8,128)(2,1)}), bf16[32,24,128]{2,1,0:T(8,128)(2,1)}, u32[]{:S(2)}, u32[]{:S(2)}) async-start(bf16[32,24,128]{2,1,0:T(8,128)(2,1)} %get-tuple-element.97.y_ref), calls=%async_computation.1 | async-start | bytes 393216 | tf_op jit(solution)/shard_map/all_to_all | solution.py:1046
  43.0 0.8 slice_bitcast_fusion.2
  43.9 0.8 slice_bitcast_fusion
  44.7 0.7 pad_maximum_fusion.refs_0_
  45.4 2.4 %collective-permute-start.9 = (bf16[4,192,128]{2,1,0:T(8,128)(2,1)}, bf16[4,192,128]{2,1,0:T(8,128)(2,1)}, u32[]{:S(2)}, u32[]{:S(2)}) collective-permute-start(bf16[4,192,128]{2,1,0:T(8,128)(2,1)} %pad_maximum_fusion.refs_0_), channel_id=1, source_target_pairs={{0,6},{2,4},{4,2},{6,0},{8,14},{10,12},{12,10},{14,8},{16,22},{18,... | collective-permute-start | bytes 589832 | tf_op jit(solution)/shard_map/ppermute | solution.py:1042
  47.9 0.6 collective-permute-start.8
  48.4 0.5 collective-permute-start.7
  48.9 2.9 %all-to-all-done.1 = bf16[32,24,128]{2,1,0:T(8,128)(2,1)} async-done(((bf16[32,24,128]{2,1,0:T(8,128)(2,1)}), bf16[32,24,128]{2,1,0:T(8,128)(2,1)}, u32[]{:S(2)}, u32[]{:S(2)}) %all-to-all-start.1) | async-done | bytes 196640 | tf_op jit(solution)/shard_map/all_to_all | solution.py:1046
  51.8 1.0 copy-done.5
  52.8 7.8 %middle_part.1 = (bf16[768,128]{1,0:T(8,128)(2,1)}, f32[128,768]{1,0:T(8,128)}, bf16[128,768]{1,0:T(8,128)(2,1)}, bf16[192,384]{1,0:T(8,128)(2,1)}, bf16[192,384...) custom-call(bf16[768,128]{1,0:T(8,128)(2,1)} %bitcast.4.conv_ref, ...), custom_call_target="tpu_custom_call" | custom-call | flops 450000000 | bytes 300000 | tf_op jit(solution)/shard_map/middle_part/pallas_call | solution.py:734
  60.7 2.9 %all-to-all-start.2 = ((bf16[32,24,128]{2,1,0:T(8,128)(2,1)}), bf16[32,24,128]{2,1,0:T(8,128)(2,1)S(1)}, u32[]{:S(2)}, u32[]{:S(2)}) async-start(bf16[32,24,128]{2,1,0:T(8,128)(2,1)} %bitcast.26), calls=%async_computation.2 | async-start | bytes 393216 | tf_op jit(solution)/shard_map/all_to_all | solution.py:1046
  63.6 0.3 collective-permute-start.13
  64.2 0.3 collective-permute-start.11
  64.7 3.6 %collective-permute-start.16 = (bf16[192,128]{1,0:T(8,128)(2,1)}, bf16[192,128]{1,0:T(8,128)(2,1)S(1)}, u32[]{:S(2)}, u32[]{:S(2)}) collective-permute-start(bf16[192,128]{1,0:T(8,128)(2,1)} %get-tuple-element.121), channel_id=1, source_target_pairs={{0,24},{2,26},{4,28},{6,30},{8,16},{10,18},{12,20},{14,22},{16,8},... | collective-permute-start | bytes 147464 | tf_op jit(solution)/shard_map/ppermute | solution.py:1042
  68.4 1.2 collective-permute-start.14
  69.6 4.9 %channel_mixer.1 = (f32[32,72,128]{2,1,0:T(8,128)}, f32[32,72,128]{2,1,0:T(8,128)}) custom-call(bf16[3,192,768]{2,1,0:T(8,128)(2,1)} %bitcast.19, f32[3,3,768]{2,1,0:T(4,128)} %taps_ref.5, bf16[4,192,128]{2,1,0:T(8,128)(2,1)} %pad_maximum_fusion.refs_0_, bf16[4,192,128]{2,1,0:T(8,128)(2,1)} %collective-permute-done.7.refs_1_, ...), custom_call_target="tpu_custom_call" | custom-call | flops 150000000 | bytes 300000 | tf_op jit(solution)/shard_map/channel_mixer/pallas_call | solution.py:489
  74.5 1.3 collective-permute-done.15.zc
  75.8 1.1 copy-done.12
  76.9 3.9 %glu_grads.1 = (f32[576,384]{1,0:T(8,128)S(1)}, bf16[576,384]{1,0:T(8,128)(2,1)S(1)}) custom-call(bf16[192,128]{1,0:T(8,128)(2,1)S(1)} %copy-done.23, bf16[192,128]{1,0:T(8,128)(2,1)S(1)} %collective-permute-done.14.zb, bf16[192,128]{1,0:T(8,128)(2,1)S(1)} %collective-permute-done.15.zc, bf16[192,128]{1,0:T(8,128)(2,1)S(1)} %collective-permute-done.16.zd, ...), custom_call_target="tpu_custom_call" | custom-call | flops 450000000 | bytes 200000 | tf_op jit(solution)/shard_map/glu_grads/pallas_call | solution.py:780
  80.9 0.5 collective-permute-start.18
  81.4 1.5 collective-permute-done.18.theirs_ref
  82.9 0.9 plane_add.1
  83.8 3.6 %all-to-all-start.3 = ((bf16[4,192,384]{2,1,0:T(8,128)(2,1)}), bf16[4,192,384]{2,1,0:T(8,128)(2,1)S(1)}, u32[]{:S(2)}, u32[]{:S(2)}) async-start(bf16[4,192,384]{2,1,0:T(8,128)(2,1)} %plane_add.1), calls=%async_computation.3 | async-start | bytes 1179648 | tf_op jit(solution)/shard_map/all_to_all | solution.py:1046
  87.5 7.9 %conv_backward.1 = (bf16[32,72,128]{2,1,0:T(8,128)(2,1)}, f32[960,256]{1,0:T(8,128)}, f32[72,128]{1,0:T(8,128)}) custom-call(bf16[32,24,128]{2,1,0:T(8,128)(2,1)} %copy-done.28, f32[32,72,128]{2,1,0:T(8,128)} %get-tuple-element.128.sm_ref, f32[32,72,128]{2,1,0:T(8,128)} %get-tuple-element.115.p_ref, bf16[32,24,128]{2,1,0:T(8,128)(2,1)} %get-tuple-element.97.y_ref, ...), custom_call_target="tpu_custom_call" | custom-call | flops 350000000 | bytes 450000 | tf_op jit(solution)/shard_map/conv_backward/pallas_call | solution.py:413
  95.4 1.2 all-to-all-done.3.x_ref
  96.6 3.8 %all-to-all-start.4 = ((bf16[32,72,128]{2,1,0:T(8,128)(2,1)}), bf16[32,72,128]{2,1,0:T(8,128)(2,1)S(1)}, u32[]{:S(2)}, u32[]{:S(2)}) async-start(bf16[32,72,128]{2,1,0:T(8,128)(2,1)} %get-tuple-element.145.pg_ref), calls=%async_computation.4 | async-start | bytes 1179648 | tf_op jit(solution)/shard_map/all_to_all | solution.py:1046
  100.5 3.6 %collective-permute-start.22 = (bf16[192,384]{1,0:T(8,128)(2,1)S(1)}, bf16[192,384]{1,0:T(8,128)(2,1)S(1)}, u32[]{:S(2)}, u32[]{:S(2)}) collective-permute-start(bf16[192,384]{1,0:T(8,128)(2,1)S(1)} %plane_sum.1.a0), channel_id=1, source_target_pairs={{0,24},{2,26},{4,28},{6,30},{8,16},{10,18},{12,20},{14,22},{16,8},... | collective-permute-start | bytes 442376 | tf_op jit(solution)/shard_map/ppermute | solution.py:1042
  104.1 0.9 collective-permute-start.20
  105.0 0.9 copy-done.27
  105.9 10.9 %channel_grads.1 = (bf16[144,256]{1,0:T(8,128)(2,1)}, f32[48,128]{1,0:T(8,128)}) custom-call(bf16[32,72,128]{2,1,0:T(8,128)(2,1)} %get-tuple-element.145.pg_ref, f32[72,128]{1,0:T(8,128)} %get-tuple-element.133.st_ref, f32[960,256]{1,0:T(8,128)} %get-tuple-element.134.own_ref, f32[960,256]{1,0:T(8,128)} %copy-done.27, f32[4,40,128]{2,1,0:T(8,128)} %constant.37.clone.tw, ...), custom_call_target="tpu_custom_call" | custom-call | flops 400000000 | bytes 400000 | tf_op jit(solution)/shard_map/channel_grads/pallas_call | solution.py:560
  116.8 2.6 %collective-permute-start.25 = (bf16[144,256]{1,0:T(8,128)(2,1)}, bf16[144,256]{1,0:T(8,128)(2,1)S(1)}, u32[]{:S(2)}, u32[]{:S(2)}) collective-permute-start(bf16[144,256]{1,0:T(8,128)(2,1)} %get-tuple-element.148.a0), channel_id=1, source_target_pairs={{0,6},{2,4},{4,2},{6,0},{8,14},{10,12},{12,10},{14,8},{16,22},{18,... | collective-permute-start | bytes 221192 | tf_op jit(solution)/shard_map/ppermute | solution.py:1042
  119.5 0.6 collective-permute-start.24
  120.0 0.4 collective-permute-start.23
  120.4 8.8 %collective-permute-done.21.a2 = bf16[192,384]{1,0:T(8,128)(2,1)S(1)} collective-permute-done((bf16[192,384]{1,0:T(8,128)(2,1)S(1)}, bf16[192,384]{1,0:T(8,128)(2,1)S(1)}, u32[]{:S(2)}, u32[]{:S(2)}) %collective-permute-start.21) | collective-permute-done | bytes 147488 | tf_op jit(solution)/shard_map/ppermute | solution.py:1042
  129.4 1.2 copy-done.4
  130.6 0.7 mixer_back.1.half_ref
  131.6 3.7 %all-to-all-start.5 = ((bf16[4,624,384]{2,1,0:T(8,128)(2,1)}), bf16[4,624,384]{2,1,0:T(8,128)(2,1)S(1)}, u32[]{:S(2)}, u32[]{:S(2)}) async-start(bf16[4,624,384]{2,1,0:T(8,128)(2,1)} %copy-done.4), calls=%async_computation.5 | async-start | bytes 3833856 | tf_op jit(solution)/shard_map/all_to_all | solution.py:1046
  135.3 1.9 %collective-permute-start.27 = (bf16[360,256]{1,0:T(8,128)(2,1)S(1)}, bf16[360,256]{1,0:T(8,128)(2,1)}, u32[]{:S(2)}, u32[]{:S(2)}) collective-permute-start(bf16[360,256]{1,0:T(8,128)(2,1)S(1)} %plane_join.3.refs_0_), channel_id=1, source_target_pairs={{0,16},{2,18},{4,20},{6,22},{8,24},{10,26},{12,28},{14,30},{16,0},... | collective-permute-start | bytes 552968 | tf_op jit(solution)/shard_map/ppermute | solution.py:1042
  137.2 2.4 %collective-permute-start.28 = (bf16[360,256]{1,0:T(8,128)(2,1)S(1)}, bf16[360,256]{1,0:T(8,128)(2,1)}, u32[]{:S(2)}, u32[]{:S(2)}) collective-permute-start(bf16[360,256]{1,0:T(8,128)(2,1)S(1)} %plane_join.3.refs_0_), channel_id=1, source_target_pairs={{0,24},{2,26},{4,28},{6,30},{8,16},{10,18},{12,20},{14,22},{16,8},... | collective-permute-start | bytes 552968 | tf_op jit(solution)/shard_map/ppermute | solution.py:1042
  139.6 4.6 %collective-permute-done.26.refs_1_ = bf16[360,256]{1,0:T(8,128)(2,1)} collective-permute-done((bf16[360,256]{1,0:T(8,128)(2,1)S(1)}, bf16[360,256]{1,0:T(8,128)(2,1)}, u32[]{:S(2)}, u32[]{:S(2)}) %collective-permute-start.26) | collective-permute-done | bytes 184352 | tf_op jit(solution)/shard_map/ppermute | solution.py:1042
  144.2 7.6 %collective-permute-done.27.refs_2_ = bf16[360,256]{1,0:T(8,128)(2,1)} collective-permute-done((bf16[360,256]{1,0:T(8,128)(2,1)S(1)}, bf16[360,256]{1,0:T(8,128)(2,1)}, u32[]{:S(2)}, u32[]{:S(2)}) %collective-permute-start.27) | collective-permute-done | bytes 184352 | tf_op jit(solution)/shard_map/ppermute | solution.py:1042
  151.8 0.5 collective-permute-start.32
  152.4 0.7 copy-done.19
  153.1 0.4 collective-permute-start.33
  153.6 0.3 collective-permute-done.32.refs_7_
  153.8 0.9 copy-done.20
  154.8 4.5 %in_unpack.1 = (f32[3,192,768]{2,1,0:T(8,128)}, f32[3,3,768]{2,1,0:T(4,128)}, f32[768]{0:T(1024)}, f32[5,128]{1,0:T(8,128)}, f32[128]{0:T(128)}, /*index=5*/f32[128,128]{1,0:T(8,128)}, f32[768]{0:T(1024)}) custom-call(bf16[3,192,768]{2,1,0:T(8,128)(2,1)S(1)} %bitcast.22, f32[768]{0:T(1024)S(1)} %copy-done.24, bf16[360,256]{1,0:T(8,128)(2,1)S(1)} %plane_join.3.refs_0_, ...), custom_call_target="tpu_custom_call" | custom-call | flops 5000000 | bytes 200000 | tf_op jit(solution)/shard_map/in_unpack/pallas_call | solution.py:970
  159.3 0.3 collective-permute-start.35
  159.6 0.6 fusion
  160.2 2.9 %finish.1 = (f32[4,192,2,384]{3,2,1,0:T(2,128)}, f32[384,768]{1,0:T(8,128)}, bf16[256,768]{1,0:T(8,128)(2,1)}) custom-call(bf16[4,624,384]{2,1,0:T(8,128)(2,1)S(1)} %all-to-all-done.5.a_ref, bf16[128,768]{1,0:T(8,128)(2,1)S(1)} %mixer_back.1.half_ref, bf16[128,768]{1,0:T(8,128)(2,1)S(1)} %collective-permute-done.33.back_ref), custom_call_target="tpu_custom_call" | custom-call | flops 5000000 | bytes 300000 | tf_op jit(solution)/shard_map/finish/pallas_call | solution.py:885
  163.1 0.9 out_unpack.1
  (113 shorter events, 1.8 us)
Async XLA Ops:
  0.6 14.2 %copy-start.7 = (bf16[256,768]{1,0:T(8,128)(2,1)S(1)}, bf16[256,768]{1,0:T(8,128)(2,1)}, u32[]{:S(2)}) copy-start(bf16[256,768]{1,0:T(8,128)(2,1)} %x_ref.5) | copy-start | bytes 1179652
  0.7 14.2 %copy-start = (bf16[192,3,768]{2,0,1:T(8,128)(2,1)S(1)}, bf16[192,3,768]{2,0,1:T(8,128)(2,1)}, u32[]{:S(2)}) copy-start(bf16[192,3,768]{2,0,1:T(8,128)(2,1)} %param.30) | copy-start | bytes 2654212
  0.7 14.1 %copy-start.24 = (f32[768]{0:T(1024)S(1)}, f32[768]{0:T(1024)}, u32[]{:S(2)}) copy-start(f32[768]{0:T(1024)} %gain_ref.7) | copy-start | bytes 9220
  0.7 14.1 %copy-start.16 = (f32[3,3,768]{2,1,0:T(4,128)S(1)}, f32[3,3,768]{2,1,0:T(4,128)}, u32[]{:S(2)}) copy-start(f32[3,3,768]{2,1,0:T(4,128)} %taps_ref.5) | copy-start | bytes 82948
  0.7 14.1 %copy-start.13 = (bf16[128,768]{1,0:T(8,128)(2,1)S(1)}, bf16[128,768]{1,0:T(8,128)(2,1)}, u32[]{:S(2)}) copy-start(bf16[128,768]{1,0:T(8,128)(2,1)} %og_ref.3) | copy-start | bytes 589828
  1.5 13.2 %collective-permute-start = (bf16[16,768]{1,0:T(8,128)(2,1)S(1)}, bf16[16,768]{1,0:T(8,128)(2,1)S(1)}, u32[]{:S(2)}, u32[]{:S(2)}) collective-permute-start(bf16[16,768]{1,0:T(8,128)(2,1)S(1)} %slice.30), channel_id=1, source_target_pairs={{0,2},{2,4},{4,6},{6,8},{8,10},{10,12},{12,14},{14,16},{16,18},{18... | collective-permute-start | bytes 73736 | tf_op jit(solution)/shard_map/ppermute | solution.py:1033
  14.8 1.9 %copy-start.25 = (bf16[4,192,2,384]{3,2,1,0:T(2,128)(2,1)S(1)}, bf16[4,192,2,384]{3,2,1,0:T(2,128)(2,1)}, u32[]{:S(2)}) copy-start(bf16[4,192,2,384]{3,2,1,0:T(2,128)(2,1)} %param.39) | copy-start | bytes 3538948
  16.7 10.8 %copy-start.9 = (bf16[384,768]{1,0:T(8,128)(2,1)S(1)}, bf16[384,768]{1,0:T(8,128)(2,1)}, u32[]{:S(2)}) copy-start(bf16[384,768]{1,0:T(8,128)(2,1)} %da_ref.1) | copy-start | bytes 1769476
  17.5 14.4 %copy-start.2 = (bf16[4,192,2,384]{3,1,2,0:T(8,128)(2,1)}, bf16[4,192,2,384]{3,1,2,0:T(8,128)(2,1)S(1)}, u32[]{:S(2)}) copy-start(bf16[4,192,2,384]{3,1,2,0:T(8,128)(2,1)S(1)} %copy.43) | copy-start | bytes 3538948
  17.5 34.3 %collective-permute-start.2 = (bf16[4,2,192,384]{3,2,1,0:T(8,128)(2,1)S(1)}, bf16[4,2,192,384]{3,2,1,0:T(8,128)(2,1)S(1)}, u32[]{:S(2)}, u32[]{:S(2)}) collective-permute-start(bf16[4,2,192,384]{3,2,1,0:T(8,128)(2,1)S(1)} %bitcast.23), channel_id=1, source_target_pairs={{0,1},{1,0},{2,3},{3,2},{4,5},{5,4},{6,7},{7,6},{8,9},{9,8},{10,11... | collective-permute-start | bytes 3538952 | tf_op jit(solution)/shard_map/ppermute | solution.py:1037
  17.9 9.6 %collective-permute-start.1 = (f32[24,4096]{1,0:T(8,128)S(1)}, f32[24,4096]{1,0:T(8,128)}, u32[]{:S(2)}, u32[]{:S(2)}) collective-permute-start(f32[24,4096]{1,0:T(8,128)S(1)} %copy-done.32), channel_id=1, source_target_pairs={{0,1},{1,0},{2,3},{3,2},{4,5},{5,4},{6,7},{7,6},{8,9},{9,8},{10,11... | collective-permute-start | bytes 1179656 | tf_op jit(solution)/shard_map/ppermute | solution.py:1037
  18.0 14.4 %all-to-all-start = ((bf16[32,24,128]{2,1,0:T(8,128)(2,1)}), bf16[32,24,128]{2,1,0:T(8,128)(2,1)}, u32[]{:S(2)}, u32[]{:S(2)}) async-start(bf16[32,24,128]{2,1,0:T(8,128)(2,1)} %bitcast.2), calls=%async_computation | async-start | bytes 393216 | tf_op jit(solution)/shard_map/all_to_all | solution.py:1046
  23.1 19.9 %collective-permute-start.4 = (bf16[384,128]{1,0:T(8,128)(2,1)}, bf16[384,128]{1,0:T(8,128)(2,1)}, u32[]{:S(2)}, u32[]{:S(2)}) collective-permute-start(bf16[384,128]{1,0:T(8,128)(2,1)} %get-tuple-element.104), channel_id=1, source_target_pairs={{0,8},{2,10},{4,12},{6,14},{8,0},{10,2},{12,4},{14,6},{16,24},{18,... | collective-permute-start | bytes 294920 | tf_op jit(solution)/shard_map/ppermute | solution.py:1042
  24.9 19.0 %collective-permute-start.5 = (bf16[384,128]{1,0:T(8,128)(2,1)}, bf16[384,128]{1,0:T(8,128)(2,1)}, u32[]{:S(2)}, u32[]{:S(2)}) collective-permute-start(bf16[384,128]{1,0:T(8,128)(2,1)} %get-tuple-element.106), channel_id=1, source_target_pairs={{0,16},{2,18},{4,20},{6,22},{8,24},{10,26},{12,28},{14,30},{16,0},... | collective-permute-start | bytes 294920 | tf_op jit(solution)/shard_map/ppermute | solution.py:1042
  27.3 16.6 %collective-permute-start.6 = (bf16[384,128]{1,0:T(8,128)(2,1)}, bf16[384,128]{1,0:T(8,128)(2,1)}, u32[]{:S(2)}, u32[]{:S(2)}) collective-permute-start(bf16[384,128]{1,0:T(8,128)(2,1)} %get-tuple-element.108), channel_id=1, source_target_pairs={{0,24},{2,26},{4,28},{6,30},{8,16},{10,18},{12,20},{14,22},{16,8},... | collective-permute-start | bytes 294920 | tf_op jit(solution)/shard_map/ppermute | solution.py:1042
  27.5 21.4 %collective-permute-start.3 = (bf16[384,768]{1,0:T(8,128)(2,1)S(1)}, bf16[384,768]{1,0:T(8,128)(2,1)S(1)}, u32[]{:S(2)}, u32[]{:S(2)}) collective-permute-start(bf16[384,768]{1,0:T(8,128)(2,1)S(1)} %copy-done.9), channel_id=1, source_target_pairs={{0,1},{1,0},{2,3},{3,2},{4,5},{5,4},{6,7},{7,6},{8,9},{9,8},{10,11... | collective-permute-start | bytes 1769480 | tf_op jit(solution)/shard_map/ppermute | solution.py:1037
  37.4 14.4 %all-to-all-start.1 = ((bf16[32,24,128]{2,1,0:T(8,128)(2,1)}), bf16[32,24,128]{2,1,0:T(8,128)(2,1)}, u32[]{:S(2)}, u32[]{:S(2)}) async-start(bf16[32,24,128]{2,1,0:T(8,128)(2,1)} %get-tuple-element.97.y_ref), calls=%async_computation.1 | async-start | bytes 393216 | tf_op jit(solution)/shard_map/all_to_all | solution.py:1046
  45.4 18.1 %collective-permute-start.9 = (bf16[4,192,128]{2,1,0:T(8,128)(2,1)}, bf16[4,192,128]{2,1,0:T(8,128)(2,1)}, u32[]{:S(2)}, u32[]{:S(2)}) collective-permute-start(bf16[4,192,128]{2,1,0:T(8,128)(2,1)} %pad_maximum_fusion.refs_0_), channel_id=1, source_target_pairs={{0,6},{2,4},{4,2},{6,0},{8,14},{10,12},{12,10},{14,8},{16,22},{18,... | collective-permute-start | bytes 589832 | tf_op jit(solution)/shard_map/ppermute | solution.py:1042
  47.9 16.1 %collective-permute-start.8 = (bf16[4,192,128]{2,1,0:T(8,128)(2,1)}, bf16[4,192,128]{2,1,0:T(8,128)(2,1)}, u32[]{:S(2)}, u32[]{:S(2)}) collective-permute-start(bf16[4,192,128]{2,1,0:T(8,128)(2,1)} %pad_maximum_fusion.refs_0_), channel_id=1, source_target_pairs={{0,4},{2,6},{4,0},{6,2},{8,12},{10,14},{12,8},{14,10},{16,20},{18,... | collective-permute-start | bytes 589832 | tf_op jit(solution)/shard_map/ppermute | solution.py:1042
  48.4 15.7 %collective-permute-start.7 = (bf16[4,192,128]{2,1,0:T(8,128)(2,1)}, bf16[4,192,128]{2,1,0:T(8,128)(2,1)}, u32[]{:S(2)}, u32[]{:S(2)}) collective-permute-start(bf16[4,192,128]{2,1,0:T(8,128)(2,1)} %pad_maximum_fusion.refs_0_), channel_id=1, source_target_pairs={{0,2},{2,0},{4,6},{6,4},{8,10},{10,8},{12,14},{14,12},{16,18},{18,... | collective-permute-start | bytes 589832 | tf_op jit(solution)/shard_map/ppermute | solution.py:1042
  48.9 2.9 %copy-start.11 = (bf16[384,768]{1,0:T(8,128)(2,1)}, bf16[384,768]{1,0:T(8,128)(2,1)S(1)}, u32[]{:S(2)}) copy-start(bf16[384,768]{1,0:T(8,128)(2,1)S(1)} %collective-permute-done.3.db_ref) | copy-start | bytes 1769476
  52.8 22.9 %copy-start.10 = (bf16[384,768]{1,0:T(8,128)(2,1)S(1)}, bf16[384,768]{1,0:T(8,128)(2,1)}, u32[]{:S(2)}) copy-start(bf16[384,768]{1,0:T(8,128)(2,1)} %da_ref.1) | copy-start | bytes 1769476
  60.7 15.1 %copy-start.23 = (bf16[192,128]{1,0:T(8,128)(2,1)S(1)}, bf16[192,128]{1,0:T(8,128)(2,1)}, u32[]{:S(2)}) copy-start(bf16[192,128]{1,0:T(8,128)(2,1)} %get-tuple-element.116.za) | copy-start | bytes 147460
  60.7 13.8 %all-to-all-start.2 = ((bf16[32,24,128]{2,1,0:T(8,128)(2,1)}), bf16[32,24,128]{2,1,0:T(8,128)(2,1)S(1)}, u32[]{:S(2)}, u32[]{:S(2)}) async-start(bf16[32,24,128]{2,1,0:T(8,128)(2,1)} %bitcast.26), calls=%async_computation.2 | async-start | bytes 393216 | tf_op jit(solution)/shard_map/all_to_all | solution.py:1046
  63.6 4.7 %collective-permute-start.13 = (bf16[4,192,128]{2,1,0:T(8,128)(2,1)}, bf16[4,192,128]{2,1,0:T(8,128)(2,1)S(1)}, u32[]{:S(2)}, u32[]{:S(2)}) collective-permute-start(bf16[4,192,128]{2,1,0:T(8,128)(2,1)} %collective-permute-done.9.refs_3_), channel_id=1, source_target_pairs={{0,1},{1,0},{2,3},{3,2},{4,5},{5,4},{6,7},{7,6},{8,9},{9,8},{10,11... | collective-permute-start | bytes 589832 | tf_op jit(solution)/shard_map/ppermute | solution.py:1037
  63.9 4.4 %collective-permute-start.12 = (bf16[4,192,128]{2,1,0:T(8,128)(2,1)}, bf16[4,192,128]{2,1,0:T(8,128)(2,1)S(1)}, u32[]{:S(2)}, u32[]{:S(2)}) collective-permute-start(bf16[4,192,128]{2,1,0:T(8,128)(2,1)} %collective-permute-done.8.refs_2_), channel_id=1, source_target_pairs={{0,1},{1,0},{2,3},{3,2},{4,5},{5,4},{6,7},{7,6},{8,9},{9,8},{10,11... | collective-permute-start | bytes 589832 | tf_op jit(solution)/shard_map/ppermute | solution.py:1037
  64.2 5.4 %collective-permute-start.11 = (bf16[4,192,128]{2,1,0:T(8,128)(2,1)}, bf16[4,192,128]{2,1,0:T(8,128)(2,1)}, u32[]{:S(2)}, u32[]{:S(2)}) collective-permute-start(bf16[4,192,128]{2,1,0:T(8,128)(2,1)} %collective-permute-done.7.refs_1_), channel_id=1, source_target_pairs={{0,1},{1,0},{2,3},{3,2},{4,5},{5,4},{6,7},{7,6},{8,9},{9,8},{10,11... | collective-permute-start | bytes 589832 | tf_op jit(solution)/shard_map/ppermute | solution.py:1037
  64.4 5.2 %collective-permute-start.10 = (bf16[4,192,128]{2,1,0:T(8,128)(2,1)}, bf16[4,192,128]{2,1,0:T(8,128)(2,1)}, u32[]{:S(2)}, u32[]{:S(2)}) collective-permute-start(bf16[4,192,128]{2,1,0:T(8,128)(2,1)} %pad_maximum_fusion.refs_0_), channel_id=1, source_target_pairs={{0,1},{1,0},{2,3},{3,2},{4,5},{5,4},{6,7},{7,6},{8,9},{9,8},{10,11... | collective-permute-start | bytes 589832 | tf_op jit(solution)/shard_map/ppermute | solution.py:1037
  64.7 9.8 %collective-permute-start.16 = (bf16[192,128]{1,0:T(8,128)(2,1)}, bf16[192,128]{1,0:T(8,128)(2,1)S(1)}, u32[]{:S(2)}, u32[]{:S(2)}) collective-permute-start(bf16[192,128]{1,0:T(8,128)(2,1)} %get-tuple-element.121), channel_id=1, source_target_pairs={{0,24},{2,26},{4,28},{6,30},{8,16},{10,18},{12,20},{14,22},{16,8},... | collective-permute-start | bytes 147464 | tf_op jit(solution)/shard_map/ppermute | solution.py:1042
  68.3 7.5 %collective-permute-start.15 = (bf16[192,128]{1,0:T(8,128)(2,1)}, bf16[192,128]{1,0:T(8,128)(2,1)S(1)}, u32[]{:S(2)}, u32[]{:S(2)}) collective-permute-start(bf16[192,128]{1,0:T(8,128)(2,1)} %get-tuple-element.119), channel_id=1, source_target_pairs={{0,16},{2,18},{4,20},{6,22},{8,24},{10,26},{12,28},{14,30},{16,0},... | collective-permute-start | bytes 147464 | tf_op jit(solution)/shard_map/ppermute | solution.py:1042
  68.3 7.4 %copy-start.3 = (bf16[4,192,2,384]{3,1,2,0:T(8,128)(2,1)S(1)}, bf16[4,192,2,384]{3,1,2,0:T(8,128)(2,1)}, u32[]{:S(2)}) copy-start(bf16[4,192,2,384]{3,1,2,0:T(8,128)(2,1)} %copy-done.2) | copy-start | bytes 3538948
  68.3 7.4 %copy-start.6 = (bf16[4,2,192,384]{3,2,1,0:T(8,128)(2,1)S(1)}, bf16[4,2,192,384]{3,2,1,0:T(8,128)(2,1)}, u32[]{:S(2)}) copy-start(bf16[4,2,192,384]{3,2,1,0:T(8,128)(2,1)} %copy-done.5) | copy-start | bytes 3538948
  68.3 7.4 %copy-start.18 = (bf16[384,128]{1,0:T(8,128)(2,1)S(1)}, bf16[384,128]{1,0:T(8,128)(2,1)}, u32[]{:S(2)}) copy-start(bf16[384,128]{1,0:T(8,128)(2,1)} %copy-done.17) | copy-start | bytes 294916
  68.4 7.4 %collective-permute-start.14 = (bf16[192,128]{1,0:T(8,128)(2,1)}, bf16[192,128]{1,0:T(8,128)(2,1)S(1)}, u32[]{:S(2)}, u32[]{:S(2)}) collective-permute-start(bf16[192,128]{1,0:T(8,128)(2,1)} %get-tuple-element.117), channel_id=1, source_target_pairs={{0,8},{2,10},{4,12},{6,14},{8,0},{10,2},{12,4},{14,6},{16,24},{18,... | collective-permute-start | bytes 147464 | tf_op jit(solution)/shard_map/ppermute | solution.py:1042
  74.5 6.3 %copy-start.28 = (bf16[32,24,128]{2,1,0:T(8,128)(2,1)}, bf16[32,24,128]{2,1,0:T(8,128)(2,1)S(1)}, u32[]{:S(2)}) copy-start(bf16[32,24,128]{2,1,0:T(8,128)(2,1)S(1)} %all-to-all-done.2.g_ref) | copy-start | bytes 589828
  76.9 4.0 %copy-start.33 = (bf16[192,384]{1,0:T(8,128)(2,1)S(1)}, bf16[192,384]{1,0:T(8,128)(2,1)}, u32[]{:S(2)}) copy-start(bf16[192,384]{1,0:T(8,128)(2,1)} %get-tuple-element.126) | copy-start | bytes 442372
  76.9 6.0 %copy-start.21 = (bf16[192,384]{1,0:T(8,128)(2,1)S(1)}, bf16[192,384]{1,0:T(8,128)(2,1)}, u32[]{:S(2)}) copy-start(bf16[192,384]{1,0:T(8,128)(2,1)} %get-tuple-element.125.mine_ref) | copy-start | bytes 442372
  80.8 2.1 %collective-permute-start.17 = (bf16[576,384]{1,0:T(8,128)(2,1)S(1)}, bf16[576,384]{1,0:T(8,128)(2,1)S(1)}, u32[]{:S(2)}, u32[]{:S(2)}) collective-permute-start(bf16[576,384]{1,0:T(8,128)(2,1)S(1)} %get-tuple-element.124), channel_id=1, source_target_pairs={{0,1},{1,0},{2,3},{3,2},{4,5},{5,4},{6,7},{7,6},{8,9},{9,8},{10,11... | collective-permute-start | bytes 1327112 | tf_op jit(solution)/shard_map/ppermute | solution.py:1037
  80.9 2.0 %collective-permute-start.18 = (bf16[192,384]{1,0:T(8,128)(2,1)S(1)}, bf16[192,384]{1,0:T(8,128)(2,1)S(1)}, u32[]{:S(2)}, u32[]{:S(2)}) collective-permute-start(bf16[192,384]{1,0:T(8,128)(2,1)S(1)} %copy-done.33), channel_id=1, source_target_pairs={{0,1},{1,0},{2,3},{3,2},{4,5},{5,4},{6,7},{7,6},{8,9},{9,8},{10,11... | collective-permute-start | bytes 442376 | tf_op jit(solution)/shard_map/ppermute | solution.py:1037
  83.8 12.8 %all-to-all-start.3 = ((bf16[4,192,384]{2,1,0:T(8,128)(2,1)}), bf16[4,192,384]{2,1,0:T(8,128)(2,1)S(1)}, u32[]{:S(2)}, u32[]{:S(2)}) async-start(bf16[4,192,384]{2,1,0:T(8,128)(2,1)} %plane_add.1), calls=%async_computation.3 | async-start | bytes 1179648 | tf_op jit(solution)/shard_map/all_to_all | solution.py:1046
  95.4 4.9 %copy-start.26 = (f32[960,256]{1,0:T(8,128)S(1)}, f32[960,256]{1,0:T(8,128)}, u32[]{:S(2)}) copy-start(f32[960,256]{1,0:T(8,128)} %get-tuple-element.134.own_ref) | copy-start | bytes 2949124
  96.6 34.0 %all-to-all-start.4 = ((bf16[32,72,128]{2,1,0:T(8,128)(2,1)}), bf16[32,72,128]{2,1,0:T(8,128)(2,1)S(1)}, u32[]{:S(2)}, u32[]{:S(2)}) async-start(bf16[32,72,128]{2,1,0:T(8,128)(2,1)} %get-tuple-element.145.pg_ref), calls=%async_computation.4 | async-start | bytes 1179648 | tf_op jit(solution)/shard_map/all_to_all | solution.py:1046
  100.3 4.6 %collective-permute-start.19 = (f32[960,256]{1,0:T(8,128)S(1)}, f32[960,256]{1,0:T(8,128)S(1)}, u32[]{:S(2)}, u32[]{:S(2)}) collective-permute-start(f32[960,256]{1,0:T(8,128)S(1)} %copy-done.26), channel_id=1, source_target_pairs={{0,1},{1,0},{2,3},{3,2},{4,5},{5,4},{6,7},{7,6},{8,9},{9,8},{10,11... | collective-permute-start | bytes 2949128 | tf_op jit(solution)/shard_map/ppermute | solution.py:1037
  100.5 19.5 %collective-permute-start.22 = (bf16[192,384]{1,0:T(8,128)(2,1)S(1)}, bf16[192,384]{1,0:T(8,128)(2,1)S(1)}, u32[]{:S(2)}, u32[]{:S(2)}) collective-permute-start(bf16[192,384]{1,0:T(8,128)(2,1)S(1)} %plane_sum.1.a0), channel_id=1, source_target_pairs={{0,24},{2,26},{4,28},{6,30},{8,16},{10,18},{12,20},{14,22},{16,8},... | collective-permute-start | bytes 442376 | tf_op jit(solution)/shard_map/ppermute | solution.py:1042
  104.1 25.0 %collective-permute-start.21 = (bf16[192,384]{1,0:T(8,128)(2,1)S(1)}, bf16[192,384]{1,0:T(8,128)(2,1)S(1)}, u32[]{:S(2)}, u32[]{:S(2)}) collective-permute-start(bf16[192,384]{1,0:T(8,128)(2,1)S(1)} %plane_sum.1.a0), channel_id=1, source_target_pairs={{0,16},{2,18},{4,20},{6,22},{8,24},{10,26},{12,28},{14,30},{16,0},... | collective-permute-start | bytes 442376 | tf_op jit(solution)/shard_map/ppermute | solution.py:1042
  104.1 25.0 %collective-permute-start.20 = (bf16[192,384]{1,0:T(8,128)(2,1)S(1)}, bf16[192,384]{1,0:T(8,128)(2,1)S(1)}, u32[]{:S(2)}, u32[]{:S(2)}) collective-permute-start(bf16[192,384]{1,0:T(8,128)(2,1)S(1)} %plane_sum.1.a0), channel_id=1, source_target_pairs={{0,8},{2,10},{4,12},{6,14},{8,0},{10,2},{12,4},{14,6},{16,24},{18,... | collective-permute-start | bytes 442376 | tf_op jit(solution)/shard_map/ppermute | solution.py:1042
  116.8 13.8 %copy-start.1 = (bf16[192,3,768]{2,0,1:T(8,128)(2,1)S(1)}, bf16[192,3,768]{2,0,1:T(8,128)(2,1)}, u32[]{:S(2)}) copy-start(bf16[192,3,768]{2,0,1:T(8,128)(2,1)} %param.30) | copy-start | bytes 2654212
  116.8 13.8 %copy-start.8 = (bf16[256,768]{1,0:T(8,128)(2,1)S(1)}, bf16[256,768]{1,0:T(8,128)(2,1)}, u32[]{:S(2)}) copy-start(bf16[256,768]{1,0:T(8,128)(2,1)} %x_ref.5) | copy-start | bytes 1179652
  116.8 13.8 %copy-start.14 = (f32[128,768]{1,0:T(8,128)S(1)}, f32[128,768]{1,0:T(8,128)}, u32[]{:S(2)}) copy-start(f32[128,768]{1,0:T(8,128)} %get-tuple-element.147.mid_ref) | copy-start | bytes 1179652
  116.8 14.5 %collective-permute-start.25 = (bf16[144,256]{1,0:T(8,128)(2,1)}, bf16[144,256]{1,0:T(8,128)(2,1)S(1)}, u32[]{:S(2)}, u32[]{:S(2)}) collective-permute-start(bf16[144,256]{1,0:T(8,128)(2,1)} %get-tuple-element.148.a0), channel_id=1, source_target_pairs={{0,6},{2,4},{4,2},{6,0},{8,14},{10,12},{12,10},{14,8},{16,22},{18,... | collective-permute-start | bytes 221192 | tf_op jit(solution)/shard_map/ppermute | solution.py:1042
  119.5 11.9 %collective-permute-start.24 = (bf16[144,256]{1,0:T(8,128)(2,1)}, bf16[144,256]{1,0:T(8,128)(2,1)S(1)}, u32[]{:S(2)}, u32[]{:S(2)}) collective-permute-start(bf16[144,256]{1,0:T(8,128)(2,1)} %get-tuple-element.148.a0), channel_id=1, source_target_pairs={{0,4},{2,6},{4,0},{6,2},{8,12},{10,14},{12,8},{14,10},{16,20},{18,... | collective-permute-start | bytes 221192 | tf_op jit(solution)/shard_map/ppermute | solution.py:1042
  120.0 11.3 %collective-permute-start.23 = (bf16[144,256]{1,0:T(8,128)(2,1)}, bf16[144,256]{1,0:T(8,128)(2,1)S(1)}, u32[]{:S(2)}, u32[]{:S(2)}) collective-permute-start(bf16[144,256]{1,0:T(8,128)(2,1)} %get-tuple-element.148.a0), channel_id=1, source_target_pairs={{0,2},{2,0},{4,6},{6,4},{8,10},{10,8},{12,14},{14,12},{16,18},{18,... | collective-permute-start | bytes 221192 | tf_op jit(solution)/shard_map/ppermute | solution.py:1042
  131.5 20.8 %copy-start.31 = (f32[48,128]{1,0:T(8,128)S(1)}, f32[48,128]{1,0:T(8,128)}, u32[]{:S(2)}) copy-start(f32[48,128]{1,0:T(8,128)} %get-tuple-element.163) | copy-start | bytes 73732
  131.6 27.7 %all-to-all-start.5 = ((bf16[4,624,384]{2,1,0:T(8,128)(2,1)}), bf16[4,624,384]{2,1,0:T(8,128)(2,1)S(1)}, u32[]{:S(2)}, u32[]{:S(2)}) async-start(bf16[4,624,384]{2,1,0:T(8,128)(2,1)} %copy-done.4), calls=%async_computation.5 | async-start | bytes 3833856 | tf_op jit(solution)/shard_map/all_to_all | solution.py:1046
  135.2 9.0 %collective-permute-start.26 = (bf16[360,256]{1,0:T(8,128)(2,1)S(1)}, bf16[360,256]{1,0:T(8,128)(2,1)}, u32[]{:S(2)}, u32[]{:S(2)}) collective-permute-start(bf16[360,256]{1,0:T(8,128)(2,1)S(1)} %plane_join.3.refs_0_), channel_id=1, source_target_pairs={{0,8},{2,10},{4,12},{6,14},{8,0},{10,2},{12,4},{14,6},{16,24},{18,... | collective-permute-start | bytes 552968 | tf_op jit(solution)/shard_map/ppermute | solution.py:1042
  135.3 16.5 %collective-permute-start.27 = (bf16[360,256]{1,0:T(8,128)(2,1)S(1)}, bf16[360,256]{1,0:T(8,128)(2,1)}, u32[]{:S(2)}, u32[]{:S(2)}) collective-permute-start(bf16[360,256]{1,0:T(8,128)(2,1)S(1)} %plane_join.3.refs_0_), channel_id=1, source_target_pairs={{0,16},{2,18},{4,20},{6,22},{8,24},{10,26},{12,28},{14,30},{16,0},... | collective-permute-start | bytes 552968 | tf_op jit(solution)/shard_map/ppermute | solution.py:1042
  137.2 14.6 %collective-permute-start.28 = (bf16[360,256]{1,0:T(8,128)(2,1)S(1)}, bf16[360,256]{1,0:T(8,128)(2,1)}, u32[]{:S(2)}, u32[]{:S(2)}) collective-permute-start(bf16[360,256]{1,0:T(8,128)(2,1)S(1)} %plane_join.3.refs_0_), channel_id=1, source_target_pairs={{0,24},{2,26},{4,28},{6,30},{8,16},{10,18},{12,20},{14,22},{16,8},... | collective-permute-start | bytes 552968 | tf_op jit(solution)/shard_map/ppermute | solution.py:1042
  139.6 12.8 %collective-permute-start.29 = (bf16[360,256]{1,0:T(8,128)(2,1)S(1)}, bf16[360,256]{1,0:T(8,128)(2,1)S(1)}, u32[]{:S(2)}, u32[]{:S(2)}) collective-permute-start(bf16[360,256]{1,0:T(8,128)(2,1)S(1)} %plane_join.3.refs_0_), channel_id=1, source_target_pairs={{0,1},{1,0},{2,3},{3,2},{4,5},{5,4},{6,7},{7,6},{8,9},{9,8},{10,11... | collective-permute-start | bytes 552968 | tf_op jit(solution)/shard_map/ppermute | solution.py:1037
  144.2 9.3 %collective-permute-start.30 = (bf16[360,256]{1,0:T(8,128)(2,1)}, bf16[360,256]{1,0:T(8,128)(2,1)}, u32[]{:S(2)}, u32[]{:S(2)}) collective-permute-start(bf16[360,256]{1,0:T(8,128)(2,1)} %collective-permute-done.26.refs_1_), channel_id=1, source_target_pairs={{0,1},{1,0},{2,3},{3,2},{4,5},{5,4},{6,7},{7,6},{8,9},{9,8},{10,11... | collective-permute-start | bytes 552968 | tf_op jit(solution)/shard_map/ppermute | solution.py:1037
  151.8 1.8 %collective-permute-start.31 = (bf16[360,256]{1,0:T(8,128)(2,1)}, bf16[360,256]{1,0:T(8,128)(2,1)}, u32[]{:S(2)}, u32[]{:S(2)}) collective-permute-start(bf16[360,256]{1,0:T(8,128)(2,1)} %collective-permute-done.27.refs_2_), channel_id=1, source_target_pairs={{0,1},{1,0},{2,3},{3,2},{4,5},{5,4},{6,7},{7,6},{8,9},{9,8},{10,11... | collective-permute-start | bytes 552968 | tf_op jit(solution)/shard_map/ppermute | solution.py:1037
  151.8 2.0 %collective-permute-start.32 = (bf16[360,256]{1,0:T(8,128)(2,1)}, bf16[360,256]{1,0:T(8,128)(2,1)}, u32[]{:S(2)}, u32[]{:S(2)}) collective-permute-start(bf16[360,256]{1,0:T(8,128)(2,1)} %collective-permute-done.28.refs_3_), channel_id=1, source_target_pairs={{0,1},{1,0},{2,3},{3,2},{4,5},{5,4},{6,7},{7,6},{8,9},{9,8},{10,11... | collective-permute-start | bytes 552968 | tf_op jit(solution)/shard_map/ppermute | solution.py:1037
  152.3 7.3 %collective-permute-start.34 = (f32[48,128]{1,0:T(8,128)S(1)}, f32[48,128]{1,0:T(8,128)S(1)}, u32[]{:S(2)}, u32[]{:S(2)}) collective-permute-start(f32[48,128]{1,0:T(8,128)S(1)} %copy-done.31), channel_id=1, source_target_pairs={{0,1},{1,0},{2,3},{3,2},{4,5},{5,4},{6,7},{7,6},{8,9},{9,8},{10,11... | collective-permute-start | bytes 73736 | tf_op jit(solution)/shard_map/ppermute | solution.py:1037
  153.1 7.2 %collective-permute-start.33 = (bf16[128,768]{1,0:T(8,128)(2,1)S(1)}, bf16[128,768]{1,0:T(8,128)(2,1)S(1)}, u32[]{:S(2)}, u32[]{:S(2)}) collective-permute-start(bf16[128,768]{1,0:T(8,128)(2,1)S(1)} %mixer_back.1.half_ref), channel_id=1, source_target_pairs={{0,1},{1,0},{2,3},{3,2},{4,5},{5,4},{6,7},{7,6},{8,9},{9,8},{10,11... | collective-permute-start | bytes 589832 | tf_op jit(solution)/shard_map/ppermute | solution.py:1037
  159.3 3.9 %collective-permute-start.35 = (bf16[4,48,384]{2,1,0:T(8,128)(2,1)S(1)}, bf16[4,48,384]{2,1,0:T(8,128)(2,1)S(1)}, u32[]{:S(2)}, u32[]{:S(2)}) collective-permute-start(bf16[4,48,384]{2,1,0:T(8,128)(2,1)S(1)} %slice.35.mine_ref), channel_id=1, source_target_pairs={{0,1},{1,0},{2,3},{3,2},{4,5},{5,4},{6,7},{7,6},{8,9},{9,8},{10,11... | collective-permute-start | bytes 442376 | tf_op jit(solution)/shard_map/ppermute | solution.py:1037
  (12 other events, 12.0 us)

commit v3 on v2

--- a/solution.py
+++ b/solution.py
@@ -17,6 +17,7 @@
 GROUP = 8
 FILTER_LANES = 2048
 SMALL_ROWS = 72
+BACK_MIB = 24
 BF = jnp.bfloat16
 F32 = jnp.float32
 
@@ -335,7 +336,7 @@
 
 
 def conv_backward_kernel(padded, seqs, real, g_ref, sm_ref, p_ref, y_ref, saved_ref, taps_ref, h_ref, fh, fl, tw, sh, sl, ih, il, bh, bl,
-                         pg_ref, cross_ref, st_ref, icg_ref):
+                         pg_ref, cross_ref, st_ref, sent_ref, icg_ref):
     count, chans, _ = g_ref.shape
     gated = g_ref[...].astype(F32)
     conv_grad = gated * sm_ref[:, 2 * chans :, :]
@@ -348,9 +349,18 @@
     per_seq = count // seqs
     taps = tap_columns(taps_ref, real)
     lane = lax.broadcasted_iota(jnp.int32, (3 * chans, LANES), 1)
+    first_lanes = lane[:GROUP]
+
+    def edge_of(back):
+        out = jnp.zeros((GROUP, LANES), F32)
+        for a in range(chans // GROUP):
+            rows = back[a * GROUP : (a + 1) * GROUP]
+            rows = pltpu.roll(rows, 2 * a, 1) if a else rows
+            out = jnp.where((first_lanes >= 2 * a) & (first_lanes < 2 * a + 2), rows, out)
+        return out
 
     def step(i, carry):
-        next1, next2, acc0, acc1, acc2 = carry
+        next1, next2, acc0, acc1, acc2, next_edge = carry
         n = count - 1 - i
         keep = jnp.where(lax.rem(n + 1, per_seq) == 0, 0.0, 1.0)
         sm = sm_ref[n]
@@ -363,11 +373,12 @@
         s1 = jnp.where(lane < LANES - 1, r1, next1 * keep)
         s2 = jnp.where(lane < LANES - 2, r2, next2 * keep)
         pg_ref[n] = (taps[0] * sg + taps[1] * s1 + taps[2] * s2).astype(BF)
+        sent_ref[n] = jnp.concatenate([back, next_edge * keep], axis=0).astype(BF)
         p = p_ref[n]
-        return r1, r2, acc0 + sg * p, acc1 + s1 * p, acc2 + s2 * p
+        return r1, r2, acc0 + sg * p, acc1 + s1 * p, acc2 + s2 * p, edge_of(back)
 
     zero = jnp.zeros((3 * chans, LANES), F32)
-    _, _, acc0, acc1, acc2 = lax.fori_loop(0, count, step, (zero,) * 5, unroll=4)
+    _, _, acc0, acc1, acc2, _ = lax.fori_loop(0, count, step, (zero,) * 5 + (zero[:GROUP],), unroll=4)
     out = zero
     for k, acc in enumerate((acc0, acc1, acc2)):
         out = jnp.where(lane == k, jnp.sum(acc, axis=1, keepdims=True), out)
@@ -413,11 +424,12 @@
     return pl.pallas_call(
         functools.partial(conv_backward_kernel, padded, seqs, real),
         in_specs=vmem_specs(16),
-        out_specs=vmem_specs(3),
+        out_specs=vmem_specs(4),
         out_shape=[
             jax.ShapeDtypeStruct((count, 3 * chans, LANES), BF),
             jax.ShapeDtypeStruct((chans * padded, 2 * LANES), F32),
             jax.ShapeDtypeStruct((3 * chans, LANES), F32),
+            jax.ShapeDtypeStruct((count, chans + GROUP, LANES), BF),
         ],
         scratch_shapes=[pltpu.VMEM(gated.shape, F32)],
         compiler_params=params(),
@@ -605,7 +617,8 @@
     return ref[pl.ds(pl.multiple_of(lax.axis_index("tp") * rows, rows), rows), :]
 
 
-def mixer_in_kernel(per_plane, seq_length, x_ref, halo_ref, gain_ref, w_ref, taps_ref, og_ref, conv_ref, sm2_ref, z0, z1, z2, z3, keep_ref):
+def mixer_in_kernel(per_plane, seq_length, x_ref, halo_ref, gain_ref, w_ref, taps_ref, og_ref, conv_ref, sm2_ref, proj_ref, start_ref,
+                    z0, z1, z2, z3, keep_ref):
     rows = sm2_ref.shape[0]
     width = w_ref.shape[1]
     blocks = w_ref.shape[2] // width
@@ -623,15 +636,20 @@
         proj = jnp.concatenate(
             [mm(n1[:, column(j, width)], w_ref[p, :, column(j, width)]) for j in range(blocks)], axis=1
         )
-        proj = proj.astype(BF).astype(F32)
+        low = proj.astype(BF)
+        if p < 2:
+            proj_ref[p] = low
+        proj = low.astype(F32)
         mixed.append(
-            taps_ref[0, p : p + 1, :] * proj[lead:]
+            taps_ref[0, p : p + 1, :] * proj[lead : lead + rows]
             + taps_ref[1, p : p + 1, :] * proj[lead - 1 : lead - 1 + rows]
             + taps_ref[2, p : p + 1, :] * proj[lead - 2 : lead - 2 + rows]
         )
     sm2_ref[...] = mixed[2]
+    start_ref[:8, :] = mixed[0][:8]
+    start_ref[8:, :] = mixed[1][:8]
     conv_ref[...] = (mixed[0] * mixed[1]).T.astype(BF)
-    nt = normed[lead:].T.astype(BF)
+    nt = normed[lead : lead + rows].T.astype(BF)
     ot = og_ref[...].astype(F32).T.astype(BF)
     for j in range(blocks):
         keep_ref[j, :width, :] = nt[column(j, width)]
@@ -647,8 +665,13 @@
     return pl.pallas_call(
         functools.partial(mixer_in_kernel, per_plane, seq_length),
         in_specs=vmem_specs(6),
-        out_specs=vmem_specs(6),
-        out_shape=[jax.ShapeDtypeStruct((model, rows), BF), jax.ShapeDtypeStruct((rows, model), F32)]
+        out_specs=vmem_specs(8),
+        out_shape=[
+            jax.ShapeDtypeStruct((model, rows), BF),
+            jax.ShapeDtypeStruct((rows, model), F32),
+            jax.ShapeDtypeStruct((2, rows + halo.shape[0], model), BF),
+            jax.ShapeDtypeStruct((16, model), F32),
+        ]
         + [jax.ShapeDtypeStruct((2 * width, rows), BF)] * 4,
         scratch_shapes=[pltpu.VMEM((model // width, 2 * width, rows), BF)],
         compiler_params=params(24),
@@ -677,8 +700,8 @@
     return down, back
 
 
-def middle_kernel(per_plane, conv_ref, sm2_ref, x_ref, og_ref, gain_ref, wo_ref, ga_ref, gb_ref, da_ref, db_ref,
-                  gg_ref, mid_ref, out_ref, wo_own, wo_other, gain_out, z0, z1, z2, z3, keep_ref):
+def middle_kernel(per_plane, conv_ref, sm2_ref, start_ref, x_ref, og_ref, gain_ref, wo_ref, ga_ref, gb_ref, da_ref, db_ref,
+                  gg_ref, mid_ref, out_ref, wo_own, wo_other, gain_out, third_ref, edge_ref, z0, z1, z2, z3, keep_ref):
     width = wo_ref.shape[0]
     blocks = wo_ref.shape[1] // width
     conv = conv_ref[...].astype(F32).T
@@ -712,6 +735,10 @@
         [mm_nt(bg[:, column(j, width)], wo_ref[:, column(j, width)]) for j in range(blocks)], axis=1
     )
     gg_ref[...] = gated_grad.T.astype(BF)
+    third = gated_grad * conv
+    third_ref[...] = third
+    edge_ref[:8, :] = third[:8]
+    edge_ref[8:, :] = start_ref[...]
     gain_out[...] = jnp.sum(n2_grad * xhat, axis=0, keepdims=True).reshape(-1)
     weight = jnp.concatenate(
         [mm_tn(gated_low[:, column(j, width)], bg[:, column(j, width)]) for j in range(blocks)], axis=1
@@ -728,13 +755,13 @@
         out[...] = keep_ref[lax.bitwise_xor(plane, d)]
 
 
-def middle_part(conv, sm2, x, og, gain, wo, ga, gb, da, db, per_plane):
+def middle_part(conv, sm2, start, x, og, gain, wo, ga, gb, da, db, per_plane):
     rows, model = og.shape
     width = wo.shape[0]
     return pl.pallas_call(
         functools.partial(middle_kernel, per_plane),
-        in_specs=vmem_specs(10),
-        out_specs=vmem_specs(10),
+        in_specs=vmem_specs(11),
+        out_specs=vmem_specs(12),
         out_shape=[
             jax.ShapeDtypeStruct((model, rows), BF),
             jax.ShapeDtypeStruct((rows, model), F32),
@@ -742,13 +769,15 @@
             jax.ShapeDtypeStruct((width, model // 2), BF),
             jax.ShapeDtypeStruct((width, model // 2), BF),
             jax.ShapeDtypeStruct((model,), F32),
+            jax.ShapeDtypeStruct((rows, model), F32),
+            jax.ShapeDtypeStruct((24, model), F32),
         ]
         + [jax.ShapeDtypeStruct((width, rows), BF)] * 4,
         scratch_shapes=[pltpu.VMEM((model // width, width, rows), BF)],
         compiler_params=params(),
         cost_estimate=cost(9 * 10**9, 6 * 10**6),
         name="middle_part",
-    )(conv, sm2, x, og, gain, wo, ga, gb, da, db)
+    )(conv, sm2, start, x, og, gain, wo, ga, gb, da, db)
 
 
 def glu_grad_kernel(per_plane, za, zb, zc, zd, oa, ob, oc, od, ga_ref, gb_ref, da_ref, db_ref, own_ref, other_ref):
@@ -853,7 +882,7 @@
         out_specs=vmem_specs(1)[0],
         out_shape=jax.ShapeDtypeStruct(parts.shape[1:], BF),
         compiler_params=params(8),
-        cost_estimate=cost(10**8, 2 * 10**6),
+        cost_estimate=cost(8 * 10**11, 2 * 10**6),
         name="plane_sum",
     )(parts)
 
@@ -987,41 +1016,66 @@
     )(w, gain, *tiles)
 
 
-def mixer_back_kernel(by_source, pg_ref, mid_ref, x_ref, gain_ref, w_ref, in_ref):
+def short_mix(proj_ref, taps_ref, p, rows):
+    lead = proj_ref.shape[1] - rows
+    proj = proj_ref[p].astype(F32)
+    return (
+        taps_ref[0, p : p + 1, :] * proj[lead:]
+        + taps_ref[1, p : p + 1, :] * proj[lead - 1 : lead - 1 + rows]
+        + taps_ref[2, p : p + 1, :] * proj[lead - 2 : lead - 2 + rows]
+    )
+
+
+def mixer_back_kernel(chans, seq_length, *refs):
+    *grad_refs, third_ref, edge_ref, proj_ref, taps_ref, mid_ref, x_ref, gain_ref, w_ref, in_ref = refs
     rows, model = mid_ref.shape
     width = w_ref.shape[1]
     blocks = model // width
-    if by_source:
-        pg = pg_ref[...].astype(F32)
-        count, rows3, _ = pg.shape
-        chans = rows3 // 3
-        parts = [
-            pg[:, p * chans : (p + 1) * chans, :].reshape(count * chans, rows).astype(BF) for p in range(3)
-        ]
+    if len(grad_refs) == 1:
+        got = grad_refs[0][...].astype(F32)
+        count = got.shape[0]
+        main = got[:, :chans, :].reshape(count * chans, rows)
+        tiles = []
+        for k in range(count):
+            tile = got[k, chans:, :]
+            for a in range(chans // GROUP):
+                tiles.append(pltpu.roll(tile, LANES - 2 * a, 1) if a else tile)
+        tail = jnp.concatenate(tiles, axis=0)
     else:
-        parts = [pg_ref[p] for p in range(3)]
-    grads = []
-    for j in range(blocks):
-        total = None
-        for p in range(3):
-            part = mm(w_ref[p, :, column(j, width)], parts[p][column(j, width)])
-            total = part if total is None else total + part
-        grads.append(total)
-    n1_grad = jnp.concatenate(grads, axis=0).T
+        main, tail = grad_refs[0][...].astype(F32), grad_refs[1][...].astype(F32)
+    back = jnp.concatenate([main.T, tail.T[:8]], axis=0)
+    linear = lax.axis_index("seq") * 2 + lax.axis_index("tp")
+    keep = jnp.where(lax.rem((linear + 1) * rows, seq_length) == 0, 0.0, 1.0)
+    third = jnp.concatenate([third_ref[...], edge_ref[:8, :] * keep], axis=0)
+    mixed = [
+        jnp.concatenate([short_mix(proj_ref, taps_ref, p, rows), edge_ref[8 * p + 8 : 8 * p + 16, :]], axis=0)
+        for p in range(2)
+    ]
+    total = [None] * blocks
+    for p, sg in enumerate((back * mixed[1], back * mixed[0], third)):
+        pg = (
+            taps_ref[0, p : p + 1, :] * sg[:rows]
+            + taps_ref[1, p : p + 1, :] * sg[1 : rows + 1]
+            + taps_ref[2, p : p + 1, :] * sg[2 : rows + 2]
+        ).astype(BF)
+        for j in range(blocks):
+            part = mm_nt(pg[:, column(j, width)], w_ref[p, :, column(j, width)])
+            total[j] = part if total[j] is None else total[j] + part
+    n1_grad = jnp.concatenate(total, axis=1)
     xhat, r = norm_stats(own_part(x_ref, rows).astype(F32))
     in_ref[...] = (mid_ref[...] + norm_backward(n1_grad, gain_ref[...].reshape(1, -1), xhat, r)).astype(BF)
 
 
-def mixer_back(pg, mid, x, gain, w, by_source):
-    return pl.pallas_call(
-        functools.partial(mixer_back_kernel, by_source),
-        in_specs=vmem_specs(5),
+def mixer_back(grads, third, edge, proj, taps, mid, x, gain, w, chans, seq_length):
+    return pl.pallas_call(
+        functools.partial(mixer_back_kernel, chans, seq_length),
+        in_specs=vmem_specs(8 + len(grads)),
         out_specs=vmem_specs(1)[0],
         out_shape=jax.ShapeDtypeStruct(mid.shape, BF),
-        compiler_params=params(16),
+        compiler_params=params(BACK_MIB),
         cost_estimate=cost(3 * 10**9, 4 * 10**6),
         name="mixer_back",
-    )(pg, mid, x, gain, w)
+    )(*grads, third, edge, proj, taps, mid, x, gain, w)
 
 
 def after(x, *others):
@@ -1099,7 +1153,7 @@
     lag_back = swapped(lag_other)
 
     w_in = in_proj.transpose(1, 0, 2)
-    conv_rows, sm2, *sent = mixer_in(
+    conv_rows, sm2, proj_rows, start_rows, *sent = mixer_in(
         layer_input, after(halo, lag_own), mixer_gain, w_in, short_taps, out_grad, per_plane, seq_length
     )
 
@@ -1128,14 +1182,15 @@
     else:
         plane_tiles = [gathered_over(rows_in, per_plane, within).reshape(per_plane * blocks, width, rows)]
         turns = [[(0, r) for r in range(per_plane)]]
-    gated_grad, mid, layer_output, extra, extra_other, gain_sum, *sent = middle_part(
-        conv_tokens, sm2, layer_input, out_grad, glu_gain, out_proj, glu_own, glu_other,
+    gated_grad, mid, layer_output, extra, extra_other, gain_sum, third, edge, *sent = middle_part(
+        conv_tokens, sm2, start_rows, layer_input, out_grad, glu_gain, out_proj, glu_own, glu_other,
         down_own, down_other, per_plane
     )
     gated_channels = to_channels(gated_grad)
     across = lambda parts: [parts[0]] + [crossed(parts[d], d * per_plane) for d in range(1, blocks)]
     late = across(sent)
     extra_back = swapped(extra_other)
+    edge = permuted(edge, both, devices, -1)
     plane_tiles = [after(x, gated_grad) for x in plane_tiles]
     tiles = plane_tiles + [swapped(x) for x in plane_tiles]
     turns = turns + [[(1, r) for _, r in t] for t in turns]
@@ -1146,18 +1201,15 @@
     g_own, g_other = glu_grads(late, early, glu_own, glu_other, down_own, down_other, per_plane)
     g_back = swapped(g_other)
     if quick:
-        sums = exchanged(plane_add(g_own, g_back, extra, extra_back, per_plane), "seq", within)
-
-    pg, cross, tap_sums = conv_backward(
+        to_sum = plane_add(g_own, g_back, extra, extra_back, per_plane)
+        sums = exchanged(to_sum, "seq", within)
+        gated_channels = after(gated_channels, to_sum)
+
+    pg, cross, tap_sums, icg = conv_backward(
         after(gated_channels, g_own), mixed_channels, proj_channels, conv_out, signal_spec, short_taps, spectrum, tables,
         seqs, chans
     )
-    pg_sent = pg.reshape(devices, 3, chans_padded, rows)[:, :, :chans].reshape(devices, 3 * chans, rows)
-    if quick:
-        pg_sent = after(pg_sent, sums)
-    pg_tokens = exchanged(pg_sent, both)
-    if chans != chans_padded:
-        pg_tokens = pg_tokens.reshape(devices, 3, chans, rows).transpose(1, 0, 2, 3).reshape(3, model, rows)
+    icg_tokens = exchanged(after(icg, sums) if quick else icg, both)
 
     if quick:
         glu_piece = plane_sum(after(sums, pg))
@@ -1171,8 +1223,17 @@
     if quick:
         in_parts = [in_piece] + [crossed(in_piece, d) for d in range(1, per_plane)]
         glu_parts = plane_join([after(x, in_piece) for x in glu_parts], 3 * width // per_plane, (per_plane,))
-        pg_tokens = after(pg_tokens, glu_parts)
-    input_half = mixer_back(pg_tokens, mid, layer_input, mixer_gain, w_in, chans == chans_padded)
+        icg_tokens = after(icg_tokens, glu_parts)
+    if chans == chans_padded:
+        grads = [icg_tokens]
+    else:
+        grads = [
+            icg_tokens[:, :chans].reshape(model, rows),
+            icg_tokens[:, chans_padded : chans_padded + chans].reshape(model, rows),
+        ]
+    input_half = mixer_back(
+        grads, third, edge, proj_rows, short_taps, mid, layer_input, mixer_gain, w_in, chans, seq_length
+    )
     input_other = swapped(input_half)
 
     if quick:

time: 165 us -> 162 us (0.982)
  waiting for transfers between devices: 28.7 us -> 21.6 us
  starting transfers between devices: 57.9 us -> 61 us
    ppermute x18, waiting for transfers between devices: 22.3 us -> 15.2 us  [crossed(): return lax.ppermute(x, 'seq', [(i, i ^ mask) for i in range(devices)])]
    ppermute x1 -> x2, starting transfers between devices: 4.83 us -> 6.11 us  [permuted(): return lax.ppermute(x, axes, pairs)]
    unnamed x68 -> x78, local copies, waits for them, and re-layouts: 7.09 us -> 7.1 us
  transfers between devices with their start and end apart: 42 -> 43, of which waited for: 10 -> 11; matrix products, arithmetic and copies ran while one was open for 2% -> 2% of each run, Pallas kernels for 35% -> 36%
where the time goes in v3:
time: 162 us; the launch traced here: 161 us
  Pallas kernels  66.1 us (41%)
  starting transfers between devices  61 us (38%)
  waiting for transfers between devices  21.6 us (13%)
  local copies, waits for them, and re-layouts  9.78 us (6%)
    ppermute x18, starting transfers between devices, crossed(): return lax.ppermute(x, 'seq', [(i, i ^ mask) for i in range(devices)])  26.8 us
    all_to_all x6, starting transfers between devices, exchanged(): return lax.all_to_all(x, axes, 0, 0, axis_index_groups=groups, tiled=True)  24.9 us
    ppermute x18, waiting for transfers between devices, crossed(): return lax.ppermute(x, 'seq', [(i, i ^ mask) for i in range(devices)])  15.2 us
    pallas_call x1, Pallas kernels, channel_grads(): pl.pallas_call(functools.partial(channel_grads_kernel, place, turns, tabl...  10.9 us
    pallas_call x1, Pallas kernels, filter_forward(): pl.pallas_call(filter_forward_kernel, in_specs=vmem_specs(6), out_specs=v...  8.42 us
    pallas_call x1, Pallas kernels, conv_backward(): pl.pallas_call(functools.partial(conv_backward_kernel, padded, seqs, real...  8.07 us
    pallas_call x1, Pallas kernels, middle_part(): pl.pallas_call(functools.partial(middle_kernel, per_plane), in_specs=vmem...  7.97 us
    unnamed x78, local copies, waits for them, and re-layouts  7.1 us
  transfers between devices with their start and end apart: 43, of which 11 were waited for; matrix products, arithmetic and copies ran while one was open for 2% of the time, Pallas kernels for 36%

profile of v3, /device:TPU:0, one launch (start us, length us, event | category | flops | bytes accessed | tf_op | source)
XLA Modules:
  0.0 161.0 jit_solution(10423145433683645465)
XLA Ops:
  0.7 0.8 slice.30
  1.5 4.8 %collective-permute-start = (bf16[16,768]{1,0:T(8,128)(2,1)S(1)}, bf16[16,768]{1,0:T(8,128)(2,1)S(1)}, u32[]{:S(2)}, u32[]{:S(2)}) collective-permute-start(bf16[16,768]{1,0:T(8,128)(2,1)S(1)} %slice.30), channel_id=1, source_target_pairs={{0,2},{2,4},{4,6},{6,8},{8,10},{10,12},{12,14},{14,16},{16,18},{18... | collective-permute-start | bytes 73736 | tf_op jit(solution)/shard_map/ppermute | solution.py:1087
  6.4 8.4 %filter_forward.1 = (f32[24,4096]{1,0:T(8,128)}, f32[24,4096]{1,0:T(8,128)}, bf16[128,4096]{1,0:T(8,128)(2,1)}, bf16[128,4096]{1,0:T(8,128)(2,1)}, bf16[128,4096]{1,0:T(8,128)(2,1)}, /*index=5*/bf16[128,4096]{1,0:T(8,128)(2,1)}) custom-call(bf16[48,8192]{1,0:T(8,128)(2,1)} %constant.34.clone.feat_ref, f32[5,128]{1,0:T(8,128)} %w1_ref.1, f32[128]{0:T(128)} %b1_ref.1, ...), custom_call_target="tpu_custom_call" | custom-call | flops 400000000 | bytes 400000 | tf_op jit(solution)/shard_map/filter_forward/pallas_call | solution.py:225
  14.9 1.9 %mixer_in.1 = (bf16[768,128]{1,0:T(8,128)(2,1)}, f32[128,768]{1,0:T(8,128)S(1)}, bf16[2,144,768]{2,1,0:T(8,128)(2,1)S(1)}, f32[16,768]{1,0:T(8,128)S(1)}, bf16[3...) custom-call(bf16[256,768]{1,0:T(8,128)(2,1)S(1)} %copy-done.7, ...), custom_call_target="tpu_custom_call" | custom-call | flops 200000000 | bytes 200000 | tf_op jit(solution)/shard_map/mixer_in/pallas_call | solution.py:665
  17.0 0.6 copy-done.16
  17.7 0.4 copy-done.36
  18.2 5.1 %all-to-all-start = ((bf16[32,24,128]{2,1,0:T(8,128)(2,1)}), bf16[32,24,128]{2,1,0:T(8,128)(2,1)}, u32[]{:S(2)}, u32[]{:S(2)}) async-start(bf16[32,24,128]{2,1,0:T(8,128)(2,1)} %bitcast.2), calls=%async_computation | async-start | bytes 393216 | tf_op jit(solution)/shard_map/all_to_all | solution.py:1100
  23.3 1.8 %collective-permute-start.4 = (bf16[384,128]{1,0:T(8,128)(2,1)}, bf16[384,128]{1,0:T(8,128)(2,1)}, u32[]{:S(2)}, u32[]{:S(2)}) collective-permute-start(bf16[384,128]{1,0:T(8,128)(2,1)} %get-tuple-element.111), channel_id=1, source_target_pairs={{0,8},{2,10},{4,12},{6,14},{8,0},{10,2},{12,4},{14,6},{16,24},{18,... | collective-permute-start | bytes 294920 | tf_op jit(solution)/shard_map/ppermute | solution.py:1096
  25.0 2.4 %collective-permute-start.5 = (bf16[384,128]{1,0:T(8,128)(2,1)}, bf16[384,128]{1,0:T(8,128)(2,1)}, u32[]{:S(2)}, u32[]{:S(2)}) collective-permute-start(bf16[384,128]{1,0:T(8,128)(2,1)} %get-tuple-element.113), channel_id=1, source_target_pairs={{0,16},{2,18},{4,20},{6,22},{8,24},{10,26},{12,28},{14,30},{16,0},... | collective-permute-start | bytes 294920 | tf_op jit(solution)/shard_map/ppermute | solution.py:1096
  27.7 4.3 %filter_spectrum.1.h_ref = f32[960,256]{1,0:T(8,128)} custom-call(f32[24,4096]{1,0:T(8,128)} %get-tuple-element.100.own_ref, f32[24,4096]{1,0:T(8,128)} %collective-permute-done.1.other_ref, bf16[640,512]{1,0:T(8,128)(2,1)} %constant.35.clone.fh, bf16[640,512]{1,0:T(8,128)(2,1)} %constant.36.clone.fl, f32[4,40,128]{2,1,0:T(8,128)} %constant.37.clone.tw, ...), custom_call_target="tpu_custom_call" | custom-call | flops 200000000 | bytes 200000 | tf_op jit(solution)/shard_map/filter_spectrum/pallas_call | solution.py:390
  32.0 0.6 all-to-all-done.x_ref
  32.6 5.0 %conv_forward.1 = (bf16[32,24,128]{2,1,0:T(8,128)(2,1)}, f32[960,256]{1,0:T(8,128)}) custom-call(bf16[32,24,128]{2,1,0:T(8,128)(2,1)} %all-to-all-done.x_ref, f32[960,256]{1,0:T(8,128)} %filter_spectrum.1.h_ref, bf16[640,256]{1,0:T(8,128)(2,1)} %constant.40.clone.fh, bf16[640,256]{1,0:T(8,128)(2,1)} %constant.41.clone.fl, f32[4,40,128]{2,1,0:T(8,128)} %constant.37.clone.tw, ...), custom_call_target="tpu_custom_call" | custom-call | flops 250000000 | bytes 300000 | tf_op jit(solution)/shard_map/conv_forward/pallas_call | solution.py:407
  37.6 5.6 %all-to-all-start.1 = ((bf16[32,24,128]{2,1,0:T(8,128)(2,1)}), bf16[32,24,128]{2,1,0:T(8,128)(2,1)}, u32[]{:S(2)}, u32[]{:S(2)}) async-start(bf16[32,24,128]{2,1,0:T(8,128)(2,1)} %get-tuple-element.103.y_ref), calls=%async_computation.1 | async-start | bytes 393216 | tf_op jit(solution)/shard_map/all_to_all | solution.py:1100
  43.2 0.8 slice_bitcast_fusion.2
  44.0 0.8 slice_bitcast_fusion
  44.9 0.7 pad_maximum_fusion.refs_0_
  45.6 2.4 %collective-permute-start.9 = (bf16[4,192,128]{2,1,0:T(8,128)(2,1)}, bf16[4,192,128]{2,1,0:T(8,128)(2,1)}, u32[]{:S(2)}, u32[]{:S(2)}) collective-permute-start(bf16[4,192,128]{2,1,0:T(8,128)(2,1)} %pad_maximum_fusion.refs_0_), channel_id=1, source_target_pairs={{0,6},{2,4},{4,2},{6,0},{8,14},{10,12},{12,10},{14,8},{16,22},{18,... | collective-permute-start | bytes 589832 | tf_op jit(solution)/shard_map/ppermute | solution.py:1096
  48.0 0.6 collective-permute-start.8
  48.6 0.5 collective-permute-start.7
  49.1 2.9 %all-to-all-done.1 = bf16[32,24,128]{2,1,0:T(8,128)(2,1)} async-done(((bf16[32,24,128]{2,1,0:T(8,128)(2,1)}), bf16[32,24,128]{2,1,0:T(8,128)(2,1)}, u32[]{:S(2)}, u32[]{:S(2)}) %all-to-all-start.1) | async-done | bytes 196640 | tf_op jit(solution)/shard_map/all_to_all | solution.py:1100
  52.0 1.0 copy-done.5
  53.0 8.0 %middle_part.1 = (bf16[768,128]{1,0:T(8,128)(2,1)}, f32[128,768]{1,0:T(8,128)}, bf16[128,768]{1,0:T(8,128)(2,1)}, bf16[192,384]{1,0:T(8,128)(2,1)}, bf16[192,384...) custom-call(bf16[768,128]{1,0:T(8,128)(2,1)} %bitcast.4.conv_ref, ...), custom_call_target="tpu_custom_call" | custom-call | flops 450000000 | bytes 300000 | tf_op jit(solution)/shard_map/middle_part/pallas_call | solution.py:761
  61.0 2.9 %all-to-all-start.2 = ((bf16[32,24,128]{2,1,0:T(8,128)(2,1)}), bf16[32,24,128]{2,1,0:T(8,128)(2,1)S(1)}, u32[]{:S(2)}, u32[]{:S(2)}) async-start(bf16[32,24,128]{2,1,0:T(8,128)(2,1)} %bitcast.26), calls=%async_computation.2 | async-start | bytes 393216 | tf_op jit(solution)/shard_map/all_to_all | solution.py:1100
  63.9 0.3 collective-permute-start.13
  64.5 0.3 collective-permute-start.11
  65.0 3.6 %collective-permute-start.16 = (bf16[192,128]{1,0:T(8,128)(2,1)}, bf16[192,128]{1,0:T(8,128)(2,1)S(1)}, u32[]{:S(2)}, u32[]{:S(2)}) collective-permute-start(bf16[192,128]{1,0:T(8,128)(2,1)} %get-tuple-element.128), channel_id=1, source_target_pairs={{0,24},{2,26},{4,28},{6,30},{8,16},{10,18},{12,20},{14,22},{16,8},... | collective-permute-start | bytes 147464 | tf_op jit(solution)/shard_map/ppermute | solution.py:1096
  68.6 1.2 collective-permute-start.14
  69.9 4.9 %channel_mixer.1 = (f32[32,72,128]{2,1,0:T(8,128)}, f32[32,72,128]{2,1,0:T(8,128)}) custom-call(bf16[3,192,768]{2,1,0:T(8,128)(2,1)} %bitcast.19, f32[3,3,768]{2,1,0:T(4,128)} %refs_4_.1, bf16[4,192,128]{2,1,0:T(8,128)(2,1)} %pad_maximum_fusion.refs_0_, bf16[4,192,128]{2,1,0:T(8,128)(2,1)} %collective-permute-done.7.refs_1_, ...), custom_call_target="tpu_custom_call" | custom-call | flops 150000000 | bytes 300000 | tf_op jit(solution)/shard_map/channel_mixer/pallas_call | solution.py:501
  74.8 1.3 collective-permute-done.15.zc
  76.1 1.1 copy-done.12
  77.2 3.9 %glu_grads.1 = (f32[576,384]{1,0:T(8,128)S(1)}, bf16[576,384]{1,0:T(8,128)(2,1)S(1)}) custom-call(bf16[192,128]{1,0:T(8,128)(2,1)S(1)} %copy-done.28, bf16[192,128]{1,0:T(8,128)(2,1)S(1)} %collective-permute-done.14.zb, bf16[192,128]{1,0:T(8,128)(2,1)S(1)} %collective-permute-done.15.zc, bf16[192,128]{1,0:T(8,128)(2,1)S(1)} %collective-permute-done.16.zd, ...), custom_call_target="tpu_custom_call" | custom-call | flops 450000000 | bytes 200000 | tf_op jit(solution)/shard_map/glu_grads/pallas_call | solution.py:809
  81.2 0.5 collective-permute-start.18
  81.6 1.5 collective-permute-done.18.theirs_ref
  83.1 0.9 plane_add.1
  84.1 3.7 %all-to-all-start.3 = ((bf16[4,192,384]{2,1,0:T(8,128)(2,1)}), bf16[4,192,384]{2,1,0:T(8,128)(2,1)S(1)}, u32[]{:S(2)}, u32[]{:S(2)}) async-start(bf16[4,192,384]{2,1,0:T(8,128)(2,1)} %plane_add.1), calls=%async_computation.3 | async-start | bytes 1179648 | tf_op jit(solution)/shard_map/all_to_all | solution.py:1100
  87.7 8.1 %conv_backward.1 = (bf16[32,72,128]{2,1,0:T(8,128)(2,1)}, f32[960,256]{1,0:T(8,128)}, f32[72,128]{1,0:T(8,128)}, bf16[32,32,128]{2,1,0:T(8,128)(2,1)}) custom-call(bf16[32,24,128]{2,1,0:T(8,128)(2,1)} %copy-done.32, f32[32,72,128]{2,1,0:T(8,128)} %get-tuple-element.136.sm_ref, f32[32,72,128]{2,1,0:T(8,128)} %get-tuple-element.122.p_ref, ...), custom_call_target="tpu_custom_call" | custom-call | flops 350000000 | bytes 450000 | tf_op jit(solution)/shard_map/conv_backward/pallas_call | solution.py:424
  95.8 1.0 all-to-all-done.3.x_ref
  96.8 4.1 %all-to-all-start.4 = ((bf16[32,32,128]{2,1,0:T(8,128)(2,1)}), bf16[32,32,128]{2,1,0:T(8,128)(2,1)S(1)}, u32[]{:S(2)}, u32[]{:S(2)}) async-start(bf16[32,32,128]{2,1,0:T(8,128)(2,1)} %get-tuple-element.154), calls=%async_computation.4 | async-start | bytes 524288 | tf_op jit(solution)/shard_map/all_to_all | solution.py:1100
  101.0 3.5 %collective-permute-start.22 = (bf16[192,384]{1,0:T(8,128)(2,1)S(1)}, bf16[192,384]{1,0:T(8,128)(2,1)S(1)}, u32[]{:S(2)}, u32[]{:S(2)}) collective-permute-start(bf16[192,384]{1,0:T(8,128)(2,1)S(1)} %plane_sum.1.a0), channel_id=1, source_target_pairs={{0,24},{2,26},{4,28},{6,30},{8,16},{10,18},{12,20},{14,22},{16,8},... | collective-permute-start | bytes 442376 | tf_op jit(solution)/shard_map/ppermute | solution.py:1096
  104.5 1.0 collective-permute-start.20
  105.4 1.3 collective-permute-start.23
  106.8 0.9 copy-done.31
  107.7 10.9 %channel_grads.1 = (bf16[144,256]{1,0:T(8,128)(2,1)}, f32[48,128]{1,0:T(8,128)}) custom-call(bf16[32,72,128]{2,1,0:T(8,128)(2,1)} %get-tuple-element.138.pg_ref, f32[72,128]{1,0:T(8,128)} %get-tuple-element.141.st_ref, f32[960,256]{1,0:T(8,128)} %get-tuple-element.142.own_ref, f32[960,256]{1,0:T(8,128)} %copy-done.31, f32[4,40,128]{2,1,0:T(8,128)} %constant.37.clone.tw, ...), custom_call_target="tpu_custom_call" | custom-call | flops 400000000 | bytes 400000 | tf_op jit(solution)/shard_map/channel_grads/pallas_call | solution.py:572
  118.7 3.1 %collective-permute-start.26 = (bf16[144,256]{1,0:T(8,128)(2,1)}, bf16[144,256]{1,0:T(8,128)(2,1)S(1)}, u32[]{:S(2)}, u32[]{:S(2)}) collective-permute-start(bf16[144,256]{1,0:T(8,128)(2,1)} %get-tuple-element.160.a0), channel_id=1, source_target_pairs={{0,6},{2,4},{4,2},{6,0},{8,14},{10,12},{12,10},{14,8},{16,22},{18,... | collective-permute-start | bytes 221192 | tf_op jit(solution)/shard_map/ppermute | solution.py:1096
  121.8 0.6 collective-permute-start.25
  122.4 0.3 collective-permute-done.21.a2
  122.7 1.5 collective-permute-start.24
  124.3 1.2 copy-done.4
  125.7 1.3 mixer_back.1.half_ref
  127.3 3.7 %all-to-all-start.5 = ((bf16[4,624,384]{2,1,0:T(8,128)(2,1)}), bf16[4,624,384]{2,1,0:T(8,128)(2,1)S(1)}, u32[]{:S(2)}, u32[]{:S(2)}) async-start(bf16[4,624,384]{2,1,0:T(8,128)(2,1)} %copy-done.4), calls=%async_computation.5 | async-start | bytes 3833856 | tf_op jit(solution)/shard_map/all_to_all | solution.py:1100
  131.0 1.3 collective-permute-start.27
  132.3 2.6 %collective-permute-start.28 = (bf16[360,256]{1,0:T(8,128)(2,1)S(1)}, bf16[360,256]{1,0:T(8,128)(2,1)}, u32[]{:S(2)}, u32[]{:S(2)}) collective-permute-start(bf16[360,256]{1,0:T(8,128)(2,1)S(1)} %plane_join.3.refs_0_), channel_id=1, source_target_pairs={{0,16},{2,18},{4,20},{6,22},{8,24},{10,26},{12,28},{14,30},{16,0},... | collective-permute-start | bytes 552968 | tf_op jit(solution)/shard_map/ppermute | solution.py:1096
  134.9 0.5 collective-permute-start.29
  135.4 4.4 %collective-permute-done.27.refs_1_ = bf16[360,256]{1,0:T(8,128)(2,1)} collective-permute-done((bf16[360,256]{1,0:T(8,128)(2,1)S(1)}, bf16[360,256]{1,0:T(8,128)(2,1)}, u32[]{:S(2)}, u32[]{:S(2)}) %collective-permute-start.27) | collective-permute-done | bytes 184352 | tf_op jit(solution)/shard_map/ppermute | solution.py:1096
  139.7 9.0 %collective-permute-done.28.refs_2_ = bf16[360,256]{1,0:T(8,128)(2,1)} collective-permute-done((bf16[360,256]{1,0:T(8,128)(2,1)S(1)}, bf16[360,256]{1,0:T(8,128)(2,1)}, u32[]{:S(2)}, u32[]{:S(2)}) %collective-permute-start.28) | collective-permute-done | bytes 184352 | tf_op jit(solution)/shard_map/ppermute | solution.py:1096
  148.8 0.5 collective-permute-start.33
  149.3 0.7 copy-done.23
  150.0 0.4 collective-permute-start.34
  150.8 0.9 copy-done.24
  151.7 4.5 %in_unpack.1 = (f32[3,192,768]{2,1,0:T(8,128)}, f32[3,3,768]{2,1,0:T(4,128)}, f32[768]{0:T(1024)}, f32[5,128]{1,0:T(8,128)}, f32[128]{0:T(128)}, /*index=5*/f32[128,128]{1,0:T(8,128)}, f32[768]{0:T(1024)}) custom-call(bf16[3,192,768]{2,1,0:T(8,128)(2,1)S(1)} %bitcast.22, f32[768]{0:T(1024)S(1)} %copy-done.29, bf16[360,256]{1,0:T(8,128)(2,1)S(1)} %plane_join.3.refs_0_, ...), custom_call_target="tpu_custom_call" | custom-call | flops 5000000 | bytes 200000 | tf_op jit(solution)/shard_map/in_unpack/pallas_call | solution.py:999
  156.2 0.3 collective-permute-start.36
  156.6 0.6 fusion
  157.2 2.9 %finish.1 = (f32[4,192,2,384]{3,2,1,0:T(2,128)}, f32[384,768]{1,0:T(8,128)}, bf16[256,768]{1,0:T(8,128)(2,1)}) custom-call(bf16[4,624,384]{2,1,0:T(8,128)(2,1)S(1)} %all-to-all-done.5.a_ref, bf16[128,768]{1,0:T(8,128)(2,1)S(1)} %mixer_back.1.half_ref, bf16[128,768]{1,0:T(8,128)(2,1)S(1)} %collective-permute-done.34.back_ref), custom_call_target="tpu_custom_call" | custom-call | flops 5000000 | bytes 300000 | tf_op jit(solution)/shard_map/finish/pallas_call | solution.py:914
  160.1 0.9 out_unpack.1
  (125 shorter events, 2.5 us)
Async XLA Ops:
  0.6 14.2 %copy-start.7 = (bf16[256,768]{1,0:T(8,128)(2,1)S(1)}, bf16[256,768]{1,0:T(8,128)(2,1)}, u32[]{:S(2)}) copy-start(bf16[256,768]{1,0:T(8,128)(2,1)} %refs_6_.1) | copy-start | bytes 1179652
  0.7 14.2 %copy-start = (bf16[192,3,768]{2,0,1:T(8,128)(2,1)S(1)}, bf16[192,3,768]{2,0,1:T(8,128)(2,1)}, u32[]{:S(2)}) copy-start(bf16[192,3,768]{2,0,1:T(8,128)(2,1)} %param.30) | copy-start | bytes 2654212
  0.7 14.2 %copy-start.29 = (f32[768]{0:T(1024)S(1)}, f32[768]{0:T(1024)}, u32[]{:S(2)}) copy-start(f32[768]{0:T(1024)} %gain_ref.5) | copy-start | bytes 9220
  0.7 14.2 %copy-start.14 = (f32[3,3,768]{2,1,0:T(4,128)S(1)}, f32[3,3,768]{2,1,0:T(4,128)}, u32[]{:S(2)}) copy-start(f32[3,3,768]{2,1,0:T(4,128)} %refs_4_.1) | copy-start | bytes 82948
  0.7 14.2 %copy-start.13 = (bf16[128,768]{1,0:T(8,128)(2,1)S(1)}, bf16[128,768]{1,0:T(8,128)(2,1)}, u32[]{:S(2)}) copy-start(bf16[128,768]{1,0:T(8,128)(2,1)} %og_ref.3) | copy-start | bytes 589828
  1.5 13.3 %collective-permute-start = (bf16[16,768]{1,0:T(8,128)(2,1)S(1)}, bf16[16,768]{1,0:T(8,128)(2,1)S(1)}, u32[]{:S(2)}, u32[]{:S(2)}) collective-permute-start(bf16[16,768]{1,0:T(8,128)(2,1)S(1)} %slice.30), channel_id=1, source_target_pairs={{0,2},{2,4},{4,6},{6,8},{8,10},{10,12},{12,14},{14,16},{16,18},{18... | collective-permute-start | bytes 73736 | tf_op jit(solution)/shard_map/ppermute | solution.py:1087
  16.8 10.9 %copy-start.9 = (bf16[384,768]{1,0:T(8,128)(2,1)S(1)}, bf16[384,768]{1,0:T(8,128)(2,1)}, u32[]{:S(2)}) copy-start(bf16[384,768]{1,0:T(8,128)(2,1)} %da_ref.1) | copy-start | bytes 1769476
  17.7 14.3 %copy-start.2 = (bf16[4,192,2,384]{3,1,2,0:T(8,128)(2,1)}, bf16[4,192,2,384]{3,1,2,0:T(8,128)(2,1)S(1)}, u32[]{:S(2)}) copy-start(bf16[4,192,2,384]{3,1,2,0:T(8,128)(2,1)S(1)} %copy.43) | copy-start | bytes 3538948
  17.7 34.3 %collective-permute-start.2 = (bf16[4,2,192,384]{3,2,1,0:T(8,128)(2,1)S(1)}, bf16[4,2,192,384]{3,2,1,0:T(8,128)(2,1)S(1)}, u32[]{:S(2)}, u32[]{:S(2)}) collective-permute-start(bf16[4,2,192,384]{3,2,1,0:T(8,128)(2,1)S(1)} %bitcast.23), channel_id=1, source_target_pairs={{0,1},{1,0},{2,3},{3,2},{4,5},{5,4},{6,7},{7,6},{8,9},{9,8},{10,11... | collective-permute-start | bytes 3538952 | tf_op jit(solution)/shard_map/ppermute | solution.py:1091
  18.1 9.7 %collective-permute-start.1 = (f32[24,4096]{1,0:T(8,128)S(1)}, f32[24,4096]{1,0:T(8,128)}, u32[]{:S(2)}, u32[]{:S(2)}) collective-permute-start(f32[24,4096]{1,0:T(8,128)S(1)} %copy-done.36), channel_id=1, source_target_pairs={{0,1},{1,0},{2,3},{3,2},{4,5},{5,4},{6,7},{7,6},{8,9},{9,8},{10,11... | collective-permute-start | bytes 1179656 | tf_op jit(solution)/shard_map/ppermute | solution.py:1091
  18.2 14.4 %all-to-all-start = ((bf16[32,24,128]{2,1,0:T(8,128)(2,1)}), bf16[32,24,128]{2,1,0:T(8,128)(2,1)}, u32[]{:S(2)}, u32[]{:S(2)}) async-start(bf16[32,24,128]{2,1,0:T(8,128)(2,1)} %bitcast.2), calls=%async_computation | async-start | bytes 393216 | tf_op jit(solution)/shard_map/all_to_all | solution.py:1100
  23.3 19.9 %collective-permute-start.4 = (bf16[384,128]{1,0:T(8,128)(2,1)}, bf16[384,128]{1,0:T(8,128)(2,1)}, u32[]{:S(2)}, u32[]{:S(2)}) collective-permute-start(bf16[384,128]{1,0:T(8,128)(2,1)} %get-tuple-element.111), channel_id=1, source_target_pairs={{0,8},{2,10},{4,12},{6,14},{8,0},{10,2},{12,4},{14,6},{16,24},{18,... | collective-permute-start | bytes 294920 | tf_op jit(solution)/shard_map/ppermute | solution.py:1096
  25.0 19.0 %collective-permute-start.5 = (bf16[384,128]{1,0:T(8,128)(2,1)}, bf16[384,128]{1,0:T(8,128)(2,1)}, u32[]{:S(2)}, u32[]{:S(2)}) collective-permute-start(bf16[384,128]{1,0:T(8,128)(2,1)} %get-tuple-element.113), channel_id=1, source_target_pairs={{0,16},{2,18},{4,20},{6,22},{8,24},{10,26},{12,28},{14,30},{16,0},... | collective-permute-start | bytes 294920 | tf_op jit(solution)/shard_map/ppermute | solution.py:1096
  27.5 16.6 %collective-permute-start.6 = (bf16[384,128]{1,0:T(8,128)(2,1)}, bf16[384,128]{1,0:T(8,128)(2,1)}, u32[]{:S(2)}, u32[]{:S(2)}) collective-permute-start(bf16[384,128]{1,0:T(8,128)(2,1)} %get-tuple-element.115), channel_id=1, source_target_pairs={{0,24},{2,26},{4,28},{6,30},{8,16},{10,18},{12,20},{14,22},{16,8},... | collective-permute-start | bytes 294920 | tf_op jit(solution)/shard_map/ppermute | solution.py:1096
  27.7 21.3 %collective-permute-start.3 = (bf16[384,768]{1,0:T(8,128)(2,1)S(1)}, bf16[384,768]{1,0:T(8,128)(2,1)S(1)}, u32[]{:S(2)}, u32[]{:S(2)}) collective-permute-start(bf16[384,768]{1,0:T(8,128)(2,1)S(1)} %copy-done.9), channel_id=1, source_target_pairs={{0,1},{1,0},{2,3},{3,2},{4,5},{5,4},{6,7},{7,6},{8,9},{9,8},{10,11... | collective-permute-start | bytes 1769480 | tf_op jit(solution)/shard_map/ppermute | solution.py:1091
  37.6 14.4 %all-to-all-start.1 = ((bf16[32,24,128]{2,1,0:T(8,128)(2,1)}), bf16[32,24,128]{2,1,0:T(8,128)(2,1)}, u32[]{:S(2)}, u32[]{:S(2)}) async-start(bf16[32,24,128]{2,1,0:T(8,128)(2,1)} %get-tuple-element.103.y_ref), calls=%async_computation.1 | async-start | bytes 393216 | tf_op jit(solution)/shard_map/all_to_all | solution.py:1100
  45.6 18.3 %collective-permute-start.9 = (bf16[4,192,128]{2,1,0:T(8,128)(2,1)}, bf16[4,192,128]{2,1,0:T(8,128)(2,1)}, u32[]{:S(2)}, u32[]{:S(2)}) collective-permute-start(bf16[4,192,128]{2,1,0:T(8,128)(2,1)} %pad_maximum_fusion.refs_0_), channel_id=1, source_target_pairs={{0,6},{2,4},{4,2},{6,0},{8,14},{10,12},{12,10},{14,8},{16,22},{18,... | collective-permute-start | bytes 589832 | tf_op jit(solution)/shard_map/ppermute | solution.py:1096
  48.0 16.2 %collective-permute-start.8 = (bf16[4,192,128]{2,1,0:T(8,128)(2,1)}, bf16[4,192,128]{2,1,0:T(8,128)(2,1)}, u32[]{:S(2)}, u32[]{:S(2)}) collective-permute-start(bf16[4,192,128]{2,1,0:T(8,128)(2,1)} %pad_maximum_fusion.refs_0_), channel_id=1, source_target_pairs={{0,4},{2,6},{4,0},{6,2},{8,12},{10,14},{12,8},{14,10},{16,20},{18,... | collective-permute-start | bytes 589832 | tf_op jit(solution)/shard_map/ppermute | solution.py:1096
  48.6 15.9 %collective-permute-start.7 = (bf16[4,192,128]{2,1,0:T(8,128)(2,1)}, bf16[4,192,128]{2,1,0:T(8,128)(2,1)}, u32[]{:S(2)}, u32[]{:S(2)}) collective-permute-start(bf16[4,192,128]{2,1,0:T(8,128)(2,1)} %pad_maximum_fusion.refs_0_), channel_id=1, source_target_pairs={{0,2},{2,0},{4,6},{6,4},{8,10},{10,8},{12,14},{14,12},{16,18},{18,... | collective-permute-start | bytes 589832 | tf_op jit(solution)/shard_map/ppermute | solution.py:1096
  53.0 23.1 %copy-start.10 = (bf16[384,768]{1,0:T(8,128)(2,1)S(1)}, bf16[384,768]{1,0:T(8,128)(2,1)}, u32[]{:S(2)}) copy-start(bf16[384,768]{1,0:T(8,128)(2,1)} %da_ref.1) | copy-start | bytes 1769476
  61.0 15.1 %copy-start.28 = (bf16[192,128]{1,0:T(8,128)(2,1)S(1)}, bf16[192,128]{1,0:T(8,128)(2,1)}, u32[]{:S(2)}) copy-start(bf16[192,128]{1,0:T(8,128)(2,1)} %get-tuple-element.123.za) | copy-start | bytes 147460
  61.0 13.8 %all-to-all-start.2 = ((bf16[32,24,128]{2,1,0:T(8,128)(2,1)}), bf16[32,24,128]{2,1,0:T(8,128)(2,1)S(1)}, u32[]{:S(2)}, u32[]{:S(2)}) async-start(bf16[32,24,128]{2,1,0:T(8,128)(2,1)} %bitcast.26), calls=%async_computation.2 | async-start | bytes 393216 | tf_op jit(solution)/shard_map/all_to_all | solution.py:1100
  63.9 4.7 %collective-permute-start.13 = (bf16[4,192,128]{2,1,0:T(8,128)(2,1)}, bf16[4,192,128]{2,1,0:T(8,128)(2,1)S(1)}, u32[]{:S(2)}, u32[]{:S(2)}) collective-permute-start(bf16[4,192,128]{2,1,0:T(8,128)(2,1)} %collective-permute-done.9.refs_3_), channel_id=1, source_target_pairs={{0,1},{1,0},{2,3},{3,2},{4,5},{5,4},{6,7},{7,6},{8,9},{9,8},{10,11... | collective-permute-start | bytes 589832 | tf_op jit(solution)/shard_map/ppermute | solution.py:1091
  64.2 4.4 %collective-permute-start.12 = (bf16[4,192,128]{2,1,0:T(8,128)(2,1)}, bf16[4,192,128]{2,1,0:T(8,128)(2,1)S(1)}, u32[]{:S(2)}, u32[]{:S(2)}) collective-permute-start(bf16[4,192,128]{2,1,0:T(8,128)(2,1)} %collective-permute-done.8.refs_2_), channel_id=1, source_target_pairs={{0,1},{1,0},{2,3},{3,2},{4,5},{5,4},{6,7},{7,6},{8,9},{9,8},{10,11... | collective-permute-start | bytes 589832 | tf_op jit(solution)/shard_map/ppermute | solution.py:1091
  64.5 5.4 %collective-permute-start.11 = (bf16[4,192,128]{2,1,0:T(8,128)(2,1)}, bf16[4,192,128]{2,1,0:T(8,128)(2,1)}, u32[]{:S(2)}, u32[]{:S(2)}) collective-permute-start(bf16[4,192,128]{2,1,0:T(8,128)(2,1)} %collective-permute-done.7.refs_1_), channel_id=1, source_target_pairs={{0,1},{1,0},{2,3},{3,2},{4,5},{5,4},{6,7},{7,6},{8,9},{9,8},{10,11... | collective-permute-start | bytes 589832 | tf_op jit(solution)/shard_map/ppermute | solution.py:1091
  64.7 5.1 %collective-permute-start.10 = (bf16[4,192,128]{2,1,0:T(8,128)(2,1)}, bf16[4,192,128]{2,1,0:T(8,128)(2,1)}, u32[]{:S(2)}, u32[]{:S(2)}) collective-permute-start(bf16[4,192,128]{2,1,0:T(8,128)(2,1)} %pad_maximum_fusion.refs_0_), channel_id=1, source_target_pairs={{0,1},{1,0},{2,3},{3,2},{4,5},{5,4},{6,7},{7,6},{8,9},{9,8},{10,11... | collective-permute-start | bytes 589832 | tf_op jit(solution)/shard_map/ppermute | solution.py:1091
  65.0 9.8 %collective-permute-start.16 = (bf16[192,128]{1,0:T(8,128)(2,1)}, bf16[192,128]{1,0:T(8,128)(2,1)S(1)}, u32[]{:S(2)}, u32[]{:S(2)}) collective-permute-start(bf16[192,128]{1,0:T(8,128)(2,1)} %get-tuple-element.128), channel_id=1, source_target_pairs={{0,24},{2,26},{4,28},{6,30},{8,16},{10,18},{12,20},{14,22},{16,8},... | collective-permute-start | bytes 147464 | tf_op jit(solution)/shard_map/ppermute | solution.py:1096
  68.6 7.5 %collective-permute-start.15 = (bf16[192,128]{1,0:T(8,128)(2,1)}, bf16[192,128]{1,0:T(8,128)(2,1)S(1)}, u32[]{:S(2)}, u32[]{:S(2)}) collective-permute-start(bf16[192,128]{1,0:T(8,128)(2,1)} %get-tuple-element.126), channel_id=1, source_target_pairs={{0,16},{2,18},{4,20},{6,22},{8,24},{10,26},{12,28},{14,30},{16,0},... | collective-permute-start | bytes 147464 | tf_op jit(solution)/shard_map/ppermute | solution.py:1096
  68.6 7.4 %copy-start.3 = (bf16[4,192,2,384]{3,1,2,0:T(8,128)(2,1)S(1)}, bf16[4,192,2,384]{3,1,2,0:T(8,128)(2,1)}, u32[]{:S(2)}) copy-start(bf16[4,192,2,384]{3,1,2,0:T(8,128)(2,1)} %copy-done.2) | copy-start | bytes 3538948
  68.6 7.4 %copy-start.6 = (bf16[4,2,192,384]{3,2,1,0:T(8,128)(2,1)S(1)}, bf16[4,2,192,384]{3,2,1,0:T(8,128)(2,1)}, u32[]{:S(2)}) copy-start(bf16[4,2,192,384]{3,2,1,0:T(8,128)(2,1)} %copy-done.5) | copy-start | bytes 3538948
  68.6 7.4 %copy-start.22 = (bf16[384,128]{1,0:T(8,128)(2,1)S(1)}, bf16[384,128]{1,0:T(8,128)(2,1)}, u32[]{:S(2)}) copy-start(bf16[384,128]{1,0:T(8,128)(2,1)} %copy-done.21) | copy-start | bytes 294916
  68.6 7.4 %collective-permute-start.14 = (bf16[192,128]{1,0:T(8,128)(2,1)}, bf16[192,128]{1,0:T(8,128)(2,1)S(1)}, u32[]{:S(2)}, u32[]{:S(2)}) collective-permute-start(bf16[192,128]{1,0:T(8,128)(2,1)} %get-tuple-element.124), channel_id=1, source_target_pairs={{0,8},{2,10},{4,12},{6,14},{8,0},{10,2},{12,4},{14,6},{16,24},{18,... | collective-permute-start | bytes 147464 | tf_op jit(solution)/shard_map/ppermute | solution.py:1096
  74.8 6.3 %copy-start.32 = (bf16[32,24,128]{2,1,0:T(8,128)(2,1)}, bf16[32,24,128]{2,1,0:T(8,128)(2,1)S(1)}, u32[]{:S(2)}) copy-start(bf16[32,24,128]{2,1,0:T(8,128)(2,1)S(1)} %all-to-all-done.2.g_ref) | copy-start | bytes 589828
  77.2 6.0 %copy-start.25 = (bf16[192,384]{1,0:T(8,128)(2,1)S(1)}, bf16[192,384]{1,0:T(8,128)(2,1)}, u32[]{:S(2)}) copy-start(bf16[192,384]{1,0:T(8,128)(2,1)} %get-tuple-element.132.mine_ref) | copy-start | bytes 442372
  81.1 2.1 %collective-permute-start.17 = (bf16[576,384]{1,0:T(8,128)(2,1)S(1)}, bf16[576,384]{1,0:T(8,128)(2,1)S(1)}, u32[]{:S(2)}, u32[]{:S(2)}) collective-permute-start(bf16[576,384]{1,0:T(8,128)(2,1)S(1)} %get-tuple-element.131), channel_id=1, source_target_pairs={{0,1},{1,0},{2,3},{3,2},{4,5},{5,4},{6,7},{7,6},{8,9},{9,8},{10,11... | collective-permute-start | bytes 1327112 | tf_op jit(solution)/shard_map/ppermute | solution.py:1091
  81.2 2.0 %collective-permute-start.18 = (bf16[192,384]{1,0:T(8,128)(2,1)S(1)}, bf16[192,384]{1,0:T(8,128)(2,1)S(1)}, u32[]{:S(2)}, u32[]{:S(2)}) collective-permute-start(bf16[192,384]{1,0:T(8,128)(2,1)S(1)} %copy-done.37), channel_id=1, source_target_pairs={{0,1},{1,0},{2,3},{3,2},{4,5},{5,4},{6,7},{7,6},{8,9},{9,8},{10,11... | collective-permute-start | bytes 442376 | tf_op jit(solution)/shard_map/ppermute | solution.py:1091
  84.1 12.8 %all-to-all-start.3 = ((bf16[4,192,384]{2,1,0:T(8,128)(2,1)}), bf16[4,192,384]{2,1,0:T(8,128)(2,1)S(1)}, u32[]{:S(2)}, u32[]{:S(2)}) async-start(bf16[4,192,384]{2,1,0:T(8,128)(2,1)} %plane_add.1), calls=%async_computation.3 | async-start | bytes 1179648 | tf_op jit(solution)/shard_map/all_to_all | solution.py:1100
  95.8 10.9 %collective-permute-start.19 = (f32[960,256]{1,0:T(8,128)}, f32[960,256]{1,0:T(8,128)S(1)}, u32[]{:S(2)}, u32[]{:S(2)}) collective-permute-start(f32[960,256]{1,0:T(8,128)} %get-tuple-element.142.own_ref), channel_id=1, source_target_pairs={{0,1},{1,0},{2,3},{3,2},{4,5},{5,4},{6,7},{7,6},{8,9},{9,8},{10,11... | collective-permute-start | bytes 2949128 | tf_op jit(solution)/shard_map/ppermute | solution.py:1091
  96.8 28.8 %all-to-all-start.4 = ((bf16[32,32,128]{2,1,0:T(8,128)(2,1)}), bf16[32,32,128]{2,1,0:T(8,128)(2,1)S(1)}, u32[]{:S(2)}, u32[]{:S(2)}) async-start(bf16[32,32,128]{2,1,0:T(8,128)(2,1)} %get-tuple-element.154), calls=%async_computation.4 | async-start | bytes 524288 | tf_op jit(solution)/shard_map/all_to_all | solution.py:1100
  101.0 20.8 %collective-permute-start.22 = (bf16[192,384]{1,0:T(8,128)(2,1)S(1)}, bf16[192,384]{1,0:T(8,128)(2,1)S(1)}, u32[]{:S(2)}, u32[]{:S(2)}) collective-permute-start(bf16[192,384]{1,0:T(8,128)(2,1)S(1)} %plane_sum.1.a0), channel_id=1, source_target_pairs={{0,24},{2,26},{4,28},{6,30},{8,16},{10,18},{12,20},{14,22},{16,8},... | collective-permute-start | bytes 442376 | tf_op jit(solution)/shard_map/ppermute | solution.py:1096
  104.5 18.2 %collective-permute-start.21 = (bf16[192,384]{1,0:T(8,128)(2,1)S(1)}, bf16[192,384]{1,0:T(8,128)(2,1)S(1)}, u32[]{:S(2)}, u32[]{:S(2)}) collective-permute-start(bf16[192,384]{1,0:T(8,128)(2,1)S(1)} %plane_sum.1.a0), channel_id=1, source_target_pairs={{0,16},{2,18},{4,20},{6,22},{8,24},{10,26},{12,28},{14,30},{16,0},... | collective-permute-start | bytes 442376 | tf_op jit(solution)/shard_map/ppermute | solution.py:1096
  104.5 19.7 %collective-permute-start.20 = (bf16[192,384]{1,0:T(8,128)(2,1)S(1)}, bf16[192,384]{1,0:T(8,128)(2,1)S(1)}, u32[]{:S(2)}, u32[]{:S(2)}) collective-permute-start(bf16[192,384]{1,0:T(8,128)(2,1)S(1)} %plane_sum.1.a0), channel_id=1, source_target_pairs={{0,8},{2,10},{4,12},{6,14},{8,0},{10,2},{12,4},{14,6},{16,24},{18,... | collective-permute-start | bytes 442376 | tf_op jit(solution)/shard_map/ppermute | solution.py:1096
  105.4 20.2 %collective-permute-start.23 = (f32[24,768]{1,0:T(8,128)S(1)}, f32[24,768]{1,0:T(8,128)S(1)}, u32[]{:S(2)}, u32[]{:S(2)}) collective-permute-start(f32[24,768]{1,0:T(8,128)S(1)} %copy-done.38), channel_id=1, source_target_pairs={{1,0},{2,1},{3,2},{4,3},{5,4},{6,5},{7,6},{8,7},{9,8},{10,9},{11,1... | collective-permute-start | bytes 221192 | tf_op jit(solution)/shard_map/ppermute | solution.py:1087
  107.7 17.9 %copy-start.19 = (f32[128,768]{1,0:T(8,128)S(1)}, f32[128,768]{1,0:T(8,128)}, u32[]{:S(2)}) copy-start(f32[128,768]{1,0:T(8,128)} %get-tuple-element.156.refs_1_) | copy-start | bytes 1179652
  118.6 7.0 %copy-start.1 = (bf16[192,3,768]{2,0,1:T(8,128)(2,1)S(1)}, bf16[192,3,768]{2,0,1:T(8,128)(2,1)}, u32[]{:S(2)}) copy-start(bf16[192,3,768]{2,0,1:T(8,128)(2,1)} %param.30) | copy-start | bytes 2654212
  118.6 7.0 %copy-start.8 = (bf16[256,768]{1,0:T(8,128)(2,1)S(1)}, bf16[256,768]{1,0:T(8,128)(2,1)}, u32[]{:S(2)}) copy-start(bf16[256,768]{1,0:T(8,128)(2,1)} %refs_6_.1) | copy-start | bytes 1179652
  118.6 7.0 %copy-start.15 = (f32[3,3,768]{2,1,0:T(4,128)S(1)}, f32[3,3,768]{2,1,0:T(4,128)}, u32[]{:S(2)}) copy-start(f32[3,3,768]{2,1,0:T(4,128)} %refs_4_.1) | copy-start | bytes 82948
  118.6 7.0 %copy-start.17 = (bf16[2,144,768]{2,1,0:T(8,128)(2,1)S(1)}, bf16[2,144,768]{2,1,0:T(8,128)(2,1)}, u32[]{:S(2)}) copy-start(bf16[2,144,768]{2,1,0:T(8,128)(2,1)} %copy-done.16) | copy-start | bytes 1327108
  118.6 7.0 %copy-start.18 = (f32[128,768]{1,0:T(8,128)S(1)}, f32[128,768]{1,0:T(8,128)}, u32[]{:S(2)}) copy-start(f32[128,768]{1,0:T(8,128)} %get-tuple-element.159.refs_5_) | copy-start | bytes 1179652
  118.7 8.3 %collective-permute-start.26 = (bf16[144,256]{1,0:T(8,128)(2,1)}, bf16[144,256]{1,0:T(8,128)(2,1)S(1)}, u32[]{:S(2)}, u32[]{:S(2)}) collective-permute-start(bf16[144,256]{1,0:T(8,128)(2,1)} %get-tuple-element.160.a0), channel_id=1, source_target_pairs={{0,6},{2,4},{4,2},{6,0},{8,14},{10,12},{12,10},{14,8},{16,22},{18,... | collective-permute-start | bytes 221192 | tf_op jit(solution)/shard_map/ppermute | solution.py:1096
  121.8 5.2 %collective-permute-start.25 = (bf16[144,256]{1,0:T(8,128)(2,1)}, bf16[144,256]{1,0:T(8,128)(2,1)S(1)}, u32[]{:S(2)}, u32[]{:S(2)}) collective-permute-start(bf16[144,256]{1,0:T(8,128)(2,1)} %get-tuple-element.160.a0), channel_id=1, source_target_pairs={{0,4},{2,6},{4,0},{6,2},{8,12},{10,14},{12,8},{14,10},{16,20},{18,... | collective-permute-start | bytes 221192 | tf_op jit(solution)/shard_map/ppermute | solution.py:1096
  122.7 4.6 %collective-permute-start.24 = (bf16[144,256]{1,0:T(8,128)(2,1)}, bf16[144,256]{1,0:T(8,128)(2,1)S(1)}, u32[]{:S(2)}, u32[]{:S(2)}) collective-permute-start(bf16[144,256]{1,0:T(8,128)(2,1)} %get-tuple-element.160.a0), channel_id=1, source_target_pairs={{0,2},{2,0},{4,6},{6,4},{8,10},{10,8},{12,14},{14,12},{16,18},{18,... | collective-permute-start | bytes 221192 | tf_op jit(solution)/shard_map/ppermute | solution.py:1096
  127.3 22.0 %copy-start.35 = (f32[48,128]{1,0:T(8,128)S(1)}, f32[48,128]{1,0:T(8,128)}, u32[]{:S(2)}) copy-start(f32[48,128]{1,0:T(8,128)} %get-tuple-element.175) | copy-start | bytes 73732
  127.3 28.9 %all-to-all-start.5 = ((bf16[4,624,384]{2,1,0:T(8,128)(2,1)}), bf16[4,624,384]{2,1,0:T(8,128)(2,1)S(1)}, u32[]{:S(2)}, u32[]{:S(2)}) async-start(bf16[4,624,384]{2,1,0:T(8,128)(2,1)} %copy-done.4), calls=%async_computation.5 | async-start | bytes 3833856 | tf_op jit(solution)/shard_map/all_to_all | solution.py:1100
  131.0 8.8 %collective-permute-start.27 = (bf16[360,256]{1,0:T(8,128)(2,1)S(1)}, bf16[360,256]{1,0:T(8,128)(2,1)}, u32[]{:S(2)}, u32[]{:S(2)}) collective-permute-start(bf16[360,256]{1,0:T(8,128)(2,1)S(1)} %plane_join.3.refs_0_), channel_id=1, source_target_pairs={{0,8},{2,10},{4,12},{6,14},{8,0},{10,2},{12,4},{14,6},{16,24},{18,... | collective-permute-start | bytes 552968 | tf_op jit(solution)/shard_map/ppermute | solution.py:1096
  132.3 16.5 %collective-permute-start.28 = (bf16[360,256]{1,0:T(8,128)(2,1)S(1)}, bf16[360,256]{1,0:T(8,128)(2,1)}, u32[]{:S(2)}, u32[]{:S(2)}) collective-permute-start(bf16[360,256]{1,0:T(8,128)(2,1)S(1)} %plane_join.3.refs_0_), channel_id=1, source_target_pairs={{0,16},{2,18},{4,20},{6,22},{8,24},{10,26},{12,28},{14,30},{16,0},... | collective-permute-start | bytes 552968 | tf_op jit(solution)/shard_map/ppermute | solution.py:1096
  134.9 13.9 %collective-permute-start.29 = (bf16[360,256]{1,0:T(8,128)(2,1)S(1)}, bf16[360,256]{1,0:T(8,128)(2,1)}, u32[]{:S(2)}, u32[]{:S(2)}) collective-permute-start(bf16[360,256]{1,0:T(8,128)(2,1)S(1)} %plane_join.3.refs_0_), channel_id=1, source_target_pairs={{0,24},{2,26},{4,28},{6,30},{8,16},{10,18},{12,20},{14,22},{16,8},... | collective-permute-start | bytes 552968 | tf_op jit(solution)/shard_map/ppermute | solution.py:1096
  135.4 14.0 %collective-permute-start.30 = (bf16[360,256]{1,0:T(8,128)(2,1)S(1)}, bf16[360,256]{1,0:T(8,128)(2,1)S(1)}, u32[]{:S(2)}, u32[]{:S(2)}) collective-permute-start(bf16[360,256]{1,0:T(8,128)(2,1)S(1)} %plane_join.3.refs_0_), channel_id=1, source_target_pairs={{0,1},{1,0},{2,3},{3,2},{4,5},{5,4},{6,7},{7,6},{8,9},{9,8},{10,11... | collective-permute-start | bytes 552968 | tf_op jit(solution)/shard_map/ppermute | solution.py:1091
  139.7 10.7 %collective-permute-start.31 = (bf16[360,256]{1,0:T(8,128)(2,1)}, bf16[360,256]{1,0:T(8,128)(2,1)}, u32[]{:S(2)}, u32[]{:S(2)}) collective-permute-start(bf16[360,256]{1,0:T(8,128)(2,1)} %collective-permute-done.27.refs_1_), channel_id=1, source_target_pairs={{0,1},{1,0},{2,3},{3,2},{4,5},{5,4},{6,7},{7,6},{8,9},{9,8},{10,11... | collective-permute-start | bytes 552968 | tf_op jit(solution)/shard_map/ppermute | solution.py:1091
  148.7 1.8 %collective-permute-start.32 = (bf16[360,256]{1,0:T(8,128)(2,1)}, bf16[360,256]{1,0:T(8,128)(2,1)}, u32[]{:S(2)}, u32[]{:S(2)}) collective-permute-start(bf16[360,256]{1,0:T(8,128)(2,1)} %collective-permute-done.28.refs_2_), channel_id=1, source_target_pairs={{0,1},{1,0},{2,3},{3,2},{4,5},{5,4},{6,7},{7,6},{8,9},{9,8},{10,11... | collective-permute-start | bytes 552968 | tf_op jit(solution)/shard_map/ppermute | solution.py:1091
  148.8 2.0 %collective-permute-start.33 = (bf16[360,256]{1,0:T(8,128)(2,1)}, bf16[360,256]{1,0:T(8,128)(2,1)}, u32[]{:S(2)}, u32[]{:S(2)}) collective-permute-start(bf16[360,256]{1,0:T(8,128)(2,1)} %collective-permute-done.29.refs_3_), channel_id=1, source_target_pairs={{0,1},{1,0},{2,3},{3,2},{4,5},{5,4},{6,7},{7,6},{8,9},{9,8},{10,11... | collective-permute-start | bytes 552968 | tf_op jit(solution)/shard_map/ppermute | solution.py:1091
  149.3 7.3 %collective-permute-start.35 = (f32[48,128]{1,0:T(8,128)S(1)}, f32[48,128]{1,0:T(8,128)S(1)}, u32[]{:S(2)}, u32[]{:S(2)}) collective-permute-start(f32[48,128]{1,0:T(8,128)S(1)} %copy-done.35), channel_id=1, source_target_pairs={{0,1},{1,0},{2,3},{3,2},{4,5},{5,4},{6,7},{7,6},{8,9},{9,8},{10,11... | collective-permute-start | bytes 73736 | tf_op jit(solution)/shard_map/ppermute | solution.py:1091
  150.0 7.2 %collective-permute-start.34 = (bf16[128,768]{1,0:T(8,128)(2,1)S(1)}, bf16[128,768]{1,0:T(8,128)(2,1)S(1)}, u32[]{:S(2)}, u32[]{:S(2)}) collective-permute-start(bf16[128,768]{1,0:T(8,128)(2,1)S(1)} %mixer_back.1.half_ref), channel_id=1, source_target_pairs={{0,1},{1,0},{2,3},{3,2},{4,5},{5,4},{6,7},{7,6},{8,9},{9,8},{10,11... | collective-permute-start | bytes 589832 | tf_op jit(solution)/shard_map/ppermute | solution.py:1091
  156.2 3.9 %collective-permute-start.36 = (bf16[4,48,384]{2,1,0:T(8,128)(2,1)S(1)}, bf16[4,48,384]{2,1,0:T(8,128)(2,1)S(1)}, u32[]{:S(2)}, u32[]{:S(2)}) collective-permute-start(bf16[4,48,384]{2,1,0:T(8,128)(2,1)S(1)} %slice.35.mine_ref), channel_id=1, source_target_pairs={{0,1},{1,0},{2,3},{3,2},{4,5},{5,4},{6,7},{7,6},{8,9},{9,8},{10,11... | collective-permute-start | bytes 442376 | tf_op jit(solution)/shard_map/ppermute | solution.py:1091
  (18 other events, 28.2 us)

commit v4 on v3

--- a/solution.py
+++ b/solution.py
@@ -15,7 +15,7 @@
 EPSILON = 1e-05
 LANES = 128
 GROUP = 8
-FILTER_LANES = 2048
+FILTER_LANES = 4096
 SMALL_ROWS = 72
 BACK_MIB = 24
 BF = jnp.bfloat16
@@ -374,11 +374,11 @@
         s2 = jnp.where(lane < LANES - 2, r2, next2 * keep)
         pg_ref[n] = (taps[0] * sg + taps[1] * s1 + taps[2] * s2).astype(BF)
         sent_ref[n] = jnp.concatenate([back, next_edge * keep], axis=0).astype(BF)
-        p = p_ref[n]
+        p = p_ref[n].astype(F32)
         return r1, r2, acc0 + sg * p, acc1 + s1 * p, acc2 + s2 * p, edge_of(back)
 
     zero = jnp.zeros((3 * chans, LANES), F32)
-    _, _, acc0, acc1, acc2, _ = lax.fori_loop(0, count, step, (zero,) * 5 + (zero[:GROUP],), unroll=4)
+    _, _, acc0, acc1, acc2, _ = lax.fori_loop(0, count, step, (zero,) * 5 + (zero[:GROUP],), unroll=8)
     out = zero
     for k, acc in enumerate((acc0, acc1, acc2)):
         out = jnp.where(lane == k, jnp.sum(acc, axis=1, keepdims=True), out)
@@ -474,7 +474,7 @@
     for ref, turn_list in zip(tiles, turns):
         for q, turn in enumerate(turn_list):
             x = jnp.concatenate([ref[4 * q + z] for z in range(4)], axis=1)
-            p = mm(wc, x).astype(BF).astype(F32)
+            p = mm(wc, x).astype(BF)
             for z in range(4):
                 p_ref[source_of(place, turn, z)] = p[:, z * LANES : (z + 1) * LANES]
     per_seq = count // seqs
@@ -484,7 +484,7 @@
     def step(n, carry):
         last1, last2 = carry
         keep = jnp.where(lax.rem(n, per_seq) == 0, 0.0, 1.0)
-        p = p_ref[n]
+        p = p_ref[n].astype(F32)
         r1 = pltpu.roll(p, 1, 1)
         r2 = pltpu.roll(p, 2, 1)
         s1 = jnp.where(lane < 1, last1 * keep, r1)
@@ -493,7 +493,7 @@
         return r1, r2
 
     zero = jnp.zeros((rows3, LANES), F32)
-    lax.fori_loop(0, count, step, (zero, zero), unroll=4)
+    lax.fori_loop(0, count, step, (zero, zero), unroll=8)
 
 
 def channel_mixer(tiles, turns, place, w, taps, count, seqs, chans):
@@ -502,7 +502,10 @@
         functools.partial(channel_mixer_kernel, place, turns, seqs, chans),
         in_specs=vmem_specs(2 + len(tiles)),
         out_specs=vmem_specs(2),
-        out_shape=[jax.ShapeDtypeStruct((count, rows3, LANES), F32)] * 2,
+        out_shape=[
+            jax.ShapeDtypeStruct((count, rows3, LANES), BF),
+            jax.ShapeDtypeStruct((count, rows3, LANES), F32),
+        ],
         compiler_params=params(),
         cost_estimate=cost(3 * 10**9, 6 * 10**6),
         name="channel_mixer",

time: 162 us -> 162 us (level)
  transfers between devices with their start and end apart: 43 -> 43, of which waited for: 11 -> 11; matrix products, arithmetic and copies ran while one was open for 2% -> 2% of each run, Pallas kernels for 36% -> 35%
where the time goes in v4:
time: 162 us; the launch traced here: 161 us
  Pallas kernels  64.6 us (40%)
  starting transfers between devices  61.1 us (38%)
  waiting for transfers between devices  22 us (14%)
  local copies, waits for them, and re-layouts  10.4 us (6%)
    ppermute x18, starting transfers between devices, crossed(): return lax.ppermute(x, 'seq', [(i, i ^ mask) for i in range(devices)])  26.7 us
    all_to_all x6, starting transfers between devices, exchanged(): return lax.all_to_all(x, axes, 0, 0, axis_index_groups=groups, tiled=True)  25.1 us
    ppermute x18, waiting for transfers between devices, crossed(): return lax.ppermute(x, 'seq', [(i, i ^ mask) for i in range(devices)])  15.2 us
    pallas_call x1, Pallas kernels, channel_grads(): pl.pallas_call(functools.partial(channel_grads_kernel, place, turns, tabl...  11 us
    pallas_call x1, Pallas kernels, filter_forward(): pl.pallas_call(filter_forward_kernel, in_specs=vmem_specs(6), out_specs=v...  8.07 us
    pallas_call x1, Pallas kernels, middle_part(): pl.pallas_call(functools.partial(middle_kernel, per_plane), in_specs=vmem...  7.96 us
    unnamed x78, local copies, waits for them, and re-layouts  7.75 us
    pallas_call x1, Pallas kernels, conv_backward(): pl.pallas_call(functools.partial(conv_backward_kernel, padded, seqs, real...  7.66 us
  transfers between devices with their start and end apart: 43, of which 11 were waited for; matrix products, arithmetic and copies ran while one was open for 2% of the time, Pallas kernels for 35%

profile of v4, /device:TPU:0, one launch (start us, length us, event | category | flops | bytes accessed | tf_op | source)
XLA Modules:
  0.0 160.7 jit_solution(2279132832980697616)
XLA Ops:
  0.7 0.8 slice.30
  1.5 4.8 %collective-permute-start = (bf16[16,768]{1,0:T(8,128)(2,1)S(1)}, bf16[16,768]{1,0:T(8,128)(2,1)S(1)}, u32[]{:S(2)}, u32[]{:S(2)}) collective-permute-start(bf16[16,768]{1,0:T(8,128)(2,1)S(1)} %slice.30), channel_id=1, source_target_pairs={{0,2},{2,4},{4,6},{6,8},{8,10},{10,12},{12,14},{14,16},{16,18},{18... | collective-permute-start | bytes 73736 | tf_op jit(solution)/shard_map/ppermute | solution.py:1090
  6.4 8.1 %filter_forward.1 = (f32[24,4096]{1,0:T(8,128)}, f32[24,4096]{1,0:T(8,128)}, bf16[128,4096]{1,0:T(8,128)(2,1)}, bf16[128,4096]{1,0:T(8,128)(2,1)}, bf16[128,4096]{1,0:T(8,128)(2,1)}, /*index=5*/bf16[128,4096]{1,0:T(8,128)(2,1)}) custom-call(bf16[48,8192]{1,0:T(8,128)(2,1)} %constant.34.clone.feat_ref, f32[5,128]{1,0:T(8,128)} %w1_ref.1, f32[128]{0:T(128)} %b1_ref.1, ...), custom_call_target="tpu_custom_call" | custom-call | flops 400000000 | bytes 400000 | tf_op jit(solution)/shard_map/filter_forward/pallas_call | solution.py:225
  14.5 1.9 %mixer_in.1 = (bf16[768,128]{1,0:T(8,128)(2,1)}, f32[128,768]{1,0:T(8,128)S(1)}, bf16[2,144,768]{2,1,0:T(8,128)(2,1)S(1)}, f32[16,768]{1,0:T(8,128)S(1)}, bf16[3...) custom-call(bf16[256,768]{1,0:T(8,128)(2,1)S(1)} %copy-done.7, ...), custom_call_target="tpu_custom_call" | custom-call | flops 200000000 | bytes 200000 | tf_op jit(solution)/shard_map/mixer_in/pallas_call | solution.py:668
  16.6 0.6 copy-done.16
  17.3 0.4 copy-done.36
  17.8 5.1 %all-to-all-start = ((bf16[32,24,128]{2,1,0:T(8,128)(2,1)}), bf16[32,24,128]{2,1,0:T(8,128)(2,1)}, u32[]{:S(2)}, u32[]{:S(2)}) async-start(bf16[32,24,128]{2,1,0:T(8,128)(2,1)} %bitcast.2), calls=%async_computation | async-start | bytes 393216 | tf_op jit(solution)/shard_map/all_to_all | solution.py:1103
  22.9 1.8 %collective-permute-start.4 = (bf16[384,128]{1,0:T(8,128)(2,1)}, bf16[384,128]{1,0:T(8,128)(2,1)}, u32[]{:S(2)}, u32[]{:S(2)}) collective-permute-start(bf16[384,128]{1,0:T(8,128)(2,1)} %get-tuple-element.111), channel_id=1, source_target_pairs={{0,8},{2,10},{4,12},{6,14},{8,0},{10,2},{12,4},{14,6},{16,24},{18,... | collective-permute-start | bytes 294920 | tf_op jit(solution)/shard_map/ppermute | solution.py:1099
  24.7 2.4 %collective-permute-start.5 = (bf16[384,128]{1,0:T(8,128)(2,1)}, bf16[384,128]{1,0:T(8,128)(2,1)}, u32[]{:S(2)}, u32[]{:S(2)}) collective-permute-start(bf16[384,128]{1,0:T(8,128)(2,1)} %get-tuple-element.113), channel_id=1, source_target_pairs={{0,16},{2,18},{4,20},{6,22},{8,24},{10,26},{12,28},{14,30},{16,0},... | collective-permute-start | bytes 294920 | tf_op jit(solution)/shard_map/ppermute | solution.py:1099
  27.4 4.3 %filter_spectrum.1.h_ref = f32[960,256]{1,0:T(8,128)} custom-call(f32[24,4096]{1,0:T(8,128)} %get-tuple-element.100.own_ref, f32[24,4096]{1,0:T(8,128)} %collective-permute-done.1.other_ref, bf16[640,512]{1,0:T(8,128)(2,1)} %constant.35.clone.fh, bf16[640,512]{1,0:T(8,128)(2,1)} %constant.36.clone.fl, f32[4,40,128]{2,1,0:T(8,128)} %constant.37.clone.tw, ...), custom_call_target="tpu_custom_call" | custom-call | flops 200000000 | bytes 200000 | tf_op jit(solution)/shard_map/filter_spectrum/pallas_call | solution.py:390
  31.7 0.6 all-to-all-done.x_ref
  32.2 5.0 %conv_forward.1 = (bf16[32,24,128]{2,1,0:T(8,128)(2,1)}, f32[960,256]{1,0:T(8,128)}) custom-call(bf16[32,24,128]{2,1,0:T(8,128)(2,1)} %all-to-all-done.x_ref, f32[960,256]{1,0:T(8,128)} %filter_spectrum.1.h_ref, bf16[640,256]{1,0:T(8,128)(2,1)} %constant.40.clone.fh, bf16[640,256]{1,0:T(8,128)(2,1)} %constant.41.clone.fl, f32[4,40,128]{2,1,0:T(8,128)} %constant.37.clone.tw, ...), custom_call_target="tpu_custom_call" | custom-call | flops 250000000 | bytes 300000 | tf_op jit(solution)/shard_map/conv_forward/pallas_call | solution.py:407
  37.2 5.6 %all-to-all-start.1 = ((bf16[32,24,128]{2,1,0:T(8,128)(2,1)}), bf16[32,24,128]{2,1,0:T(8,128)(2,1)}, u32[]{:S(2)}, u32[]{:S(2)}) async-start(bf16[32,24,128]{2,1,0:T(8,128)(2,1)} %get-tuple-element.103.y_ref), calls=%async_computation.1 | async-start | bytes 393216 | tf_op jit(solution)/shard_map/all_to_all | solution.py:1103
  42.9 0.8 slice_bitcast_fusion.2
  43.7 0.8 slice_bitcast_fusion
  44.5 0.7 pad_maximum_fusion.refs_0_
  45.2 2.4 %collective-permute-start.9 = (bf16[4,192,128]{2,1,0:T(8,128)(2,1)}, bf16[4,192,128]{2,1,0:T(8,128)(2,1)}, u32[]{:S(2)}, u32[]{:S(2)}) collective-permute-start(bf16[4,192,128]{2,1,0:T(8,128)(2,1)} %pad_maximum_fusion.refs_0_), channel_id=1, source_target_pairs={{0,6},{2,4},{4,2},{6,0},{8,14},{10,12},{12,10},{14,8},{16,22},{18,... | collective-permute-start | bytes 589832 | tf_op jit(solution)/shard_map/ppermute | solution.py:1099
  47.7 0.6 collective-permute-start.8
  48.2 0.5 collective-permute-start.7
  48.7 2.9 %all-to-all-done.1 = bf16[32,24,128]{2,1,0:T(8,128)(2,1)} async-done(((bf16[32,24,128]{2,1,0:T(8,128)(2,1)}), bf16[32,24,128]{2,1,0:T(8,128)(2,1)}, u32[]{:S(2)}, u32[]{:S(2)}) %all-to-all-start.1) | async-done | bytes 196640 | tf_op jit(solution)/shard_map/all_to_all | solution.py:1103
  51.7 1.0 copy-done.5
  52.7 8.0 %middle_part.1 = (bf16[768,128]{1,0:T(8,128)(2,1)}, f32[128,768]{1,0:T(8,128)}, bf16[128,768]{1,0:T(8,128)(2,1)}, bf16[192,384]{1,0:T(8,128)(2,1)}, bf16[192,384...) custom-call(bf16[768,128]{1,0:T(8,128)(2,1)} %bitcast.4.conv_ref, ...), custom_call_target="tpu_custom_call" | custom-call | flops 450000000 | bytes 300000 | tf_op jit(solution)/shard_map/middle_part/pallas_call | solution.py:764
  60.6 3.4 %all-to-all-start.2 = ((bf16[32,24,128]{2,1,0:T(8,128)(2,1)}), bf16[32,24,128]{2,1,0:T(8,128)(2,1)}, u32[]{:S(2)}, u32[]{:S(2)}) async-start(bf16[32,24,128]{2,1,0:T(8,128)(2,1)} %bitcast.26), calls=%async_computation.2 | async-start | bytes 393216 | tf_op jit(solution)/shard_map/all_to_all | solution.py:1103
  64.1 0.5 collective-permute-start.13
  64.7 0.4 collective-permute-start.11
  65.2 3.6 %collective-permute-start.16 = (bf16[192,128]{1,0:T(8,128)(2,1)}, bf16[192,128]{1,0:T(8,128)(2,1)S(1)}, u32[]{:S(2)}, u32[]{:S(2)}) collective-permute-start(bf16[192,128]{1,0:T(8,128)(2,1)} %get-tuple-element.128), channel_id=1, source_target_pairs={{0,24},{2,26},{4,28},{6,30},{8,16},{10,18},{12,20},{14,22},{16,8},... | collective-permute-start | bytes 147464 | tf_op jit(solution)/shard_map/ppermute | solution.py:1099
  68.8 1.2 collective-permute-start.14
  70.0 0.7 copy-done.34
  70.7 4.2 %channel_mixer.1 = (bf16[32,72,128]{2,1,0:T(8,128)(2,1)}, f32[32,72,128]{2,1,0:T(8,128)}) custom-call(bf16[3,192,768]{2,1,0:T(8,128)(2,1)} %bitcast.19, f32[3,3,768]{2,1,0:T(4,128)} %refs_4_.1, bf16[4,192,128]{2,1,0:T(8,128)(2,1)} %pad_maximum_fusion.refs_0_, bf16[4,192,128]{2,1,0:T(8,128)(2,1)} %collective-permute-done.7.refs_1_, ...), custom_call_target="tpu_custom_call" | custom-call | flops 150000000 | bytes 300000 | tf_op jit(solution)/shard_map/channel_mixer/pallas_call | solution.py:501
  74.9 1.3 collective-permute-done.15.zc
  76.2 1.1 copy-done.12
  77.2 3.9 %glu_grads.1 = (f32[576,384]{1,0:T(8,128)S(1)}, bf16[576,384]{1,0:T(8,128)(2,1)S(1)}) custom-call(bf16[192,128]{1,0:T(8,128)(2,1)S(1)} %copy-done.28, bf16[192,128]{1,0:T(8,128)(2,1)S(1)} %collective-permute-done.14.zb, bf16[192,128]{1,0:T(8,128)(2,1)S(1)} %collective-permute-done.15.zc, bf16[192,128]{1,0:T(8,128)(2,1)S(1)} %collective-permute-done.16.zd, ...), custom_call_target="tpu_custom_call" | custom-call | flops 450000000 | bytes 200000 | tf_op jit(solution)/shard_map/glu_grads/pallas_call | solution.py:812
  81.2 0.5 collective-permute-start.18
  81.7 1.5 collective-permute-done.18.theirs_ref
  83.2 0.9 plane_add.1
  84.2 3.7 %all-to-all-start.3 = ((bf16[4,192,384]{2,1,0:T(8,128)(2,1)}), bf16[4,192,384]{2,1,0:T(8,128)(2,1)S(1)}, u32[]{:S(2)}, u32[]{:S(2)}) async-start(bf16[4,192,384]{2,1,0:T(8,128)(2,1)} %plane_add.1), calls=%async_computation.3 | async-start | bytes 1179648 | tf_op jit(solution)/shard_map/all_to_all | solution.py:1103
  87.8 7.7 %conv_backward.1 = (bf16[32,72,128]{2,1,0:T(8,128)(2,1)}, f32[960,256]{1,0:T(8,128)}, f32[72,128]{1,0:T(8,128)}, bf16[32,32,128]{2,1,0:T(8,128)(2,1)}) custom-call(bf16[32,24,128]{2,1,0:T(8,128)(2,1)} %all-to-all-done.2.g_ref, f32[32,72,128]{2,1,0:T(8,128)} %get-tuple-element.136.sm_ref, bf16[32,72,128]{2,1,0:T(8,128)(2,1)} %get-tuple-element.122.p_ref, ...), custom_call_target="tpu_custom_call" | custom-call | flops 350000000 | bytes 450000 | tf_op jit(solution)/shard_map/conv_backward/pallas_call | solution.py:424
  95.5 1.4 all-to-all-done.3.x_ref
  96.9 3.7 %all-to-all-start.4 = ((bf16[32,32,128]{2,1,0:T(8,128)(2,1)}), bf16[32,32,128]{2,1,0:T(8,128)(2,1)S(1)}, u32[]{:S(2)}, u32[]{:S(2)}) async-start(bf16[32,32,128]{2,1,0:T(8,128)(2,1)} %get-tuple-element.154), calls=%async_computation.4 | async-start | bytes 524288 | tf_op jit(solution)/shard_map/all_to_all | solution.py:1103
  100.7 3.5 %collective-permute-start.22 = (bf16[192,384]{1,0:T(8,128)(2,1)S(1)}, bf16[192,384]{1,0:T(8,128)(2,1)S(1)}, u32[]{:S(2)}, u32[]{:S(2)}) collective-permute-start(bf16[192,384]{1,0:T(8,128)(2,1)S(1)} %plane_sum.1.a0), channel_id=1, source_target_pairs={{0,24},{2,26},{4,28},{6,30},{8,16},{10,18},{12,20},{14,22},{16,8},... | collective-permute-start | bytes 442376 | tf_op jit(solution)/shard_map/ppermute | solution.py:1099
  104.1 1.0 collective-permute-start.20
  105.1 1.3 collective-permute-start.23
  106.4 0.9 copy-done.31
  107.4 11.0 %channel_grads.1 = (bf16[144,256]{1,0:T(8,128)(2,1)}, f32[48,128]{1,0:T(8,128)}) custom-call(bf16[32,72,128]{2,1,0:T(8,128)(2,1)} %get-tuple-element.138.pg_ref, f32[72,128]{1,0:T(8,128)} %get-tuple-element.141.st_ref, f32[960,256]{1,0:T(8,128)} %get-tuple-element.142.own_ref, f32[960,256]{1,0:T(8,128)} %copy-done.31, f32[4,40,128]{2,1,0:T(8,128)} %constant.37.clone.tw, ...), custom_call_target="tpu_custom_call" | custom-call | flops 400000000 | bytes 400000 | tf_op jit(solution)/shard_map/channel_grads/pallas_call | solution.py:575
  118.4 3.1 %collective-permute-start.26 = (bf16[144,256]{1,0:T(8,128)(2,1)}, bf16[144,256]{1,0:T(8,128)(2,1)S(1)}, u32[]{:S(2)}, u32[]{:S(2)}) collective-permute-start(bf16[144,256]{1,0:T(8,128)(2,1)} %get-tuple-element.160.a0), channel_id=1, source_target_pairs={{0,6},{2,4},{4,2},{6,0},{8,14},{10,12},{12,10},{14,8},{16,22},{18,... | collective-permute-start | bytes 221192 | tf_op jit(solution)/shard_map/ppermute | solution.py:1099
  121.5 0.6 collective-permute-start.25
  122.4 1.5 collective-permute-start.24
  124.0 1.2 copy-done.4
  125.4 1.3 mixer_back.1.half_ref
  127.0 3.7 %all-to-all-start.5 = ((bf16[4,624,384]{2,1,0:T(8,128)(2,1)}), bf16[4,624,384]{2,1,0:T(8,128)(2,1)S(1)}, u32[]{:S(2)}, u32[]{:S(2)}) async-start(bf16[4,624,384]{2,1,0:T(8,128)(2,1)} %copy-done.4), calls=%async_computation.5 | async-start | bytes 3833856 | tf_op jit(solution)/shard_map/all_to_all | solution.py:1103
  130.7 1.3 collective-permute-start.27
  132.0 2.6 %collective-permute-start.28 = (bf16[360,256]{1,0:T(8,128)(2,1)S(1)}, bf16[360,256]{1,0:T(8,128)(2,1)}, u32[]{:S(2)}, u32[]{:S(2)}) collective-permute-start(bf16[360,256]{1,0:T(8,128)(2,1)S(1)} %plane_join.3.refs_0_), channel_id=1, source_target_pairs={{0,16},{2,18},{4,20},{6,22},{8,24},{10,26},{12,28},{14,30},{16,0},... | collective-permute-start | bytes 552968 | tf_op jit(solution)/shard_map/ppermute | solution.py:1099
  134.6 0.5 collective-permute-start.29
  135.1 4.4 %collective-permute-done.27.refs_1_ = bf16[360,256]{1,0:T(8,128)(2,1)} collective-permute-done((bf16[360,256]{1,0:T(8,128)(2,1)S(1)}, bf16[360,256]{1,0:T(8,128)(2,1)}, u32[]{:S(2)}, u32[]{:S(2)}) %collective-permute-start.27) | collective-permute-done | bytes 184352 | tf_op jit(solution)/shard_map/ppermute | solution.py:1099
  139.5 9.0 %collective-permute-done.28.refs_2_ = bf16[360,256]{1,0:T(8,128)(2,1)} collective-permute-done((bf16[360,256]{1,0:T(8,128)(2,1)S(1)}, bf16[360,256]{1,0:T(8,128)(2,1)}, u32[]{:S(2)}, u32[]{:S(2)}) %collective-permute-start.28) | collective-permute-done | bytes 184352 | tf_op jit(solution)/shard_map/ppermute | solution.py:1099
  148.5 0.5 collective-permute-start.33
  149.1 0.7 copy-done.23
  149.7 0.4 collective-permute-start.34
  150.5 0.9 copy-done.24
  151.4 4.5 %in_unpack.1 = (f32[3,192,768]{2,1,0:T(8,128)}, f32[3,3,768]{2,1,0:T(4,128)}, f32[768]{0:T(1024)}, f32[5,128]{1,0:T(8,128)}, f32[128]{0:T(128)}, /*index=5*/f32[128,128]{1,0:T(8,128)}, f32[768]{0:T(1024)}) custom-call(bf16[3,192,768]{2,1,0:T(8,128)(2,1)S(1)} %bitcast.22, f32[768]{0:T(1024)S(1)} %copy-done.29, bf16[360,256]{1,0:T(8,128)(2,1)S(1)} %plane_join.3.refs_0_, ...), custom_call_target="tpu_custom_call" | custom-call | flops 5000000 | bytes 200000 | tf_op jit(solution)/shard_map/in_unpack/pallas_call | solution.py:1002
  156.0 0.3 collective-permute-start.36
  156.3 0.6 fusion
  156.9 2.9 %finish.1 = (f32[4,192,2,384]{3,2,1,0:T(2,128)}, f32[384,768]{1,0:T(8,128)}, bf16[256,768]{1,0:T(8,128)(2,1)}) custom-call(bf16[4,624,384]{2,1,0:T(8,128)(2,1)S(1)} %all-to-all-done.5.a_ref, bf16[128,768]{1,0:T(8,128)(2,1)S(1)} %mixer_back.1.half_ref, bf16[128,768]{1,0:T(8,128)(2,1)S(1)} %collective-permute-done.34.back_ref), custom_call_target="tpu_custom_call" | custom-call | flops 5000000 | bytes 300000 | tf_op jit(solution)/shard_map/finish/pallas_call | solution.py:917
  159.8 0.9 out_unpack.1
  (125 shorter events, 2.5 us)
Async XLA Ops:
  0.6 13.8 %copy-start.7 = (bf16[256,768]{1,0:T(8,128)(2,1)S(1)}, bf16[256,768]{1,0:T(8,128)(2,1)}, u32[]{:S(2)}) copy-start(bf16[256,768]{1,0:T(8,128)(2,1)} %refs_6_.1) | copy-start | bytes 1179652
  0.7 13.8 %copy-start = (bf16[192,3,768]{2,0,1:T(8,128)(2,1)S(1)}, bf16[192,3,768]{2,0,1:T(8,128)(2,1)}, u32[]{:S(2)}) copy-start(bf16[192,3,768]{2,0,1:T(8,128)(2,1)} %param.30) | copy-start | bytes 2654212
  0.7 13.8 %copy-start.29 = (f32[768]{0:T(1024)S(1)}, f32[768]{0:T(1024)}, u32[]{:S(2)}) copy-start(f32[768]{0:T(1024)} %gain_ref.5) | copy-start | bytes 9220
  0.7 13.8 %copy-start.14 = (f32[3,3,768]{2,1,0:T(4,128)S(1)}, f32[3,3,768]{2,1,0:T(4,128)}, u32[]{:S(2)}) copy-start(f32[3,3,768]{2,1,0:T(4,128)} %refs_4_.1) | copy-start | bytes 82948
  0.7 13.8 %copy-start.13 = (bf16[128,768]{1,0:T(8,128)(2,1)S(1)}, bf16[128,768]{1,0:T(8,128)(2,1)}, u32[]{:S(2)}) copy-start(bf16[128,768]{1,0:T(8,128)(2,1)} %og_ref.3) | copy-start | bytes 589828
  1.5 12.9 %collective-permute-start = (bf16[16,768]{1,0:T(8,128)(2,1)S(1)}, bf16[16,768]{1,0:T(8,128)(2,1)S(1)}, u32[]{:S(2)}, u32[]{:S(2)}) collective-permute-start(bf16[16,768]{1,0:T(8,128)(2,1)S(1)} %slice.30), channel_id=1, source_target_pairs={{0,2},{2,4},{4,6},{6,8},{8,10},{10,12},{12,14},{14,16},{16,18},{18... | collective-permute-start | bytes 73736 | tf_op jit(solution)/shard_map/ppermute | solution.py:1090
  16.4 11.0 %copy-start.9 = (bf16[384,768]{1,0:T(8,128)(2,1)S(1)}, bf16[384,768]{1,0:T(8,128)(2,1)}, u32[]{:S(2)}) copy-start(bf16[384,768]{1,0:T(8,128)(2,1)} %da_ref.1) | copy-start | bytes 1769476
  17.3 14.3 %copy-start.2 = (bf16[4,192,2,384]{3,1,2,0:T(8,128)(2,1)}, bf16[4,192,2,384]{3,1,2,0:T(8,128)(2,1)S(1)}, u32[]{:S(2)}) copy-start(bf16[4,192,2,384]{3,1,2,0:T(8,128)(2,1)S(1)} %copy.43) | copy-start | bytes 3538948
  17.3 34.3 %collective-permute-start.2 = (bf16[4,2,192,384]{3,2,1,0:T(8,128)(2,1)S(1)}, bf16[4,2,192,384]{3,2,1,0:T(8,128)(2,1)S(1)}, u32[]{:S(2)}, u32[]{:S(2)}) collective-permute-start(bf16[4,2,192,384]{3,2,1,0:T(8,128)(2,1)S(1)} %bitcast.23), channel_id=1, source_target_pairs={{0,1},{1,0},{2,3},{3,2},{4,5},{5,4},{6,7},{7,6},{8,9},{9,8},{10,11... | collective-permute-start | bytes 3538952 | tf_op jit(solution)/shard_map/ppermute | solution.py:1094
  17.7 9.7 %collective-permute-start.1 = (f32[24,4096]{1,0:T(8,128)S(1)}, f32[24,4096]{1,0:T(8,128)}, u32[]{:S(2)}, u32[]{:S(2)}) collective-permute-start(f32[24,4096]{1,0:T(8,128)S(1)} %copy-done.36), channel_id=1, source_target_pairs={{0,1},{1,0},{2,3},{3,2},{4,5},{5,4},{6,7},{7,6},{8,9},{9,8},{10,11... | collective-permute-start | bytes 1179656 | tf_op jit(solution)/shard_map/ppermute | solution.py:1094
  17.8 14.4 %all-to-all-start = ((bf16[32,24,128]{2,1,0:T(8,128)(2,1)}), bf16[32,24,128]{2,1,0:T(8,128)(2,1)}, u32[]{:S(2)}, u32[]{:S(2)}) async-start(bf16[32,24,128]{2,1,0:T(8,128)(2,1)} %bitcast.2), calls=%async_computation | async-start | bytes 393216 | tf_op jit(solution)/shard_map/all_to_all | solution.py:1103
  22.9 19.9 %collective-permute-start.4 = (bf16[384,128]{1,0:T(8,128)(2,1)}, bf16[384,128]{1,0:T(8,128)(2,1)}, u32[]{:S(2)}, u32[]{:S(2)}) collective-permute-start(bf16[384,128]{1,0:T(8,128)(2,1)} %get-tuple-element.111), channel_id=1, source_target_pairs={{0,8},{2,10},{4,12},{6,14},{8,0},{10,2},{12,4},{14,6},{16,24},{18,... | collective-permute-start | bytes 294920 | tf_op jit(solution)/shard_map/ppermute | solution.py:1099
  24.7 19.0 %collective-permute-start.5 = (bf16[384,128]{1,0:T(8,128)(2,1)}, bf16[384,128]{1,0:T(8,128)(2,1)}, u32[]{:S(2)}, u32[]{:S(2)}) collective-permute-start(bf16[384,128]{1,0:T(8,128)(2,1)} %get-tuple-element.113), channel_id=1, source_target_pairs={{0,16},{2,18},{4,20},{6,22},{8,24},{10,26},{12,28},{14,30},{16,0},... | collective-permute-start | bytes 294920 | tf_op jit(solution)/shard_map/ppermute | solution.py:1099
  27.1 16.6 %collective-permute-start.6 = (bf16[384,128]{1,0:T(8,128)(2,1)}, bf16[384,128]{1,0:T(8,128)(2,1)}, u32[]{:S(2)}, u32[]{:S(2)}) collective-permute-start(bf16[384,128]{1,0:T(8,128)(2,1)} %get-tuple-element.115), channel_id=1, source_target_pairs={{0,24},{2,26},{4,28},{6,30},{8,16},{10,18},{12,20},{14,22},{16,8},... | collective-permute-start | bytes 294920 | tf_op jit(solution)/shard_map/ppermute | solution.py:1099
  27.4 21.3 %collective-permute-start.3 = (bf16[384,768]{1,0:T(8,128)(2,1)S(1)}, bf16[384,768]{1,0:T(8,128)(2,1)S(1)}, u32[]{:S(2)}, u32[]{:S(2)}) collective-permute-start(bf16[384,768]{1,0:T(8,128)(2,1)S(1)} %copy-done.9), channel_id=1, source_target_pairs={{0,1},{1,0},{2,3},{3,2},{4,5},{5,4},{6,7},{7,6},{8,9},{9,8},{10,11... | collective-permute-start | bytes 1769480 | tf_op jit(solution)/shard_map/ppermute | solution.py:1094
  37.2 14.4 %all-to-all-start.1 = ((bf16[32,24,128]{2,1,0:T(8,128)(2,1)}), bf16[32,24,128]{2,1,0:T(8,128)(2,1)}, u32[]{:S(2)}, u32[]{:S(2)}) async-start(bf16[32,24,128]{2,1,0:T(8,128)(2,1)} %get-tuple-element.103.y_ref), calls=%async_computation.1 | async-start | bytes 393216 | tf_op jit(solution)/shard_map/all_to_all | solution.py:1103
  45.2 18.8 %collective-permute-start.9 = (bf16[4,192,128]{2,1,0:T(8,128)(2,1)}, bf16[4,192,128]{2,1,0:T(8,128)(2,1)}, u32[]{:S(2)}, u32[]{:S(2)}) collective-permute-start(bf16[4,192,128]{2,1,0:T(8,128)(2,1)} %pad_maximum_fusion.refs_0_), channel_id=1, source_target_pairs={{0,6},{2,4},{4,2},{6,0},{8,14},{10,12},{12,10},{14,8},{16,22},{18,... | collective-permute-start | bytes 589832 | tf_op jit(solution)/shard_map/ppermute | solution.py:1099
  47.7 16.9 %collective-permute-start.8 = (bf16[4,192,128]{2,1,0:T(8,128)(2,1)}, bf16[4,192,128]{2,1,0:T(8,128)(2,1)}, u32[]{:S(2)}, u32[]{:S(2)}) collective-permute-start(bf16[4,192,128]{2,1,0:T(8,128)(2,1)} %pad_maximum_fusion.refs_0_), channel_id=1, source_target_pairs={{0,4},{2,6},{4,0},{6,2},{8,12},{10,14},{12,8},{14,10},{16,20},{18,... | collective-permute-start | bytes 589832 | tf_op jit(solution)/shard_map/ppermute | solution.py:1099
  48.2 16.4 %collective-permute-start.7 = (bf16[4,192,128]{2,1,0:T(8,128)(2,1)}, bf16[4,192,128]{2,1,0:T(8,128)(2,1)}, u32[]{:S(2)}, u32[]{:S(2)}) collective-permute-start(bf16[4,192,128]{2,1,0:T(8,128)(2,1)} %pad_maximum_fusion.refs_0_), channel_id=1, source_target_pairs={{0,2},{2,0},{4,6},{6,4},{8,10},{10,8},{12,14},{14,12},{16,18},{18,... | collective-permute-start | bytes 589832 | tf_op jit(solution)/shard_map/ppermute | solution.py:1099
  52.7 23.5 %copy-start.10 = (bf16[384,768]{1,0:T(8,128)(2,1)S(1)}, bf16[384,768]{1,0:T(8,128)(2,1)}, u32[]{:S(2)}) copy-start(bf16[384,768]{1,0:T(8,128)(2,1)} %da_ref.1) | copy-start | bytes 1769476
  60.6 15.5 %copy-start.28 = (bf16[192,128]{1,0:T(8,128)(2,1)S(1)}, bf16[192,128]{1,0:T(8,128)(2,1)}, u32[]{:S(2)}) copy-start(bf16[192,128]{1,0:T(8,128)(2,1)} %get-tuple-element.123.za) | copy-start | bytes 147460
  60.6 14.2 %all-to-all-start.2 = ((bf16[32,24,128]{2,1,0:T(8,128)(2,1)}), bf16[32,24,128]{2,1,0:T(8,128)(2,1)}, u32[]{:S(2)}, u32[]{:S(2)}) async-start(bf16[32,24,128]{2,1,0:T(8,128)(2,1)} %bitcast.26), calls=%async_computation.2 | async-start | bytes 393216 | tf_op jit(solution)/shard_map/all_to_all | solution.py:1103
  64.1 4.7 %collective-permute-start.13 = (bf16[4,192,128]{2,1,0:T(8,128)(2,1)}, bf16[4,192,128]{2,1,0:T(8,128)(2,1)S(1)}, u32[]{:S(2)}, u32[]{:S(2)}) collective-permute-start(bf16[4,192,128]{2,1,0:T(8,128)(2,1)} %collective-permute-done.9.refs_3_), channel_id=1, source_target_pairs={{0,1},{1,0},{2,3},{3,2},{4,5},{5,4},{6,7},{7,6},{8,9},{9,8},{10,11... | collective-permute-start | bytes 589832 | tf_op jit(solution)/shard_map/ppermute | solution.py:1094
  64.6 4.2 %collective-permute-start.12 = (bf16[4,192,128]{2,1,0:T(8,128)(2,1)}, bf16[4,192,128]{2,1,0:T(8,128)(2,1)S(1)}, u32[]{:S(2)}, u32[]{:S(2)}) collective-permute-start(bf16[4,192,128]{2,1,0:T(8,128)(2,1)} %collective-permute-done.8.refs_2_), channel_id=1, source_target_pairs={{0,1},{1,0},{2,3},{3,2},{4,5},{5,4},{6,7},{7,6},{8,9},{9,8},{10,11... | collective-permute-start | bytes 589832 | tf_op jit(solution)/shard_map/ppermute | solution.py:1094
  64.7 5.3 %collective-permute-start.11 = (bf16[4,192,128]{2,1,0:T(8,128)(2,1)}, bf16[4,192,128]{2,1,0:T(8,128)(2,1)S(1)}, u32[]{:S(2)}, u32[]{:S(2)}) collective-permute-start(bf16[4,192,128]{2,1,0:T(8,128)(2,1)} %collective-permute-done.7.refs_1_), channel_id=1, source_target_pairs={{0,1},{1,0},{2,3},{3,2},{4,5},{5,4},{6,7},{7,6},{8,9},{9,8},{10,11... | collective-permute-start | bytes 589832 | tf_op jit(solution)/shard_map/ppermute | solution.py:1094
  65.1 4.9 %collective-permute-start.10 = (bf16[4,192,128]{2,1,0:T(8,128)(2,1)}, bf16[4,192,128]{2,1,0:T(8,128)(2,1)}, u32[]{:S(2)}, u32[]{:S(2)}) collective-permute-start(bf16[4,192,128]{2,1,0:T(8,128)(2,1)} %pad_maximum_fusion.refs_0_), channel_id=1, source_target_pairs={{0,1},{1,0},{2,3},{3,2},{4,5},{5,4},{6,7},{7,6},{8,9},{9,8},{10,11... | collective-permute-start | bytes 589832 | tf_op jit(solution)/shard_map/ppermute | solution.py:1094
  65.2 9.7 %collective-permute-start.16 = (bf16[192,128]{1,0:T(8,128)(2,1)}, bf16[192,128]{1,0:T(8,128)(2,1)S(1)}, u32[]{:S(2)}, u32[]{:S(2)}) collective-permute-start(bf16[192,128]{1,0:T(8,128)(2,1)} %get-tuple-element.128), channel_id=1, source_target_pairs={{0,24},{2,26},{4,28},{6,30},{8,16},{10,18},{12,20},{14,22},{16,8},... | collective-permute-start | bytes 147464 | tf_op jit(solution)/shard_map/ppermute | solution.py:1099
  68.7 7.4 %collective-permute-start.15 = (bf16[192,128]{1,0:T(8,128)(2,1)}, bf16[192,128]{1,0:T(8,128)(2,1)S(1)}, u32[]{:S(2)}, u32[]{:S(2)}) collective-permute-start(bf16[192,128]{1,0:T(8,128)(2,1)} %get-tuple-element.126), channel_id=1, source_target_pairs={{0,16},{2,18},{4,20},{6,22},{8,24},{10,26},{12,28},{14,30},{16,0},... | collective-permute-start | bytes 147464 | tf_op jit(solution)/shard_map/ppermute | solution.py:1099
  68.8 7.4 %copy-start.3 = (bf16[4,192,2,384]{3,1,2,0:T(8,128)(2,1)S(1)}, bf16[4,192,2,384]{3,1,2,0:T(8,128)(2,1)}, u32[]{:S(2)}) copy-start(bf16[4,192,2,384]{3,1,2,0:T(8,128)(2,1)} %copy-done.2) | copy-start | bytes 3538948
  68.8 7.4 %copy-start.6 = (bf16[4,2,192,384]{3,2,1,0:T(8,128)(2,1)S(1)}, bf16[4,2,192,384]{3,2,1,0:T(8,128)(2,1)}, u32[]{:S(2)}) copy-start(bf16[4,2,192,384]{3,2,1,0:T(8,128)(2,1)} %copy-done.5) | copy-start | bytes 3538948
  68.8 7.4 %copy-start.22 = (bf16[384,128]{1,0:T(8,128)(2,1)S(1)}, bf16[384,128]{1,0:T(8,128)(2,1)}, u32[]{:S(2)}) copy-start(bf16[384,128]{1,0:T(8,128)(2,1)} %copy-done.21) | copy-start | bytes 294916
  68.8 7.3 %collective-permute-start.14 = (bf16[192,128]{1,0:T(8,128)(2,1)}, bf16[192,128]{1,0:T(8,128)(2,1)S(1)}, u32[]{:S(2)}, u32[]{:S(2)}) collective-permute-start(bf16[192,128]{1,0:T(8,128)(2,1)} %get-tuple-element.124), channel_id=1, source_target_pairs={{0,8},{2,10},{4,12},{6,14},{8,0},{10,2},{12,4},{14,6},{16,24},{18,... | collective-permute-start | bytes 147464 | tf_op jit(solution)/shard_map/ppermute | solution.py:1099
  77.2 6.0 %copy-start.25 = (bf16[192,384]{1,0:T(8,128)(2,1)S(1)}, bf16[192,384]{1,0:T(8,128)(2,1)}, u32[]{:S(2)}) copy-start(bf16[192,384]{1,0:T(8,128)(2,1)} %get-tuple-element.132.mine_ref) | copy-start | bytes 442372
  81.2 2.1 %collective-permute-start.17 = (bf16[576,384]{1,0:T(8,128)(2,1)S(1)}, bf16[576,384]{1,0:T(8,128)(2,1)S(1)}, u32[]{:S(2)}, u32[]{:S(2)}) collective-permute-start(bf16[576,384]{1,0:T(8,128)(2,1)S(1)} %get-tuple-element.131), channel_id=1, source_target_pairs={{0,1},{1,0},{2,3},{3,2},{4,5},{5,4},{6,7},{7,6},{8,9},{9,8},{10,11... | collective-permute-start | bytes 1327112 | tf_op jit(solution)/shard_map/ppermute | solution.py:1094
  81.2 2.0 %collective-permute-start.18 = (bf16[192,384]{1,0:T(8,128)(2,1)S(1)}, bf16[192,384]{1,0:T(8,128)(2,1)S(1)}, u32[]{:S(2)}, u32[]{:S(2)}) collective-permute-start(bf16[192,384]{1,0:T(8,128)(2,1)S(1)} %copy-done.37), channel_id=1, source_target_pairs={{0,1},{1,0},{2,3},{3,2},{4,5},{5,4},{6,7},{7,6},{8,9},{9,8},{10,11... | collective-permute-start | bytes 442376 | tf_op jit(solution)/shard_map/ppermute | solution.py:1094
  84.2 12.8 %all-to-all-start.3 = ((bf16[4,192,384]{2,1,0:T(8,128)(2,1)}), bf16[4,192,384]{2,1,0:T(8,128)(2,1)S(1)}, u32[]{:S(2)}, u32[]{:S(2)}) async-start(bf16[4,192,384]{2,1,0:T(8,128)(2,1)} %plane_add.1), calls=%async_computation.3 | async-start | bytes 1179648 | tf_op jit(solution)/shard_map/all_to_all | solution.py:1103
  95.5 10.9 %collective-permute-start.19 = (f32[960,256]{1,0:T(8,128)}, f32[960,256]{1,0:T(8,128)S(1)}, u32[]{:S(2)}, u32[]{:S(2)}) collective-permute-start(f32[960,256]{1,0:T(8,128)} %get-tuple-element.142.own_ref), channel_id=1, source_target_pairs={{0,1},{1,0},{2,3},{3,2},{4,5},{5,4},{6,7},{7,6},{8,9},{9,8},{10,11... | collective-permute-start | bytes 2949128 | tf_op jit(solution)/shard_map/ppermute | solution.py:1094
  96.9 28.4 %all-to-all-start.4 = ((bf16[32,32,128]{2,1,0:T(8,128)(2,1)}), bf16[32,32,128]{2,1,0:T(8,128)(2,1)S(1)}, u32[]{:S(2)}, u32[]{:S(2)}) async-start(bf16[32,32,128]{2,1,0:T(8,128)(2,1)} %get-tuple-element.154), calls=%async_computation.4 | async-start | bytes 524288 | tf_op jit(solution)/shard_map/all_to_all | solution.py:1103
  100.6 4.6 %copy-start.38 = (f32[24,768]{1,0:T(8,128)S(1)}, f32[24,768]{1,0:T(8,128)}, u32[]{:S(2)}) copy-start(f32[24,768]{1,0:T(8,128)} %get-tuple-element.157) | copy-start | bytes 221188
  100.7 20.9 %collective-permute-start.22 = (bf16[192,384]{1,0:T(8,128)(2,1)S(1)}, bf16[192,384]{1,0:T(8,128)(2,1)S(1)}, u32[]{:S(2)}, u32[]{:S(2)}) collective-permute-start(bf16[192,384]{1,0:T(8,128)(2,1)S(1)} %plane_sum.1.a0), channel_id=1, source_target_pairs={{0,24},{2,26},{4,28},{6,30},{8,16},{10,18},{12,20},{14,22},{16,8},... | collective-permute-start | bytes 442376 | tf_op jit(solution)/shard_map/ppermute | solution.py:1099
  104.1 18.2 %collective-permute-start.21 = (bf16[192,384]{1,0:T(8,128)(2,1)S(1)}, bf16[192,384]{1,0:T(8,128)(2,1)S(1)}, u32[]{:S(2)}, u32[]{:S(2)}) collective-permute-start(bf16[192,384]{1,0:T(8,128)(2,1)S(1)} %plane_sum.1.a0), channel_id=1, source_target_pairs={{0,16},{2,18},{4,20},{6,22},{8,24},{10,26},{12,28},{14,30},{16,0},... | collective-permute-start | bytes 442376 | tf_op jit(solution)/shard_map/ppermute | solution.py:1099
  104.1 19.7 %collective-permute-start.20 = (bf16[192,384]{1,0:T(8,128)(2,1)S(1)}, bf16[192,384]{1,0:T(8,128)(2,1)S(1)}, u32[]{:S(2)}, u32[]{:S(2)}) collective-permute-start(bf16[192,384]{1,0:T(8,128)(2,1)S(1)} %plane_sum.1.a0), channel_id=1, source_target_pairs={{0,8},{2,10},{4,12},{6,14},{8,0},{10,2},{12,4},{14,6},{16,24},{18,... | collective-permute-start | bytes 442376 | tf_op jit(solution)/shard_map/ppermute | solution.py:1099
  105.1 20.2 %collective-permute-start.23 = (f32[24,768]{1,0:T(8,128)S(1)}, f32[24,768]{1,0:T(8,128)S(1)}, u32[]{:S(2)}, u32[]{:S(2)}) collective-permute-start(f32[24,768]{1,0:T(8,128)S(1)} %copy-done.38), channel_id=1, source_target_pairs={{1,0},{2,1},{3,2},{4,3},{5,4},{6,5},{7,6},{8,7},{9,8},{10,9},{11,1... | collective-permute-start | bytes 221192 | tf_op jit(solution)/shard_map/ppermute | solution.py:1090
  107.4 17.9 %copy-start.19 = (f32[128,768]{1,0:T(8,128)S(1)}, f32[128,768]{1,0:T(8,128)}, u32[]{:S(2)}) copy-start(f32[128,768]{1,0:T(8,128)} %get-tuple-element.156.refs_1_) | copy-start | bytes 1179652
  118.3 7.0 %copy-start.1 = (bf16[192,3,768]{2,0,1:T(8,128)(2,1)S(1)}, bf16[192,3,768]{2,0,1:T(8,128)(2,1)}, u32[]{:S(2)}) copy-start(bf16[192,3,768]{2,0,1:T(8,128)(2,1)} %param.30) | copy-start | bytes 2654212
  118.3 7.0 %copy-start.8 = (bf16[256,768]{1,0:T(8,128)(2,1)S(1)}, bf16[256,768]{1,0:T(8,128)(2,1)}, u32[]{:S(2)}) copy-start(bf16[256,768]{1,0:T(8,128)(2,1)} %refs_6_.1) | copy-start | bytes 1179652
  118.4 7.0 %copy-start.15 = (f32[3,3,768]{2,1,0:T(4,128)S(1)}, f32[3,3,768]{2,1,0:T(4,128)}, u32[]{:S(2)}) copy-start(f32[3,3,768]{2,1,0:T(4,128)} %refs_4_.1) | copy-start | bytes 82948
  118.4 7.0 %copy-start.17 = (bf16[2,144,768]{2,1,0:T(8,128)(2,1)S(1)}, bf16[2,144,768]{2,1,0:T(8,128)(2,1)}, u32[]{:S(2)}) copy-start(bf16[2,144,768]{2,1,0:T(8,128)(2,1)} %copy-done.16) | copy-start | bytes 1327108
  118.4 7.0 %copy-start.18 = (f32[128,768]{1,0:T(8,128)S(1)}, f32[128,768]{1,0:T(8,128)}, u32[]{:S(2)}) copy-start(f32[128,768]{1,0:T(8,128)} %get-tuple-element.159.refs_5_) | copy-start | bytes 1179652
  118.4 8.3 %collective-permute-start.26 = (bf16[144,256]{1,0:T(8,128)(2,1)}, bf16[144,256]{1,0:T(8,128)(2,1)S(1)}, u32[]{:S(2)}, u32[]{:S(2)}) collective-permute-start(bf16[144,256]{1,0:T(8,128)(2,1)} %get-tuple-element.160.a0), channel_id=1, source_target_pairs={{0,6},{2,4},{4,2},{6,0},{8,14},{10,12},{12,10},{14,8},{16,22},{18,... | collective-permute-start | bytes 221192 | tf_op jit(solution)/shard_map/ppermute | solution.py:1099
  121.5 5.1 %collective-permute-start.25 = (bf16[144,256]{1,0:T(8,128)(2,1)}, bf16[144,256]{1,0:T(8,128)(2,1)S(1)}, u32[]{:S(2)}, u32[]{:S(2)}) collective-permute-start(bf16[144,256]{1,0:T(8,128)(2,1)} %get-tuple-element.160.a0), channel_id=1, source_target_pairs={{0,4},{2,6},{4,0},{6,2},{8,12},{10,14},{12,8},{14,10},{16,20},{18,... | collective-permute-start | bytes 221192 | tf_op jit(solution)/shard_map/ppermute | solution.py:1099
  122.4 4.6 %collective-permute-start.24 = (bf16[144,256]{1,0:T(8,128)(2,1)}, bf16[144,256]{1,0:T(8,128)(2,1)S(1)}, u32[]{:S(2)}, u32[]{:S(2)}) collective-permute-start(bf16[144,256]{1,0:T(8,128)(2,1)} %get-tuple-element.160.a0), channel_id=1, source_target_pairs={{0,2},{2,0},{4,6},{6,4},{8,10},{10,8},{12,14},{14,12},{16,18},{18,... | collective-permute-start | bytes 221192 | tf_op jit(solution)/shard_map/ppermute | solution.py:1099
  127.0 22.0 %copy-start.35 = (f32[48,128]{1,0:T(8,128)S(1)}, f32[48,128]{1,0:T(8,128)}, u32[]{:S(2)}) copy-start(f32[48,128]{1,0:T(8,128)} %get-tuple-element.175) | copy-start | bytes 73732
  127.0 28.9 %all-to-all-start.5 = ((bf16[4,624,384]{2,1,0:T(8,128)(2,1)}), bf16[4,624,384]{2,1,0:T(8,128)(2,1)S(1)}, u32[]{:S(2)}, u32[]{:S(2)}) async-start(bf16[4,624,384]{2,1,0:T(8,128)(2,1)} %copy-done.4), calls=%async_computation.5 | async-start | bytes 3833856 | tf_op jit(solution)/shard_map/all_to_all | solution.py:1103
  130.7 8.8 %collective-permute-start.27 = (bf16[360,256]{1,0:T(8,128)(2,1)S(1)}, bf16[360,256]{1,0:T(8,128)(2,1)}, u32[]{:S(2)}, u32[]{:S(2)}) collective-permute-start(bf16[360,256]{1,0:T(8,128)(2,1)S(1)} %plane_join.3.refs_0_), channel_id=1, source_target_pairs={{0,8},{2,10},{4,12},{6,14},{8,0},{10,2},{12,4},{14,6},{16,24},{18,... | collective-permute-start | bytes 552968 | tf_op jit(solution)/shard_map/ppermute | solution.py:1099
  132.0 16.5 %collective-permute-start.28 = (bf16[360,256]{1,0:T(8,128)(2,1)S(1)}, bf16[360,256]{1,0:T(8,128)(2,1)}, u32[]{:S(2)}, u32[]{:S(2)}) collective-permute-start(bf16[360,256]{1,0:T(8,128)(2,1)S(1)} %plane_join.3.refs_0_), channel_id=1, source_target_pairs={{0,16},{2,18},{4,20},{6,22},{8,24},{10,26},{12,28},{14,30},{16,0},... | collective-permute-start | bytes 552968 | tf_op jit(solution)/shard_map/ppermute | solution.py:1099
  134.6 13.9 %collective-permute-start.29 = (bf16[360,256]{1,0:T(8,128)(2,1)S(1)}, bf16[360,256]{1,0:T(8,128)(2,1)}, u32[]{:S(2)}, u32[]{:S(2)}) collective-permute-start(bf16[360,256]{1,0:T(8,128)(2,1)S(1)} %plane_join.3.refs_0_), channel_id=1, source_target_pairs={{0,24},{2,26},{4,28},{6,30},{8,16},{10,18},{12,20},{14,22},{16,8},... | collective-permute-start | bytes 552968 | tf_op jit(solution)/shard_map/ppermute | solution.py:1099
  135.1 14.0 %collective-permute-start.30 = (bf16[360,256]{1,0:T(8,128)(2,1)S(1)}, bf16[360,256]{1,0:T(8,128)(2,1)S(1)}, u32[]{:S(2)}, u32[]{:S(2)}) collective-permute-start(bf16[360,256]{1,0:T(8,128)(2,1)S(1)} %plane_join.3.refs_0_), channel_id=1, source_target_pairs={{0,1},{1,0},{2,3},{3,2},{4,5},{5,4},{6,7},{7,6},{8,9},{9,8},{10,11... | collective-permute-start | bytes 552968 | tf_op jit(solution)/shard_map/ppermute | solution.py:1094
  139.5 10.7 %collective-permute-start.31 = (bf16[360,256]{1,0:T(8,128)(2,1)}, bf16[360,256]{1,0:T(8,128)(2,1)}, u32[]{:S(2)}, u32[]{:S(2)}) collective-permute-start(bf16[360,256]{1,0:T(8,128)(2,1)} %collective-permute-done.27.refs_1_), channel_id=1, source_target_pairs={{0,1},{1,0},{2,3},{3,2},{4,5},{5,4},{6,7},{7,6},{8,9},{9,8},{10,11... | collective-permute-start | bytes 552968 | tf_op jit(solution)/shard_map/ppermute | solution.py:1094
  148.5 1.8 %collective-permute-start.32 = (bf16[360,256]{1,0:T(8,128)(2,1)}, bf16[360,256]{1,0:T(8,128)(2,1)}, u32[]{:S(2)}, u32[]{:S(2)}) collective-permute-start(bf16[360,256]{1,0:T(8,128)(2,1)} %collective-permute-done.28.refs_2_), channel_id=1, source_target_pairs={{0,1},{1,0},{2,3},{3,2},{4,5},{5,4},{6,7},{7,6},{8,9},{9,8},{10,11... | collective-permute-start | bytes 552968 | tf_op jit(solution)/shard_map/ppermute | solution.py:1094
  148.5 2.0 %collective-permute-start.33 = (bf16[360,256]{1,0:T(8,128)(2,1)}, bf16[360,256]{1,0:T(8,128)(2,1)}, u32[]{:S(2)}, u32[]{:S(2)}) collective-permute-start(bf16[360,256]{1,0:T(8,128)(2,1)} %collective-permute-done.29.refs_3_), channel_id=1, source_target_pairs={{0,1},{1,0},{2,3},{3,2},{4,5},{5,4},{6,7},{7,6},{8,9},{9,8},{10,11... | collective-permute-start | bytes 552968 | tf_op jit(solution)/shard_map/ppermute | solution.py:1094
  149.0 7.3 %collective-permute-start.35 = (f32[48,128]{1,0:T(8,128)S(1)}, f32[48,128]{1,0:T(8,128)S(1)}, u32[]{:S(2)}, u32[]{:S(2)}) collective-permute-start(f32[48,128]{1,0:T(8,128)S(1)} %copy-done.35), channel_id=1, source_target_pairs={{0,1},{1,0},{2,3},{3,2},{4,5},{5,4},{6,7},{7,6},{8,9},{9,8},{10,11... | collective-permute-start | bytes 73736 | tf_op jit(solution)/shard_map/ppermute | solution.py:1094
  149.7 7.2 %collective-permute-start.34 = (bf16[128,768]{1,0:T(8,128)(2,1)S(1)}, bf16[128,768]{1,0:T(8,128)(2,1)S(1)}, u32[]{:S(2)}, u32[]{:S(2)}) collective-permute-start(bf16[128,768]{1,0:T(8,128)(2,1)S(1)} %mixer_back.1.half_ref), channel_id=1, source_target_pairs={{0,1},{1,0},{2,3},{3,2},{4,5},{5,4},{6,7},{7,6},{8,9},{9,8},{10,11... | collective-permute-start | bytes 589832 | tf_op jit(solution)/shard_map/ppermute | solution.py:1094
  156.0 3.9 %collective-permute-start.36 = (bf16[4,48,384]{2,1,0:T(8,128)(2,1)S(1)}, bf16[4,48,384]{2,1,0:T(8,128)(2,1)S(1)}, u32[]{:S(2)}, u32[]{:S(2)}) collective-permute-start(bf16[4,48,384]{2,1,0:T(8,128)(2,1)S(1)} %slice.35.mine_ref), channel_id=1, source_target_pairs={{0,1},{1,0},{2,3},{3,2},{4,5},{5,4},{6,7},{7,6},{8,9},{9,8},{10,11... | collective-permute-start | bytes 442376 | tf_op jit(solution)/shard_map/ppermute | solution.py:1094
  (18 other events, 24.4 us)
